TPU v7x, 32 devices: a whole 2x2x4 slice. The times are simulated.
32 devices in a mesh: row: 4 (over x, core), col: 4 (over z), win: 2 (over y).
Axes of the slice: x: 2, y: 2, z: 4, core: 2. Of those that a mesh axis runs over, the one named last changes fastest.
Arguments:
- spectra: float32 [2, 2, 16, 2, 16384], P('win', None, ('row', 'col')), may hold values from -8 to 8
- tile_rows: int32 [8256], P(('row', 'col')), may hold values from 0 to 127, as said below
- tile_cols: int32 [8256], P(('row', 'col')), may hold values from 0 to 127, as said below
Outputs:
- cross: float32 [8256, 2, 2, 128, 128], P(('row', 'col'), None, None, 'win')
Inputs may be any that keep to these rules, and one draw needn't show every extreme that they name: tile_rows[k] <= tile_cols[k] for every k, and the pairs (tile_rows[k], tile_cols[k]) are all pairs of channel blocks with row block at most column block, each exactly once, in an order drawn from the seed. `tile_cols`: see tile_rows.
All inputs are finite; a program needn't handle non-finite values.
Results may differ from a plain program's by a relative error of at most 0.006.
Values may be sent and summed in bfloat16 or wider, within the bound.
No kernel may reach another device: no remote copies, remote signals or barrier semaphores. Data moves between devices by JAX's collectives and lax.ppermute only.
A program may use at most 320 MiB of HBM per device.

v0:
```python
import functools

import jax
import jax.numpy as jnp
from jax import lax
from jax.experimental import pallas as pl
from jax.experimental.pallas import tpu as pltpu
from jax.sharding import PartitionSpec as P

BLOCK = 128


def whiten_kernel(spectra_ref, *out_refs):
    freqs = spectra_ref.shape[0]
    power = None
    for freq in range(freqs):
        slab = spectra_ref[freq]
        term = jnp.sum(slab * slab, axis=1, keepdims=True)
        power = term if power is None else power + term
    floor = jnp.maximum(jnp.sqrt(power / freqs), 1.0)
    for freq in range(freqs):
        out_refs[freq][...] = (spectra_ref[freq] / floor).astype(jnp.bfloat16)


def whiten(spectra):
    freqs, windows, parts, channels = spectra.shape
    shape = jax.ShapeDtypeStruct((windows, parts, channels), jnp.bfloat16)
    slabs = pl.pallas_call(whiten_kernel, out_shape=[shape] * freqs, name="whiten")(spectra)
    return [slab.reshape(windows * parts, channels) for slab in slabs]


def shift(value, axis, step, inner=1):
    size = lax.axis_size(axis)
    stops = size // inner
    perm = [(at, (at // inner + step) % stops * inner + at % inner) for at in range(size)]
    return lax.ppermute(value, axis, perm)


def gather_windows(own):
    row_size = lax.axis_size("row")
    cores = 2 if row_size % 2 == 0 else 1
    line = [own] + [shift(own, "col", step) for step in range(1, lax.axis_size("col"))]
    block = jnp.concatenate(line, axis=0)
    half = block.shape[1] // 2
    along_row = [shift(block, "row", step, cores) for step in range(1, row_size // cores)]
    along_win = [shift(block, "win", step) for step in range(1, lax.axis_size("win"))]
    whole = [block] + along_row + along_win
    split = []
    for row_step, from_row in enumerate(along_row, 1):
        for win_step, from_win in enumerate(along_win, 1):
            low = shift(from_win[:, :half], "row", row_step, cores)
            high = shift(from_row[:, half:], "win", win_step)
            split.append((low, high))
    if cores == 2:
        swap = functools.partial(
            lax.ppermute, axis_name="row", perm=[(at, at ^ 1) for at in range(row_size)]
        )
        whole = whole + [swap(value) for value in whole]
        split = split + [(swap(low), swap(high)) for low, high in split]
    return whole, split


def stack_kernel(
    counts, parts_rows, scale, rows_ref, cols_ref, *refs
):
    whole_count, split_count, aliased = counts
    whole = refs[:whole_count]
    low = refs[whole_count : whole_count + split_count]
    high = refs[whole_count + split_count : whole_count + 2 * split_count]
    out_ref, left_ref, right_ref = refs[whole_count + 2 * split_count + aliased :]
    depth = left_ref.shape[1]
    row_count = out_ref.shape[3]
    tiles = out_ref.shape[0]
    step = pl.program_id(0)

    @pl.when(step == 0)
    def _():
        offset = lax.axis_index("win") * row_count
        pick_at = lax.broadcasted_iota(jnp.int32, (2 * row_count, 2 * BLOCK), 0)
        pick_lane = lax.broadcasted_iota(jnp.int32, (2 * row_count, 2 * BLOCK), 1)
        want = pick_at % row_count + offset + pick_at // row_count * BLOCK
        pick = (pick_lane == want).astype(jnp.bfloat16)
        turn_at = lax.broadcasted_iota(jnp.int32, (depth, depth), 0)
        turn_lane = lax.broadcasted_iota(jnp.int32, (depth, depth), 1)
        is_imag = turn_at % 2 == 1
        turn = jnp.where(
            is_imag,
            jnp.where(turn_lane == turn_at - 1, -1.0, 0.0),
            jnp.where(turn_lane == turn_at + 1, 1.0, 0.0),
        ).astype(jnp.bfloat16)

        def prepare(halves, first):
            pairs = halves[0].shape[1] // (2 * BLOCK) if halves else whole[0].shape[1] // (4 * BLOCK)

            def body(at, carry):
                here = pl.multiple_of((at + first) * 2 * BLOCK, 2 * BLOCK)
                near = pl.multiple_of(at * 2 * BLOCK, 2 * BLOCK)
                pieces = [ref[:, pl.ds(here, 2 * BLOCK)] for ref in whole]
                pieces += [ref[:, pl.ds(near, 2 * BLOCK)] for ref in halves]
                rows = jnp.concatenate(pieces, axis=0)
                turned = jnp.dot(turn, rows, preferred_element_type=jnp.float32)
                turned = turned.astype(jnp.bfloat16)
                left = lax.dot_general(
                    pick, rows, (((1,), (1,)), ((), ())), preferred_element_type=jnp.float32
                )
                where = pl.multiple_of((at + first) * 2 * row_count, 2 * row_count)
                left_ref[pl.ds(where, 2 * row_count), :] = left.astype(jnp.bfloat16)
                for half in range(2):
                    lanes = slice(half * BLOCK, (half + 1) * BLOCK)
                    right_ref[(at + first) * 2 + half, :, :BLOCK] = rows[:, lanes]
                    right_ref[(at + first) * 2 + half, :, BLOCK:] = turned[:, lanes]
                return carry

            lax.fori_loop(0, pairs, body, 0, unroll=4)
            return pairs

        prepare(high, prepare(low, 0))

    for tile in range(tiles):
        at = step * tiles + tile
        left_at = pl.multiple_of(rows_ref[at] * row_count, row_count)
        product = jnp.dot(
            left_ref[pl.ds(left_at, row_count), :],
            right_ref[cols_ref[at]],
            preferred_element_type=jnp.float32,
        )
        product = product * scale
        out_ref[tile, 0, 0] = product[:, :BLOCK]
        out_ref[tile, 0, 1] = product[:, BLOCK:]


def stack_bin(freq, out_shape, tile_rows, tile_cols, whole, split, scale, so_far):
    low = [pair[0] for pair in split]
    high = [pair[1] for pair in split]
    pieces = whole + low + high
    channels = whole[0].shape[1]
    depth = sum(value.shape[0] for value in whole + low)
    tile_total, _, parts, row_count, _ = out_shape.shape
    tiles = max(size for size in range(1, 17) if tile_total % size == 0)
    blocks = channels // BLOCK
    in_specs = [
        pl.BlockSpec(value.shape, lambda step, *_: (0, 0), pipeline_mode=pl.Buffered(1))
        for value in pieces
    ]
    operands = [tile_rows, tile_cols] + pieces
    aliases = {}
    if so_far is not None:
        in_specs.append(pl.BlockSpec(memory_space=pl.ANY))
        aliases = {len(operands): 0}
        operands.append(so_far)
    block = (tiles, 1, parts, row_count, BLOCK)
    scratch = [
        pltpu.VMEM((blocks * row_count, depth), jnp.bfloat16),
        pltpu.VMEM((blocks, depth, 2 * BLOCK), jnp.bfloat16),
    ]
    product = tile_total * row_count * 2 * BLOCK
    return pl.pallas_call(
        functools.partial(stack_kernel, (len(whole), len(split), len(aliases)), row_count, scale),
        out_shape=out_shape,
        grid_spec=pltpu.PrefetchScalarGridSpec(
            num_scalar_prefetch=2,
            grid=(tile_total // tiles,),
            in_specs=in_specs,
            out_specs=pl.BlockSpec(block, lambda step, *_: (step, freq, 0, 0, 0)),
            scratch_shapes=scratch,
        ),
        input_output_aliases=aliases,
        cost_estimate=pl.CostEstimate(
            flops=2 * product * depth, bytes_accessed=4 * product, transcendentals=0
        ),
        compiler_params=pltpu.CompilerParams(vmem_limit_bytes=56 * 1024 * 1024),
        name="stack",
    )(*operands)


def on_device(spectra, tile_rows, tile_cols):
    window_total = (
        spectra.shape[2] * lax.axis_size("row") * lax.axis_size("col") * lax.axis_size("win")
    )
    scale = float(1.0 / window_total**0.5)
    slabs = whiten(spectra[0])
    row_count = BLOCK // lax.axis_size("win")
    out_shape = jax.ShapeDtypeStruct(
        (tile_rows.shape[0], len(slabs), 2, row_count, BLOCK), jnp.float32
    )
    gathered = [gather_windows(slab) for slab in slabs]
    out = None
    for freq, (whole, split) in enumerate(gathered):
        out = stack_bin(freq, out_shape, tile_rows, tile_cols, whole, split, scale, out)
    return out


def solution(mesh):
    in_specs = (P("win", None, ("row", "col"), None, None), P(("row", "col")), P(("row", "col")))
    out_specs = P(("row", "col"), None, None, "win", None)
    return jax.shard_map(
        on_device, mesh=mesh, in_specs=in_specs, out_specs=out_specs, check_vma=False
    )
```

profile of v0, /device:TPU:0, one launch (start us, length us, event | category | flops | bytes accessed | tf_op | source)
XLA Modules:
  0.0 111.1 jit_solution(11972696362382512681)
XLA Ops:
  0.0 2.2 %whiten.1 = (bf16[1,2,16384]{2,1,0:T(2,128)(2,1)}, bf16[1,2,16384]{2,1,0:T(2,128)(2,1)}) custom-call(f32[2,1,2,16384]{3,2,1,0:T(2,128)} %bitcast.3), custom_call_target="tpu_custom_call" | custom-call | tf_op jit(solution)/shard_map/whiten/pallas_call | solution.py:28
  2.2 5.0 %collective-permute-start.2 = (bf16[2,16384]{1,0:T(2,128)(2,1)}, bf16[2,16384]{1,0:T(2,128)(2,1)S(1)}, u32[]{:S(2)}, u32[]{:S(2)}) collective-permute-start(bf16[2,16384]{1,0:T(2,128)(2,1)} %bitcast.8), channel_id=1, source_target_pairs={{0,6},{2,0},{4,2},{6,4},{1,7},{3,1},{5,3},{7,5},{8,14},{10,8},{12,... | collective-permute-start | bytes 196616 | tf_op jit(solution)/shard_map/ppermute | solution.py:36
  7.2 1.0 collective-permute-start
  8.2 2.8 %collective-permute-start.14 = (bf16[2,16384]{1,0:T(2,128)(2,1)}, bf16[2,16384]{1,0:T(2,128)(2,1)S(1)}, u32[]{:S(2)}, u32[]{:S(2)}) collective-permute-start(bf16[2,16384]{1,0:T(2,128)(2,1)} %bitcast.4), channel_id=1, source_target_pairs={{0,6},{2,0},{4,2},{6,4},{1,7},{3,1},{5,3},{7,5},{8,14},{10,8},{12,... | collective-permute-start | bytes 196616 | tf_op jit(solution)/shard_map/ppermute | solution.py:36
  11.1 1.1 %collective-permute-start.13 = (bf16[2,16384]{1,0:T(2,128)(2,1)}, bf16[2,16384]{1,0:T(2,128)(2,1)S(1)}, u32[]{:S(2)}, u32[]{:S(2)}) collective-permute-start(bf16[2,16384]{1,0:T(2,128)(2,1)} %bitcast.5), channel_id=1, source_target_pairs={{0,4},{2,6},{4,0},{6,2},{1,5},{3,7},{5,1},{7,3},{8,12},{10,14},{12... | collective-permute-start | bytes 196616 | tf_op jit(solution)/shard_map/ppermute | solution.py:36
  12.2 2.8 %collective-permute-done.1 = bf16[2,16384]{1,0:T(2,128)(2,1)S(1)} collective-permute-done((bf16[2,16384]{1,0:T(2,128)(2,1)}, bf16[2,16384]{1,0:T(2,128)(2,1)S(1)}, u32[]{:S(2)}, u32[]{:S(2)}) %collective-permute-start.1) | collective-permute-done | bytes 65568 | tf_op jit(solution)/shard_map/ppermute | solution.py:36
  14.9 1.1 %pad_maximum_fusion.refs_0_ = bf16[8,16384]{1,0:T(8,128)(2,1)S(1)} fusion(bf16[2,16384]{1,0:T(2,128)(2,1)S(1)} %collective-permute-done.2, bf16[2,16384]{1,0:T(2,128)(2,1)S(1)} %collective-permute-done.1, bf16[2,16384]{1,0:T(2,128)(2,1)S(1)} %collective-permute-done, bf16[2,16384]{1,0:T(2,128)(2,1)} %bitcast.11), kind=kLoop, calls=%fused_computation | loop fusion | flops 1048576 | bytes 524288 | tf_op jit(solution)/shard_map/concatenate | solution.py:43
  16.1 1.6 %collective-permute-start.4 = (bf16[8,16384]{1,0:T(8,128)(2,1)S(1)}, bf16[8,16384]{1,0:T(8,128)(2,1)S(1)}, u32[]{:S(2)}, u32[]{:S(2)}) collective-permute-start(bf16[8,16384]{1,0:T(8,128)(2,1)S(1)} %pad_maximum_fusion.refs_0_), channel_id=1, source_target_pairs={{0,1},{1,0},{2,3},{3,2},{4,5},{5,4},{6,7},{7,6},{8,9},{9,8},{10,11... | collective-permute-start | bytes 786440 | tf_op jit(solution)/shard_map/ppermute | solution.py:36
  17.7 1.9 %collective-permute-done.13 = bf16[2,16384]{1,0:T(2,128)(2,1)S(1)} collective-permute-done((bf16[2,16384]{1,0:T(2,128)(2,1)}, bf16[2,16384]{1,0:T(2,128)(2,1)S(1)}, u32[]{:S(2)}, u32[]{:S(2)}) %collective-permute-start.13) | collective-permute-done | bytes 65568 | tf_op jit(solution)/shard_map/ppermute | solution.py:36
  19.6 1.1 %pad_maximum_fusion.1.refs_0_ = bf16[8,16384]{1,0:T(8,128)(2,1)S(1)} fusion(bf16[2,16384]{1,0:T(2,128)(2,1)S(1)} %collective-permute-done.14, bf16[2,16384]{1,0:T(2,128)(2,1)S(1)} %collective-permute-done.13, bf16[2,16384]{1,0:T(2,128)(2,1)S(1)} %collective-permute-done.12, bf16[2,16384]{1,0:T(2,128)(2,1)} %bitcast.7), kind=kLoop, calls=%fused_computation.1 | loop fusion | flops 1048576 | bytes 524288 | tf_op jit(solution)/shard_map/concatenate | solution.py:43
  20.7 1.6 %collective-permute-start.16 = (bf16[8,16384]{1,0:T(8,128)(2,1)S(1)}, bf16[8,16384]{1,0:T(8,128)(2,1)S(1)}, u32[]{:S(2)}, u32[]{:S(2)}) collective-permute-start(bf16[8,16384]{1,0:T(8,128)(2,1)S(1)} %pad_maximum_fusion.1.refs_0_), channel_id=1, source_target_pairs={{0,1},{1,0},{2,3},{3,2},{4,5},{5,4},{6,7},{7,6},{8,9},{9,8},{10,11... | collective-permute-start | bytes 786440 | tf_op jit(solution)/shard_map/ppermute | solution.py:36
  22.3 1.5 %collective-permute-start.15 = (bf16[8,16384]{1,0:T(8,128)(2,1)S(1)}, bf16[8,16384]{1,0:T(8,128)(2,1)S(1)}, u32[]{:S(2)}, u32[]{:S(2)}) collective-permute-start(bf16[8,16384]{1,0:T(8,128)(2,1)S(1)} %pad_maximum_fusion.1.refs_0_), channel_id=1, source_target_pairs={{0,16},{8,24},{16,0},{24,8},{1,17},{9,25},{17,1},{25,9},{2,18},{10... | collective-permute-start | bytes 786440 | tf_op jit(solution)/shard_map/ppermute | solution.py:36
  23.8 0.5 collective-permute-start.3
  24.6 1.6 %collective-permute-start.8 = (bf16[8,8192]{1,0:T(8,128)(2,1)S(1)}, bf16[8,8192]{1,0:T(8,128)(2,1)S(1)}, u32[]{:S(2)}, u32[]{:S(2)}) collective-permute-start(bf16[8,8192]{1,0:T(8,128)(2,1)S(1)} %slice.16), channel_id=1, source_target_pairs={{0,16},{8,24},{16,0},{24,8},{1,17},{9,25},{17,1},{25,9},{2,18},{10... | collective-permute-start | bytes 393224 | tf_op jit(solution)/shard_map/ppermute | solution.py:36
  26.1 3.4 %collective-permute-done.16.refs_2_ = bf16[8,16384]{1,0:T(8,128)(2,1)S(1)} collective-permute-done((bf16[8,16384]{1,0:T(8,128)(2,1)S(1)}, bf16[8,16384]{1,0:T(8,128)(2,1)S(1)}, u32[]{:S(2)}, u32[]{:S(2)}) %collective-permute-start.16) | collective-permute-done | bytes 262176 | tf_op jit(solution)/shard_map/ppermute | solution.py:36
  29.5 2.0 %collective-permute-done.15.refs_1_ = bf16[8,16384]{1,0:T(8,128)(2,1)S(1)} collective-permute-done((bf16[8,16384]{1,0:T(8,128)(2,1)S(1)}, bf16[8,16384]{1,0:T(8,128)(2,1)S(1)}, u32[]{:S(2)}, u32[]{:S(2)}) %collective-permute-start.15) | collective-permute-done | bytes 262176 | tf_op jit(solution)/shard_map/ppermute | solution.py:36
  31.6 5.5 %collective-permute-done.3.refs_1_ = bf16[8,16384]{1,0:T(8,128)(2,1)S(1)} collective-permute-done((bf16[8,16384]{1,0:T(8,128)(2,1)S(1)}, bf16[8,16384]{1,0:T(8,128)(2,1)S(1)}, u32[]{:S(2)}, u32[]{:S(2)}) %collective-permute-start.3) | collective-permute-done | bytes 262176 | tf_op jit(solution)/shard_map/ppermute | solution.py:36
  37.1 0.6 collective-permute-start.10
  37.7 1.6 %collective-permute-start.20 = (bf16[8,8192]{1,0:T(8,128)(2,1)S(1)}, bf16[8,8192]{1,0:T(8,128)(2,1)S(1)}, u32[]{:S(2)}, u32[]{:S(2)}) collective-permute-start(bf16[8,8192]{1,0:T(8,128)(2,1)S(1)} %slice.18), channel_id=1, source_target_pairs={{0,16},{8,24},{16,0},{24,8},{1,17},{9,25},{17,1},{25,9},{2,18},{10... | collective-permute-start | bytes 393224 | tf_op jit(solution)/shard_map/ppermute | solution.py:36
  39.3 0.3 collective-permute-done.8.refs_6_
  39.6 1.2 %collective-permute-start.22 = (bf16[8,8192]{1,0:T(8,128)(2,1)S(1)}, bf16[8,8192]{1,0:T(8,128)(2,1)S(1)}, u32[]{:S(2)}, u32[]{:S(2)}) collective-permute-start(bf16[8,8192]{1,0:T(8,128)(2,1)S(1)} %slice.19), channel_id=1, source_target_pairs={{0,1},{1,0},{2,3},{3,2},{4,5},{5,4},{6,7},{7,6},{8,9},{9,8},{10,11... | collective-permute-start | bytes 393224 | tf_op jit(solution)/shard_map/ppermute | solution.py:36
  40.8 1.7 %collective-permute-done.10.refs_8_ = bf16[8,8192]{1,0:T(8,128)(2,1)S(1)} collective-permute-done((bf16[8,8192]{1,0:T(8,128)(2,1)S(1)}, bf16[8,8192]{1,0:T(8,128)(2,1)S(1)}, u32[]{:S(2)}, u32[]{:S(2)}) %collective-permute-start.10) | collective-permute-done | bytes 131104 | tf_op jit(solution)/shard_map/ppermute | solution.py:36
  42.5 0.2 collective-permute-done.20.refs_6_
  42.8 0.3 collective-permute-start.7
  43.1 1.5 %collective-permute-done.22.refs_8_ = bf16[8,8192]{1,0:T(8,128)(2,1)S(1)} collective-permute-done((bf16[8,8192]{1,0:T(8,128)(2,1)S(1)}, bf16[8,8192]{1,0:T(8,128)(2,1)S(1)}, u32[]{:S(2)}, u32[]{:S(2)}) %collective-permute-start.22) | collective-permute-done | bytes 131104 | tf_op jit(solution)/shard_map/ppermute | solution.py:36
  44.6 0.5 collective-permute-start.21
  45.2 1.1 %collective-permute-done.21.refs_7_ = bf16[8,8192]{1,0:T(8,128)(2,1)S(1)} collective-permute-done((bf16[8,8192]{1,0:T(8,128)(2,1)S(1)}, bf16[8,8192]{1,0:T(8,128)(2,1)S(1)}, u32[]{:S(2)}, u32[]{:S(2)}) %collective-permute-start.21) | collective-permute-done | bytes 131104 | tf_op jit(solution)/shard_map/ppermute | solution.py:59
  46.5 0.3 collective-permute-start.11
  47.1 31.2 %stack.2.refs_10_ = f32[516,2,2,64,128]{4,3,2,1,0:T(8,128)} custom-call(s32[516]{0:T(1024)} %rows_ref.3, s32[516]{0:T(1024)} %cols_ref.3, bf16[8,16384]{1,0:T(8,128)(2,1)} %copy-done.1, bf16[8,16384]{1,0:T(8,128)(2,1)} %copy-done.5, bf16[8,16384]{1,0:T(8,128)(2,1)} %copy-done.4, bf16[8,16384]{1,0:T(8,128)(2,1)} %copy-done.6, bf16[8,16384]{1,0:T(8,128)(2,1)} %copy-done.8, ...), custom_call_target="tpu_custom_call" | custom-call | flops 1082130432 | bytes 33816576 | tf_op jit(solution)/shard_map/stack/pallas_call | solution.py:157
  78.4 0.6 copy-done.9
  79.2 0.6 copy-done.19
  79.9 31.2 %stack.3 = f32[516,2,2,64,128]{4,3,2,1,0:T(8,128)} custom-call(s32[516]{0:T(1024)} %rows_ref.3, s32[516]{0:T(1024)} %cols_ref.3, bf16[8,16384]{1,0:T(8,128)(2,1)} %copy-done, bf16[8,16384]{1,0:T(8,128)(2,1)} %copy-done.3, bf16[8,16384]{1,0:T(8,128)(2,1)} %copy-done.2, bf16[8,16384]{1,0:T(8,128)(2,1)} %copy-done.9, ...), custom_call_target="tpu_custom_call", output_to_operand_aliasing={{}: (12, {})} | custom-call | flops 1082130432 | bytes 33816576 | tf_op jit(solution)/shard_map/stack/pallas_call | solution.py:157
  (65 shorter events, 1.1 us)
Async XLA Ops:
  2.2 10.0 %collective-permute-start.2 = (bf16[2,16384]{1,0:T(2,128)(2,1)}, bf16[2,16384]{1,0:T(2,128)(2,1)S(1)}, u32[]{:S(2)}, u32[]{:S(2)}) collective-permute-start(bf16[2,16384]{1,0:T(2,128)(2,1)} %bitcast.8), channel_id=1, source_target_pairs={{0,6},{2,0},{4,2},{6,4},{1,7},{3,1},{5,3},{7,5},{8,14},{10,8},{12,... | collective-permute-start | bytes 196616 | tf_op jit(solution)/shard_map/ppermute | solution.py:36
  7.2 7.7 %collective-permute-start.1 = (bf16[2,16384]{1,0:T(2,128)(2,1)}, bf16[2,16384]{1,0:T(2,128)(2,1)S(1)}, u32[]{:S(2)}, u32[]{:S(2)}) collective-permute-start(bf16[2,16384]{1,0:T(2,128)(2,1)} %bitcast.9), channel_id=1, source_target_pairs={{0,4},{2,6},{4,0},{6,2},{1,5},{3,7},{5,1},{7,3},{8,12},{10,14},{12... | collective-permute-start | bytes 196616 | tf_op jit(solution)/shard_map/ppermute | solution.py:36
  7.2 7.7 %collective-permute-start = (bf16[2,16384]{1,0:T(2,128)(2,1)}, bf16[2,16384]{1,0:T(2,128)(2,1)S(1)}, u32[]{:S(2)}, u32[]{:S(2)}) collective-permute-start(bf16[2,16384]{1,0:T(2,128)(2,1)} %bitcast.10), channel_id=1, source_target_pairs={{0,2},{2,4},{4,6},{6,0},{1,3},{3,5},{5,7},{7,1},{8,10},{10,12},{12... | collective-permute-start | bytes 196616 | tf_op jit(solution)/shard_map/ppermute | solution.py:36
  8.2 9.4 %collective-permute-start.14 = (bf16[2,16384]{1,0:T(2,128)(2,1)}, bf16[2,16384]{1,0:T(2,128)(2,1)S(1)}, u32[]{:S(2)}, u32[]{:S(2)}) collective-permute-start(bf16[2,16384]{1,0:T(2,128)(2,1)} %bitcast.4), channel_id=1, source_target_pairs={{0,6},{2,0},{4,2},{6,4},{1,7},{3,1},{5,3},{7,5},{8,14},{10,8},{12,... | collective-permute-start | bytes 196616 | tf_op jit(solution)/shard_map/ppermute | solution.py:36
  11.1 8.5 %collective-permute-start.13 = (bf16[2,16384]{1,0:T(2,128)(2,1)}, bf16[2,16384]{1,0:T(2,128)(2,1)S(1)}, u32[]{:S(2)}, u32[]{:S(2)}) collective-permute-start(bf16[2,16384]{1,0:T(2,128)(2,1)} %bitcast.5), channel_id=1, source_target_pairs={{0,4},{2,6},{4,0},{6,2},{1,5},{3,7},{5,1},{7,3},{8,12},{10,14},{12... | collective-permute-start | bytes 196616 | tf_op jit(solution)/shard_map/ppermute | solution.py:36
  12.2 7.4 %collective-permute-start.12 = (bf16[2,16384]{1,0:T(2,128)(2,1)}, bf16[2,16384]{1,0:T(2,128)(2,1)S(1)}, u32[]{:S(2)}, u32[]{:S(2)}) collective-permute-start(bf16[2,16384]{1,0:T(2,128)(2,1)} %bitcast.6), channel_id=1, source_target_pairs={{0,2},{2,4},{4,6},{6,0},{1,3},{3,5},{5,7},{7,1},{8,10},{10,12},{12... | collective-permute-start | bytes 196616 | tf_op jit(solution)/shard_map/ppermute | solution.py:36
  16.1 62.3 %copy-start = (bf16[8,16384]{1,0:T(8,128)(2,1)}, bf16[8,16384]{1,0:T(8,128)(2,1)S(1)}, u32[]{:S(2)}) copy-start(bf16[8,16384]{1,0:T(8,128)(2,1)S(1)} %pad_maximum_fusion.refs_0_) | copy-start | bytes 786436
  16.1 8.4 %collective-permute-start.4 = (bf16[8,16384]{1,0:T(8,128)(2,1)S(1)}, bf16[8,16384]{1,0:T(8,128)(2,1)S(1)}, u32[]{:S(2)}, u32[]{:S(2)}) collective-permute-start(bf16[8,16384]{1,0:T(8,128)(2,1)S(1)} %pad_maximum_fusion.refs_0_), channel_id=1, source_target_pairs={{0,1},{1,0},{2,3},{3,2},{4,5},{5,4},{6,7},{7,6},{8,9},{9,8},{10,11... | collective-permute-start | bytes 786440 | tf_op jit(solution)/shard_map/ppermute | solution.py:36
  20.7 26.1 %copy-start.1 = (bf16[8,16384]{1,0:T(8,128)(2,1)}, bf16[8,16384]{1,0:T(8,128)(2,1)S(1)}, u32[]{:S(2)}) copy-start(bf16[8,16384]{1,0:T(8,128)(2,1)S(1)} %pad_maximum_fusion.1.refs_0_) | copy-start | bytes 786436
  20.7 8.8 %collective-permute-start.16 = (bf16[8,16384]{1,0:T(8,128)(2,1)S(1)}, bf16[8,16384]{1,0:T(8,128)(2,1)S(1)}, u32[]{:S(2)}, u32[]{:S(2)}) collective-permute-start(bf16[8,16384]{1,0:T(8,128)(2,1)S(1)} %pad_maximum_fusion.1.refs_0_), channel_id=1, source_target_pairs={{0,1},{1,0},{2,3},{3,2},{4,5},{5,4},{6,7},{7,6},{8,9},{9,8},{10,11... | collective-permute-start | bytes 786440 | tf_op jit(solution)/shard_map/ppermute | solution.py:36
  22.3 9.2 %collective-permute-start.15 = (bf16[8,16384]{1,0:T(8,128)(2,1)S(1)}, bf16[8,16384]{1,0:T(8,128)(2,1)S(1)}, u32[]{:S(2)}, u32[]{:S(2)}) collective-permute-start(bf16[8,16384]{1,0:T(8,128)(2,1)S(1)} %pad_maximum_fusion.1.refs_0_), channel_id=1, source_target_pairs={{0,16},{8,24},{16,0},{24,8},{1,17},{9,25},{17,1},{25,9},{2,18},{10... | collective-permute-start | bytes 786440 | tf_op jit(solution)/shard_map/ppermute | solution.py:36
  23.8 13.3 %collective-permute-start.3 = (bf16[8,16384]{1,0:T(8,128)(2,1)S(1)}, bf16[8,16384]{1,0:T(8,128)(2,1)S(1)}, u32[]{:S(2)}, u32[]{:S(2)}) collective-permute-start(bf16[8,16384]{1,0:T(8,128)(2,1)S(1)} %pad_maximum_fusion.refs_0_), channel_id=1, source_target_pairs={{0,16},{8,24},{16,0},{24,8},{1,17},{9,25},{17,1},{25,9},{2,18},{10... | collective-permute-start | bytes 786440 | tf_op jit(solution)/shard_map/ppermute | solution.py:36
  24.3 13.4 %collective-permute-start.17 = (bf16[8,16384]{1,0:T(8,128)(2,1)S(1)}, bf16[8,16384]{1,0:T(8,128)(2,1)S(1)}, u32[]{:S(2)}, u32[]{:S(2)}) collective-permute-start(bf16[8,16384]{1,0:T(8,128)(2,1)S(1)} %pad_maximum_fusion.1.refs_0_), channel_id=1, source_target_pairs={{0,8},{8,0},{16,24},{24,16},{1,9},{9,1},{17,25},{25,17},{2,10},{10... | collective-permute-start | bytes 786440 | tf_op jit(solution)/shard_map/ppermute | solution.py:58
  24.5 53.9 %copy-start.2 = (bf16[8,16384]{1,0:T(8,128)(2,1)}, bf16[8,16384]{1,0:T(8,128)(2,1)S(1)}, u32[]{:S(2)}) copy-start(bf16[8,16384]{1,0:T(8,128)(2,1)S(1)} %collective-permute-done.4.refs_2_) | copy-start | bytes 786436
  24.6 15.0 %collective-permute-start.8 = (bf16[8,8192]{1,0:T(8,128)(2,1)S(1)}, bf16[8,8192]{1,0:T(8,128)(2,1)S(1)}, u32[]{:S(2)}, u32[]{:S(2)}) collective-permute-start(bf16[8,8192]{1,0:T(8,128)(2,1)S(1)} %slice.16), channel_id=1, source_target_pairs={{0,16},{8,24},{16,0},{24,8},{1,17},{9,25},{17,1},{25,9},{2,18},{10... | collective-permute-start | bytes 393224 | tf_op jit(solution)/shard_map/ppermute | solution.py:36
  29.5 17.3 %copy-start.4 = (bf16[8,16384]{1,0:T(8,128)(2,1)}, bf16[8,16384]{1,0:T(8,128)(2,1)S(1)}, u32[]{:S(2)}) copy-start(bf16[8,16384]{1,0:T(8,128)(2,1)S(1)} %collective-permute-done.16.refs_2_) | copy-start | bytes 786436
  29.5 15.0 %collective-permute-start.19 = (bf16[8,16384]{1,0:T(8,128)(2,1)S(1)}, bf16[8,16384]{1,0:T(8,128)(2,1)S(1)}, u32[]{:S(2)}, u32[]{:S(2)}) collective-permute-start(bf16[8,16384]{1,0:T(8,128)(2,1)S(1)} %collective-permute-done.16.refs_2_), channel_id=1, source_target_pairs={{0,8},{8,0},{16,24},{24,16},{1,9},{9,1},{17,25},{25,17},{2,10},{10... | collective-permute-start | bytes 786440 | tf_op jit(solution)/shard_map/ppermute | solution.py:58
  31.5 15.3 %copy-start.5 = (bf16[8,16384]{1,0:T(8,128)(2,1)}, bf16[8,16384]{1,0:T(8,128)(2,1)S(1)}, u32[]{:S(2)}) copy-start(bf16[8,16384]{1,0:T(8,128)(2,1)S(1)} %collective-permute-done.15.refs_1_) | copy-start | bytes 786436
  31.6 13.5 %collective-permute-start.18 = (bf16[8,16384]{1,0:T(8,128)(2,1)S(1)}, bf16[8,16384]{1,0:T(8,128)(2,1)S(1)}, u32[]{:S(2)}, u32[]{:S(2)}) collective-permute-start(bf16[8,16384]{1,0:T(8,128)(2,1)S(1)} %collective-permute-done.15.refs_1_), channel_id=1, source_target_pairs={{0,8},{8,0},{16,24},{24,16},{1,9},{9,1},{17,25},{25,17},{2,10},{10... | collective-permute-start | bytes 786440 | tf_op jit(solution)/shard_map/ppermute | solution.py:58
  37.1 41.3 %copy-start.3 = (bf16[8,16384]{1,0:T(8,128)(2,1)}, bf16[8,16384]{1,0:T(8,128)(2,1)S(1)}, u32[]{:S(2)}) copy-start(bf16[8,16384]{1,0:T(8,128)(2,1)S(1)} %collective-permute-done.3.refs_1_) | copy-start | bytes 786436
  37.1 5.4 %collective-permute-start.10 = (bf16[8,8192]{1,0:T(8,128)(2,1)S(1)}, bf16[8,8192]{1,0:T(8,128)(2,1)S(1)}, u32[]{:S(2)}, u32[]{:S(2)}) collective-permute-start(bf16[8,8192]{1,0:T(8,128)(2,1)S(1)} %slice.17), channel_id=1, source_target_pairs={{0,1},{1,0},{2,3},{3,2},{4,5},{5,4},{6,7},{7,6},{8,9},{9,8},{10,11... | collective-permute-start | bytes 393224 | tf_op jit(solution)/shard_map/ppermute | solution.py:36
  37.7 5.0 %collective-permute-start.20 = (bf16[8,8192]{1,0:T(8,128)(2,1)S(1)}, bf16[8,8192]{1,0:T(8,128)(2,1)S(1)}, u32[]{:S(2)}, u32[]{:S(2)}) collective-permute-start(bf16[8,8192]{1,0:T(8,128)(2,1)S(1)} %slice.18), channel_id=1, source_target_pairs={{0,16},{8,24},{16,0},{24,8},{1,17},{9,25},{17,1},{25,9},{2,18},{10... | collective-permute-start | bytes 393224 | tf_op jit(solution)/shard_map/ppermute | solution.py:36
  39.6 38.8 %copy-start.16 = (bf16[8,8192]{1,0:T(8,128)(2,1)}, bf16[8,8192]{1,0:T(8,128)(2,1)S(1)}, u32[]{:S(2)}) copy-start(bf16[8,8192]{1,0:T(8,128)(2,1)S(1)} %collective-permute-done.8.refs_6_) | copy-start | bytes 393220
  39.6 5.0 %collective-permute-start.22 = (bf16[8,8192]{1,0:T(8,128)(2,1)S(1)}, bf16[8,8192]{1,0:T(8,128)(2,1)S(1)}, u32[]{:S(2)}, u32[]{:S(2)}) collective-permute-start(bf16[8,8192]{1,0:T(8,128)(2,1)S(1)} %slice.19), channel_id=1, source_target_pairs={{0,1},{1,0},{2,3},{3,2},{4,5},{5,4},{6,7},{7,6},{8,9},{9,8},{10,11... | collective-permute-start | bytes 393224 | tf_op jit(solution)/shard_map/ppermute | solution.py:36
  42.5 35.9 %copy-start.17 = (bf16[8,8192]{1,0:T(8,128)(2,1)}, bf16[8,8192]{1,0:T(8,128)(2,1)S(1)}, u32[]{:S(2)}) copy-start(bf16[8,8192]{1,0:T(8,128)(2,1)S(1)} %collective-permute-done.10.refs_8_) | copy-start | bytes 393220
  42.5 35.8 %collective-permute-start.5 = (bf16[8,16384]{1,0:T(8,128)(2,1)S(1)}, bf16[8,16384]{1,0:T(8,128)(2,1)S(1)}, u32[]{:S(2)}, u32[]{:S(2)}) collective-permute-start(bf16[8,16384]{1,0:T(8,128)(2,1)S(1)} %pad_maximum_fusion.refs_0_), channel_id=1, source_target_pairs={{0,8},{8,0},{16,24},{24,16},{1,9},{9,1},{17,25},{25,17},{2,10},{10... | collective-permute-start | bytes 786440 | tf_op jit(solution)/shard_map/ppermute | solution.py:58
  42.8 35.6 %collective-permute-start.7 = (bf16[8,16384]{1,0:T(8,128)(2,1)S(1)}, bf16[8,16384]{1,0:T(8,128)(2,1)S(1)}, u32[]{:S(2)}, u32[]{:S(2)}) collective-permute-start(bf16[8,16384]{1,0:T(8,128)(2,1)S(1)} %collective-permute-done.4.refs_2_), channel_id=1, source_target_pairs={{0,8},{8,0},{16,24},{24,16},{1,9},{9,1},{17,25},{25,17},{2,10},{10... | collective-permute-start | bytes 786440 | tf_op jit(solution)/shard_map/ppermute | solution.py:58
  44.6 33.8 %collective-permute-start.6 = (bf16[8,16384]{1,0:T(8,128)(2,1)S(1)}, bf16[8,16384]{1,0:T(8,128)(2,1)S(1)}, u32[]{:S(2)}, u32[]{:S(2)}) collective-permute-start(bf16[8,16384]{1,0:T(8,128)(2,1)S(1)} %collective-permute-done.3.refs_1_), channel_id=1, source_target_pairs={{0,8},{8,0},{16,24},{24,16},{1,9},{9,1},{17,25},{25,17},{2,10},{10... | collective-permute-start | bytes 786440 | tf_op jit(solution)/shard_map/ppermute | solution.py:58
  44.6 1.7 %collective-permute-start.21 = (bf16[8,8192]{1,0:T(8,128)(2,1)S(1)}, bf16[8,8192]{1,0:T(8,128)(2,1)S(1)}, u32[]{:S(2)}, u32[]{:S(2)}) collective-permute-start(bf16[8,8192]{1,0:T(8,128)(2,1)S(1)} %collective-permute-done.20.refs_6_), channel_id=1, source_target_pairs={{0,8},{8,0},{16,24},{24,16},{1,9},{9,1},{17,25},{25,17},{2,10},{10... | collective-permute-start | bytes 393224 | tf_op jit(solution)/shard_map/ppermute | solution.py:59
  45.1 1.4 %collective-permute-start.23 = (bf16[8,8192]{1,0:T(8,128)(2,1)S(1)}, bf16[8,8192]{1,0:T(8,128)(2,1)S(1)}, u32[]{:S(2)}, u32[]{:S(2)}) collective-permute-start(bf16[8,8192]{1,0:T(8,128)(2,1)S(1)} %collective-permute-done.22.refs_8_), channel_id=1, source_target_pairs={{0,8},{8,0},{16,24},{24,16},{1,9},{9,1},{17,25},{25,17},{2,10},{10... | collective-permute-start | bytes 393224 | tf_op jit(solution)/shard_map/ppermute | solution.py:59
  46.3 32.1 %collective-permute-start.9 = (bf16[8,8192]{1,0:T(8,128)(2,1)S(1)}, bf16[8,8192]{1,0:T(8,128)(2,1)S(1)}, u32[]{:S(2)}, u32[]{:S(2)}) collective-permute-start(bf16[8,8192]{1,0:T(8,128)(2,1)S(1)} %collective-permute-done.8.refs_6_), channel_id=1, source_target_pairs={{0,8},{8,0},{16,24},{24,16},{1,9},{9,1},{17,25},{25,17},{2,10},{10... | collective-permute-start | bytes 393224 | tf_op jit(solution)/shard_map/ppermute | solution.py:59
  46.5 31.9 %collective-permute-start.11 = (bf16[8,8192]{1,0:T(8,128)(2,1)S(1)}, bf16[8,8192]{1,0:T(8,128)(2,1)S(1)}, u32[]{:S(2)}, u32[]{:S(2)}) collective-permute-start(bf16[8,8192]{1,0:T(8,128)(2,1)S(1)} %collective-permute-done.10.refs_8_), channel_id=1, source_target_pairs={{0,8},{8,0},{16,24},{24,16},{1,9},{9,1},{17,25},{25,17},{2,10},{10... | collective-permute-start | bytes 393224 | tf_op jit(solution)/shard_map/ppermute | solution.py:59
  (12 other events, 24.6 us)
where the time goes:
time: 111 us
  Pallas kernels  64.6 us (58%)
  starting transfers between devices  21.5 us (19%)
  waiting for transfers between devices  20.7 us (19%)
  other arithmetic  2.28 us (2%)
  local copies, waits for them, and re-layouts  1.81 us (2%)
    pallas_call x2, Pallas kernels, stack_bin(): pl.pallas_call(functools.partial(stack_kernel, (len(whole), len(split), l...  62.4 us
    ppermute x14, starting transfers between devices, shift(): return lax.ppermute(value, axis, perm)  20.1 us
    ppermute x14, waiting for transfers between devices, shift(): return lax.ppermute(value, axis, perm)  19.6 us
    concatenate x2, other arithmetic, gather_windows(): block = jnp.concatenate(line, axis=0)  2.28 us
  transfers between devices with their start and end apart: 24, of which 11 were waited for; matrix products, arithmetic and copies ran while one was open for 2% of the time, Pallas kernels for 28%

commit v1 on v0

v1 whole, which is shorter than its diff:
```python
import functools
import math

import jax
import jax.numpy as jnp
from jax import lax
from jax.experimental import pallas as pl
from jax.experimental.pallas import tpu as pltpu
from jax.sharding import PartitionSpec as P

BLOCK = 128
MXU = 256


def whiten_kernel(spectra_ref, *out_refs):
    freqs = spectra_ref.shape[0]
    power = None
    for freq in range(freqs):
        slab = spectra_ref[freq]
        term = jnp.sum(slab * slab, axis=1, keepdims=True)
        power = term if power is None else power + term
    floor = jnp.maximum(jnp.sqrt(power / freqs), 1.0)
    for freq in range(freqs):
        out_refs[freq][...] = (spectra_ref[freq] / floor).astype(jnp.bfloat16)


def whiten(spectra):
    freqs, windows, parts, channels = spectra.shape
    shape = jax.ShapeDtypeStruct((windows, parts, channels), jnp.bfloat16)
    slabs = pl.pallas_call(whiten_kernel, out_shape=[shape] * freqs, name="whiten")(spectra)
    return [slab.reshape(windows * parts, channels) for slab in slabs]


def shift(value, axis, step, inner=1):
    size = lax.axis_size(axis)
    stops = size // inner
    perm = [(at, (at // inner + step) % stops * inner + at % inner) for at in range(size)]
    return lax.ppermute(value, axis, perm)


def gather_line(own):
    line = [own] + [shift(own, "col", step) for step in range(1, lax.axis_size("col"))]
    return jnp.concatenate(line, axis=0)


def row_cores():
    return 2 if lax.axis_size("row") % 2 == 0 else 1


def gather_cross(block):
    cores = row_cores()
    along_row = [
        shift(block, "row", step, cores) for step in range(1, lax.axis_size("row") // cores)
    ]
    along_win = [shift(block, "win", step) for step in range(1, lax.axis_size("win"))]
    return along_row, along_win


def gather_rest(block, along_row, along_win):
    cores = row_cores()
    half = block.shape[1] // 2
    whole = [block] + along_row + along_win
    split = []
    for row_step, from_row in enumerate(along_row, 1):
        for win_step, from_win in enumerate(along_win, 1):
            low = shift(from_win[:, :half], "row", row_step, cores)
            high = shift(from_row[:, half:], "win", win_step)
            split.append((low, high))
    if cores == 2:
        swap = functools.partial(
            lax.ppermute,
            axis_name="row",
            perm=[(at, at ^ 1) for at in range(lax.axis_size("row"))],
        )
        whole = whole + [swap(value) for value in whole]
        split = split + [(swap(low), swap(high)) for low, high in split]
    return whole, split


def gather_windows(slabs):
    gathered = []
    after = None
    for own in slabs:
        if after is not None:
            own, after = lax.optimization_barrier((own, after[0])), after[1]
            own = own[0]
        block = gather_line(own)
        sent = block
        if after is not None:
            sent = lax.optimization_barrier((block, after))[0]
        along_row, along_win = gather_cross(sent)
        gathered.append(gather_rest(block, along_row, along_win))
        after = (block, along_row + along_win)
    return gathered


def stack_kernel(counts, freq, scale, pack, rows_ref, cols_ref, *refs):
    whole_count, split_count, aliased = counts
    whole = refs[:whole_count]
    low = refs[whole_count : whole_count + split_count]
    high = refs[whole_count + split_count : whole_count + 2 * split_count]
    out_ref, left_ref, right_ref, ring_ref, sems = refs[whole_count + 2 * split_count + aliased :]
    copies, _, width = left_ref.shape
    depth = right_ref.shape[1]
    slots, tiles, _, row_count, _ = ring_ref.shape
    chunks = pack // copies

    offset = lax.axis_index("win") * row_count
    pick_at = lax.broadcasted_iota(jnp.int32, (2 * row_count, 2 * BLOCK), 0)
    pick_lane = lax.broadcasted_iota(jnp.int32, (2 * row_count, 2 * BLOCK), 1)
    want = pick_at % row_count + offset + pick_at // row_count * BLOCK
    pick = (pick_lane == want).astype(jnp.bfloat16)
    turn_at = lax.broadcasted_iota(jnp.int32, (depth, depth), 0)
    turn_lane = lax.broadcasted_iota(jnp.int32, (depth, depth), 1)
    turn = jnp.where(
        turn_at % 2 == 1,
        jnp.where(turn_lane == turn_at - 1, -1.0, 0.0),
        jnp.where(turn_lane == turn_at + 1, 1.0, 0.0),
    ).astype(jnp.bfloat16)
    place = lax.broadcasted_iota(jnp.int32, (2 * row_count, width), 1) // depth

    def prepare(halves, first, pairs):
        def body(at, carry):
            here = pl.multiple_of((at + first) * 2 * BLOCK, 2 * BLOCK)
            near = pl.multiple_of(at * 2 * BLOCK, 2 * BLOCK)
            pieces = [ref[:, pl.ds(here, 2 * BLOCK)] for ref in whole]
            pieces += [ref[:, pl.ds(near, 2 * BLOCK)] for ref in halves]
            rows = jnp.concatenate(pieces, axis=0)
            turned = jnp.dot(turn, rows, preferred_element_type=jnp.float32).astype(jnp.bfloat16)
            left = lax.dot_general(
                pick,
                jnp.concatenate([rows] * copies, axis=0),
                (((1,), (1,)), ((), ())),
                preferred_element_type=jnp.float32,
            )
            where = pl.multiple_of((at + first) * 2 * row_count, 2 * row_count)
            for copy in range(copies):
                only = left if copies == 1 else jnp.where(place == copy, left, 0.0)
                left_ref[copy, pl.ds(where, 2 * row_count), :] = only.astype(jnp.bfloat16)
            for half in range(2):
                lanes = slice(half * BLOCK, (half + 1) * BLOCK)
                right_ref[(at + first) * 2 + half, :, :BLOCK] = rows[:, lanes]
                right_ref[(at + first) * 2 + half, :, BLOCK:] = turned[:, lanes]
            return carry

        lax.fori_loop(0, pairs, body, 0, unroll=8 if pairs % 8 == 0 else 1)

    half_pairs = whole[0].shape[1] // (4 * BLOCK)
    prepare(low, 0, half_pairs)
    prepare(high, half_pairs, half_pairs)

    def send(step, slot):
        return pltpu.make_async_copy(
            ring_ref.at[slot], out_ref.at[pl.ds(step * tiles, tiles), freq], sems.at[slot]
        )

    steps = out_ref.shape[0] // tiles

    def stack(step, carry):
        slot = lax.rem(step, slots)

        @pl.when(step >= slots)
        def _():
            send(step - slots, slot).wait()

        for group in range(tiles // pack):
            lefts = []
            rights = []
            for member in range(pack):
                at = step * tiles + group * pack + member
                left_at = pl.multiple_of(rows_ref[at] * row_count, row_count)
                left = left_ref[member % copies, pl.ds(left_at, row_count), :]
                if chunks > 1:
                    chunk = member // copies
                    empty = jnp.zeros_like(left)
                    left = jnp.concatenate(
                        [left if spot == chunk else empty for spot in range(chunks)], axis=1
                    )
                lefts.append(left)
                rights.append(right_ref[cols_ref[at]])
            product = jnp.dot(
                jnp.concatenate(lefts, axis=0),
                jnp.concatenate(rights, axis=0),
                preferred_element_type=jnp.float32,
            )
            product = product * scale
            for member in range(pack):
                mine = product[member * row_count : (member + 1) * row_count]
                ring_ref[slot, group * pack + member, 0] = mine[:, :BLOCK]
                ring_ref[slot, group * pack + member, 1] = mine[:, BLOCK:]
        send(step, slot).start()
        return carry

    lax.fori_loop(0, steps, stack, 0)
    for step in range(max(0, steps - slots), steps):
        send(step, step % slots).wait()


def stack_bin(freq, out_shape, tile_rows, tile_cols, whole, split, scale, so_far):
    low = [pair[0] for pair in split]
    high = [pair[1] for pair in split]
    pieces = whole + low + high
    channels = whole[0].shape[1]
    depth = sum(value.shape[0] for value in whole + low)
    tile_total, _, parts, row_count, _ = out_shape.shape
    pack = math.gcd(tile_total, max(1, MXU // depth))
    copies = min(pack, max(1, BLOCK // depth))
    tiles = max(size for size in range(pack, pack + 13) if tile_total % size + size % pack == 0)
    blocks = channels // BLOCK
    vmem = pl.BlockSpec(memory_space=pltpu.VMEM)
    smem = pl.BlockSpec(memory_space=pltpu.SMEM)
    in_specs = [smem, smem] + [vmem] * len(pieces)
    operands = [tile_rows, tile_cols] + pieces
    aliases = {}
    if so_far is not None:
        in_specs.append(pl.BlockSpec(memory_space=pl.ANY))
        aliases = {len(operands): 0}
        operands.append(so_far)
    slots = 4
    scratch = [
        ((copies, blocks * row_count, copies * depth), jnp.bfloat16),
        ((blocks, depth, 2 * BLOCK), jnp.bfloat16),
        ((slots, tiles, parts, row_count, BLOCK), jnp.float32),
    ]
    used = [(value.shape, value.dtype) for value in pieces] + scratch
    vmem_bytes = sum(math.prod(shape) * jnp.dtype(kind).itemsize for shape, kind in used)
    product = tile_total * row_count * 2 * BLOCK
    return pl.pallas_call(
        functools.partial(stack_kernel, (len(whole), len(split), len(aliases)), freq, scale, pack),
        out_shape=out_shape,
        in_specs=in_specs,
        out_specs=pl.BlockSpec(memory_space=pl.ANY),
        scratch_shapes=[pltpu.VMEM(*spec) for spec in scratch]
        + [pltpu.SemaphoreType.DMA((slots,))],
        input_output_aliases=aliases,
        cost_estimate=pl.CostEstimate(
            flops=2 * product * depth, bytes_accessed=4 * product, transcendentals=0
        ),
        compiler_params=pltpu.CompilerParams(vmem_limit_bytes=vmem_bytes + 8 * 1024 * 1024),
        name="stack",
    )(*operands)


def on_device(spectra, tile_rows, tile_cols):
    window_total = (
        spectra.shape[2] * lax.axis_size("row") * lax.axis_size("col") * lax.axis_size("win")
    )
    scale = float(1.0 / window_total**0.5)
    slabs = whiten(spectra[0])
    row_count = BLOCK // lax.axis_size("win")
    out_shape = jax.ShapeDtypeStruct(
        (tile_rows.shape[0], len(slabs), 2, row_count, BLOCK), jnp.float32
    )
    out = None
    for freq, (whole, split) in enumerate(gather_windows(slabs)):
        out = stack_bin(freq, out_shape, tile_rows, tile_cols, whole, split, scale, out)
    return out


def solution(mesh):
    in_specs = (P("win", None, ("row", "col"), None, None), P(("row", "col")), P(("row", "col")))
    out_specs = P(("row", "col"), None, None, "win", None)
    return jax.shard_map(
        on_device, mesh=mesh, in_specs=in_specs, out_specs=out_specs, check_vma=False
    )
```

time: 111 us -> 79.9 us (0.72)
  Pallas kernels: 64.6 us -> 36.2 us
  waiting for transfers between devices: 20.7 us -> 18.1 us
    pallas_call x2, Pallas kernels: 62.4 us -> 34 us  [stack_bin(): pl.pallas_call(functools.partial(stack_kernel, (len(whole), len(split), l...]
    ppermute x14, waiting for transfers between devices: 19.6 us -> 18.1 us  [shift(): return lax.ppermute(value, axis, perm)]
    ppermute x10, waiting for transfers between devices: 1.18 us -> 0.03 us  [the longest x6 0.02 us: gather_rest(): whole = whole + [swap(value) for value in whole]]
  transfers between devices with their start and end apart: 24 -> 24, of which waited for: 11 -> 11; matrix products, arithmetic and copies ran while one was open for 2% -> 1% of each run, Pallas kernels for 28% -> 22%
where the time goes in v1:
time: 79.9 us; the launch traced here: 79 us
  Pallas kernels  36.2 us (45%)
  starting transfers between devices  20.9 us (26%)
  waiting for transfers between devices  18.1 us (23%)
  other arithmetic  2.28 us (3%)
  local copies, waits for them, and re-layouts  1.41 us (2%)
    pallas_call x2, Pallas kernels, stack_bin(): pl.pallas_call(functools.partial(stack_kernel, (len(whole), len(split), l...  34 us
    ppermute x14, starting transfers between devices, shift(): return lax.ppermute(value, axis, perm)  19.8 us
    ppermute x14, waiting for transfers between devices, shift(): return lax.ppermute(value, axis, perm)  18.1 us
    concatenate x2, other arithmetic, gather_line(): return jnp.concatenate(line, axis=0)  2.28 us
    pallas_call x1, Pallas kernels, whiten(): pl.pallas_call(whiten_kernel, out_shape=[shape] * freqs, name='whiten')  2.19 us
  transfers between devices with their start and end apart: 24, of which 11 were waited for; matrix products, arithmetic and copies ran while one was open for 1% of the time, Pallas kernels for 22%

profile of v1, /device:TPU:0, one launch (start us, length us, event | category | flops | bytes accessed | tf_op | source)
XLA Modules:
  0.0 79.0 jit_solution(11215120433711302144)
XLA Ops:
  0.0 2.2 %whiten.1 = (bf16[1,2,16384]{2,1,0:T(2,128)(2,1)}, bf16[1,2,16384]{2,1,0:T(2,128)(2,1)}) custom-call(f32[2,1,2,16384]{3,2,1,0:T(2,128)} %bitcast.3), custom_call_target="tpu_custom_call" | custom-call | tf_op jit(solution)/shard_map/whiten/pallas_call | solution.py:30
  2.2 5.0 %collective-permute-start.2 = (bf16[2,16384]{1,0:T(2,128)(2,1)}, bf16[2,16384]{1,0:T(2,128)(2,1)S(1)}, u32[]{:S(2)}, u32[]{:S(2)}) collective-permute-start(bf16[2,16384]{1,0:T(2,128)(2,1)} %bitcast.8), channel_id=1, source_target_pairs={{0,6},{2,0},{4,2},{6,4},{1,7},{3,1},{5,3},{7,5},{8,14},{10,8},{12,... | collective-permute-start | bytes 196616 | tf_op jit(solution)/shard_map/ppermute | solution.py:38
  7.2 1.0 %collective-permute-start = (bf16[2,16384]{1,0:T(2,128)(2,1)}, bf16[2,16384]{1,0:T(2,128)(2,1)S(1)}, u32[]{:S(2)}, u32[]{:S(2)}) collective-permute-start(bf16[2,16384]{1,0:T(2,128)(2,1)} %bitcast.10), channel_id=1, source_target_pairs={{0,2},{2,4},{4,6},{6,0},{1,3},{3,5},{5,7},{7,1},{8,10},{10,12},{12... | collective-permute-start | bytes 196616 | tf_op jit(solution)/shard_map/ppermute | solution.py:38
  8.3 1.8 %collective-permute-done.2 = bf16[2,16384]{1,0:T(2,128)(2,1)S(1)} collective-permute-done((bf16[2,16384]{1,0:T(2,128)(2,1)}, bf16[2,16384]{1,0:T(2,128)(2,1)S(1)}, u32[]{:S(2)}, u32[]{:S(2)}) %collective-permute-start.2) | collective-permute-done | bytes 65568 | tf_op jit(solution)/shard_map/ppermute | solution.py:38
  10.1 3.9 %collective-permute-done.1 = bf16[2,16384]{1,0:T(2,128)(2,1)S(1)} collective-permute-done((bf16[2,16384]{1,0:T(2,128)(2,1)}, bf16[2,16384]{1,0:T(2,128)(2,1)S(1)}, u32[]{:S(2)}, u32[]{:S(2)}) %collective-permute-start.1) | collective-permute-done | bytes 65568 | tf_op jit(solution)/shard_map/ppermute | solution.py:38
  13.9 1.1 %pad_maximum_fusion.refs_0_ = bf16[8,16384]{1,0:T(8,128)(2,1)S(1)} fusion(bf16[2,16384]{1,0:T(2,128)(2,1)S(1)} %collective-permute-done.2, bf16[2,16384]{1,0:T(2,128)(2,1)S(1)} %collective-permute-done.1, bf16[2,16384]{1,0:T(2,128)(2,1)S(1)} %collective-permute-done, bf16[2,16384]{1,0:T(2,128)(2,1)} %bitcast.11), kind=kLoop, calls=%fused_computation | loop fusion | flops 1048576 | bytes 524288 | tf_op jit(solution)/shard_map/concatenate | solution.py:43
  15.1 1.9 %collective-permute-start.5 = (bf16[2,16384]{1,0:T(2,128)(2,1)}, bf16[2,16384]{1,0:T(2,128)(2,1)S(1)}, u32[]{:S(2)}, u32[]{:S(2)}) collective-permute-start(bf16[2,16384]{1,0:T(2,128)(2,1)} %bitcast.4), channel_id=1, source_target_pairs={{0,6},{2,0},{4,2},{6,4},{1,7},{3,1},{5,3},{7,5},{8,14},{10,8},{12,... | collective-permute-start | bytes 196616 | tf_op jit(solution)/shard_map/ppermute | solution.py:38
  17.0 1.9 %collective-permute-start.3 = (bf16[2,16384]{1,0:T(2,128)(2,1)}, bf16[2,16384]{1,0:T(2,128)(2,1)S(1)}, u32[]{:S(2)}, u32[]{:S(2)}) collective-permute-start(bf16[2,16384]{1,0:T(2,128)(2,1)} %bitcast.6), channel_id=1, source_target_pairs={{0,2},{2,4},{4,6},{6,0},{1,3},{3,5},{5,7},{7,1},{8,10},{10,12},{12... | collective-permute-start | bytes 196616 | tf_op jit(solution)/shard_map/ppermute | solution.py:38
  18.9 1.5 %collective-permute-start.7 = (bf16[8,16384]{1,0:T(8,128)(2,1)S(1)}, bf16[8,16384]{1,0:T(8,128)(2,1)S(1)}, u32[]{:S(2)}, u32[]{:S(2)}) collective-permute-start(bf16[8,16384]{1,0:T(8,128)(2,1)S(1)} %pad_maximum_fusion.refs_0_), channel_id=1, source_target_pairs={{0,1},{1,0},{2,3},{3,2},{4,5},{5,4},{6,7},{7,6},{8,9},{9,8},{10,11... | collective-permute-start | bytes 786440 | tf_op jit(solution)/shard_map/ppermute | solution.py:38
  20.4 1.5 %collective-permute-start.6 = (bf16[8,16384]{1,0:T(8,128)(2,1)S(1)}, bf16[8,16384]{1,0:T(8,128)(2,1)S(1)}, u32[]{:S(2)}, u32[]{:S(2)}) collective-permute-start(bf16[8,16384]{1,0:T(8,128)(2,1)S(1)} %pad_maximum_fusion.refs_0_), channel_id=1, source_target_pairs={{0,16},{8,24},{16,0},{24,8},{1,17},{9,25},{17,1},{25,9},{2,18},{10... | collective-permute-start | bytes 786440 | tf_op jit(solution)/shard_map/ppermute | solution.py:38
  21.9 2.1 %collective-permute-done.4 = bf16[2,16384]{1,0:T(2,128)(2,1)S(1)} collective-permute-done((bf16[2,16384]{1,0:T(2,128)(2,1)}, bf16[2,16384]{1,0:T(2,128)(2,1)S(1)}, u32[]{:S(2)}, u32[]{:S(2)}) %collective-permute-start.4) | collective-permute-done | bytes 65568 | tf_op jit(solution)/shard_map/ppermute | solution.py:38
  24.0 1.1 %pad_maximum_fusion.1.refs_0_ = bf16[8,16384]{1,0:T(8,128)(2,1)S(1)} fusion(bf16[2,16384]{1,0:T(2,128)(2,1)S(1)} %collective-permute-done.5, bf16[2,16384]{1,0:T(2,128)(2,1)S(1)} %collective-permute-done.4, bf16[2,16384]{1,0:T(2,128)(2,1)S(1)} %collective-permute-done.3, bf16[2,16384]{1,0:T(2,128)(2,1)} %bitcast.7), kind=kLoop, calls=%fused_computation.1 | loop fusion | flops 1048576 | bytes 524288 | tf_op jit(solution)/shard_map/concatenate | solution.py:43
  25.2 0.6 collective-permute-done.7.refs_2_
  25.8 1.6 %collective-permute-start.20 = (bf16[8,8192]{1,0:T(8,128)(2,1)S(1)}, bf16[8,8192]{1,0:T(8,128)(2,1)S(1)}, u32[]{:S(2)}, u32[]{:S(2)}) collective-permute-start(bf16[8,8192]{1,0:T(8,128)(2,1)S(1)} %slice.18), channel_id=1, source_target_pairs={{0,16},{8,24},{16,0},{24,8},{1,17},{9,25},{17,1},{25,9},{2,18},{10... | collective-permute-start | bytes 393224 | tf_op jit(solution)/shard_map/ppermute | solution.py:38
  27.3 0.4 collective-permute-done.6.refs_1_
  27.8 1.1 %collective-permute-start.22 = (bf16[8,8192]{1,0:T(8,128)(2,1)S(1)}, bf16[8,8192]{1,0:T(8,128)(2,1)S(1)}, u32[]{:S(2)}, u32[]{:S(2)}) collective-permute-start(bf16[8,8192]{1,0:T(8,128)(2,1)S(1)} %slice.19), channel_id=1, source_target_pairs={{0,1},{1,0},{2,3},{3,2},{4,5},{5,4},{6,7},{7,6},{8,9},{9,8},{10,11... | collective-permute-start | bytes 393224 | tf_op jit(solution)/shard_map/ppermute | solution.py:38
  28.9 0.9 %collective-permute-start.9 = (bf16[8,16384]{1,0:T(8,128)(2,1)S(1)}, bf16[8,16384]{1,0:T(8,128)(2,1)S(1)}, u32[]{:S(2)}, u32[]{:S(2)}) collective-permute-start(bf16[8,16384]{1,0:T(8,128)(2,1)S(1)} %pad_maximum_fusion.1.refs_0_), channel_id=1, source_target_pairs={{0,1},{1,0},{2,3},{3,2},{4,5},{5,4},{6,7},{7,6},{8,9},{9,8},{10,11... | collective-permute-start | bytes 786440 | tf_op jit(solution)/shard_map/ppermute | solution.py:38
  29.9 1.5 %collective-permute-start.8 = (bf16[8,16384]{1,0:T(8,128)(2,1)S(1)}, bf16[8,16384]{1,0:T(8,128)(2,1)S(1)}, u32[]{:S(2)}, u32[]{:S(2)}) collective-permute-start(bf16[8,16384]{1,0:T(8,128)(2,1)S(1)} %pad_maximum_fusion.1.refs_0_), channel_id=1, source_target_pairs={{0,16},{8,24},{16,0},{24,8},{1,17},{9,25},{17,1},{25,9},{2,18},{10... | collective-permute-start | bytes 786440 | tf_op jit(solution)/shard_map/ppermute | solution.py:38
  31.4 0.8 collective-permute-done.20.refs_6_
  32.1 0.9 %collective-permute-done.22.refs_8_ = bf16[8,8192]{1,0:T(8,128)(2,1)S(1)} collective-permute-done((bf16[8,8192]{1,0:T(8,128)(2,1)S(1)}, bf16[8,8192]{1,0:T(8,128)(2,1)S(1)}, u32[]{:S(2)}, u32[]{:S(2)}) %collective-permute-start.22) | collective-permute-done | bytes 131104 | tf_op jit(solution)/shard_map/ppermute | solution.py:38
  33.1 2.8 %collective-permute-done.9.refs_2_ = bf16[8,16384]{1,0:T(8,128)(2,1)S(1)} collective-permute-done((bf16[8,16384]{1,0:T(8,128)(2,1)S(1)}, bf16[8,16384]{1,0:T(8,128)(2,1)S(1)}, u32[]{:S(2)}, u32[]{:S(2)}) %collective-permute-start.9) | collective-permute-done | bytes 262176 | tf_op jit(solution)/shard_map/ppermute | solution.py:38
  35.9 0.4 collective-permute-done.8.refs_1_
  36.4 0.4 collective-permute-start.10
  36.9 1.5 %collective-permute-start.13 = (bf16[8,8192]{1,0:T(8,128)(2,1)S(1)}, bf16[8,8192]{1,0:T(8,128)(2,1)S(1)}, u32[]{:S(2)}, u32[]{:S(2)}) collective-permute-start(bf16[8,8192]{1,0:T(8,128)(2,1)S(1)} %slice.16), channel_id=1, source_target_pairs={{0,16},{8,24},{16,0},{24,8},{1,17},{9,25},{17,1},{25,9},{2,18},{10... | collective-permute-start | bytes 393224 | tf_op jit(solution)/shard_map/ppermute | solution.py:38
  38.4 0.3 collective-permute-start.15
  38.7 0.5 collective-permute-start.11
  39.2 3.2 %collective-permute-done.13.refs_6_ = bf16[8,8192]{1,0:T(8,128)(2,1)S(1)} collective-permute-done((bf16[8,8192]{1,0:T(8,128)(2,1)S(1)}, bf16[8,8192]{1,0:T(8,128)(2,1)S(1)}, u32[]{:S(2)}, u32[]{:S(2)}) %collective-permute-start.13) | collective-permute-done | bytes 131104 | tf_op jit(solution)/shard_map/ppermute | solution.py:38
  42.4 1.2 %collective-permute-done.15.refs_8_ = bf16[8,8192]{1,0:T(8,128)(2,1)S(1)} collective-permute-done((bf16[8,8192]{1,0:T(8,128)(2,1)S(1)}, bf16[8,8192]{1,0:T(8,128)(2,1)S(1)}, u32[]{:S(2)}, u32[]{:S(2)}) %collective-permute-start.15) | collective-permute-done | bytes 131104 | tf_op jit(solution)/shard_map/ppermute | solution.py:38
  43.6 0.7 copy-done
  44.3 0.7 copy-done.1
  45.0 17.0 %stack.2.refs_10_ = f32[516,2,2,64,128]{4,3,2,1,0:T(8,128)} custom-call(s32[516]{0:T(1024)S(1)} %copy-done, s32[516]{0:T(1024)S(1)} %copy-done.1, bf16[8,16384]{1,0:T(8,128)(2,1)S(1)} %pad_maximum_fusion.refs_0_, bf16[8,16384]{1,0:T(8,128)(2,1)S(1)} %collective-permute-done.6.refs_1_, bf16[8,16384]{1,0:T(8,128)(2,1)S(1)} %collective-permute-done.7.refs_2_, ...), custom_call_target="tpu_custom_call" | custom-call | flops 1082130432 | bytes 33816576 | tf_op jit(solution)/shard_map/stack/pallas_call | solution.py:228
  62.0 17.0 %stack.3 = f32[516,2,2,64,128]{4,3,2,1,0:T(8,128)} custom-call(s32[516]{0:T(1024)S(1)} %copy-done, s32[516]{0:T(1024)S(1)} %copy-done.1, bf16[8,16384]{1,0:T(8,128)(2,1)S(1)} %pad_maximum_fusion.1.refs_0_, bf16[8,16384]{1,0:T(8,128)(2,1)S(1)} %collective-permute-done.8.refs_1_, ...), custom_call_target="tpu_custom_call", output_to_operand_aliasing={{}: (12, {})} | custom-call | flops 1082130432 | bytes 33816576 | tf_op jit(solution)/shard_map/stack/pallas_call | solution.py:228
  (29 shorter events, 0.2 us)
Async XLA Ops:
  2.2 7.9 %collective-permute-start.2 = (bf16[2,16384]{1,0:T(2,128)(2,1)}, bf16[2,16384]{1,0:T(2,128)(2,1)S(1)}, u32[]{:S(2)}, u32[]{:S(2)}) collective-permute-start(bf16[2,16384]{1,0:T(2,128)(2,1)} %bitcast.8), channel_id=1, source_target_pairs={{0,6},{2,0},{4,2},{6,4},{1,7},{3,1},{5,3},{7,5},{8,14},{10,8},{12,... | collective-permute-start | bytes 196616 | tf_op jit(solution)/shard_map/ppermute | solution.py:38
  7.2 6.7 %collective-permute-start.1 = (bf16[2,16384]{1,0:T(2,128)(2,1)}, bf16[2,16384]{1,0:T(2,128)(2,1)S(1)}, u32[]{:S(2)}, u32[]{:S(2)}) collective-permute-start(bf16[2,16384]{1,0:T(2,128)(2,1)} %bitcast.9), channel_id=1, source_target_pairs={{0,4},{2,6},{4,0},{6,2},{1,5},{3,7},{5,1},{7,3},{8,12},{10,14},{12... | collective-permute-start | bytes 196616 | tf_op jit(solution)/shard_map/ppermute | solution.py:38
  7.2 6.7 %collective-permute-start = (bf16[2,16384]{1,0:T(2,128)(2,1)}, bf16[2,16384]{1,0:T(2,128)(2,1)S(1)}, u32[]{:S(2)}, u32[]{:S(2)}) collective-permute-start(bf16[2,16384]{1,0:T(2,128)(2,1)} %bitcast.10), channel_id=1, source_target_pairs={{0,2},{2,4},{4,6},{6,0},{1,3},{3,5},{5,7},{7,1},{8,10},{10,12},{12... | collective-permute-start | bytes 196616 | tf_op jit(solution)/shard_map/ppermute | solution.py:38
  15.1 6.9 %collective-permute-start.5 = (bf16[2,16384]{1,0:T(2,128)(2,1)}, bf16[2,16384]{1,0:T(2,128)(2,1)S(1)}, u32[]{:S(2)}, u32[]{:S(2)}) collective-permute-start(bf16[2,16384]{1,0:T(2,128)(2,1)} %bitcast.4), channel_id=1, source_target_pairs={{0,6},{2,0},{4,2},{6,4},{1,7},{3,1},{5,3},{7,5},{8,14},{10,8},{12,... | collective-permute-start | bytes 196616 | tf_op jit(solution)/shard_map/ppermute | solution.py:38
  17.0 7.0 %collective-permute-start.4 = (bf16[2,16384]{1,0:T(2,128)(2,1)}, bf16[2,16384]{1,0:T(2,128)(2,1)S(1)}, u32[]{:S(2)}, u32[]{:S(2)}) collective-permute-start(bf16[2,16384]{1,0:T(2,128)(2,1)} %bitcast.5), channel_id=1, source_target_pairs={{0,4},{2,6},{4,0},{6,2},{1,5},{3,7},{5,1},{7,3},{8,12},{10,14},{12... | collective-permute-start | bytes 196616 | tf_op jit(solution)/shard_map/ppermute | solution.py:38
  17.0 7.0 %collective-permute-start.3 = (bf16[2,16384]{1,0:T(2,128)(2,1)}, bf16[2,16384]{1,0:T(2,128)(2,1)S(1)}, u32[]{:S(2)}, u32[]{:S(2)}) collective-permute-start(bf16[2,16384]{1,0:T(2,128)(2,1)} %bitcast.6), channel_id=1, source_target_pairs={{0,2},{2,4},{4,6},{6,0},{1,3},{3,5},{5,7},{7,1},{8,10},{10,12},{12... | collective-permute-start | bytes 196616 | tf_op jit(solution)/shard_map/ppermute | solution.py:38
  18.9 6.9 %collective-permute-start.7 = (bf16[8,16384]{1,0:T(8,128)(2,1)S(1)}, bf16[8,16384]{1,0:T(8,128)(2,1)S(1)}, u32[]{:S(2)}, u32[]{:S(2)}) collective-permute-start(bf16[8,16384]{1,0:T(8,128)(2,1)S(1)} %pad_maximum_fusion.refs_0_), channel_id=1, source_target_pairs={{0,1},{1,0},{2,3},{3,2},{4,5},{5,4},{6,7},{7,6},{8,9},{9,8},{10,11... | collective-permute-start | bytes 786440 | tf_op jit(solution)/shard_map/ppermute | solution.py:38
  20.4 7.3 %collective-permute-start.6 = (bf16[8,16384]{1,0:T(8,128)(2,1)S(1)}, bf16[8,16384]{1,0:T(8,128)(2,1)S(1)}, u32[]{:S(2)}, u32[]{:S(2)}) collective-permute-start(bf16[8,16384]{1,0:T(8,128)(2,1)S(1)} %pad_maximum_fusion.refs_0_), channel_id=1, source_target_pairs={{0,16},{8,24},{16,0},{24,8},{1,17},{9,25},{17,1},{25,9},{2,18},{10... | collective-permute-start | bytes 786440 | tf_op jit(solution)/shard_map/ppermute | solution.py:38
  25.8 6.4 %collective-permute-start.20 = (bf16[8,8192]{1,0:T(8,128)(2,1)S(1)}, bf16[8,8192]{1,0:T(8,128)(2,1)S(1)}, u32[]{:S(2)}, u32[]{:S(2)}) collective-permute-start(bf16[8,8192]{1,0:T(8,128)(2,1)S(1)} %slice.18), channel_id=1, source_target_pairs={{0,16},{8,24},{16,0},{24,8},{1,17},{9,25},{17,1},{25,9},{2,18},{10... | collective-permute-start | bytes 393224 | tf_op jit(solution)/shard_map/ppermute | solution.py:38
  27.8 5.3 %collective-permute-start.22 = (bf16[8,8192]{1,0:T(8,128)(2,1)S(1)}, bf16[8,8192]{1,0:T(8,128)(2,1)S(1)}, u32[]{:S(2)}, u32[]{:S(2)}) collective-permute-start(bf16[8,8192]{1,0:T(8,128)(2,1)S(1)} %slice.19), channel_id=1, source_target_pairs={{0,1},{1,0},{2,3},{3,2},{4,5},{5,4},{6,7},{7,6},{8,9},{9,8},{10,11... | collective-permute-start | bytes 393224 | tf_op jit(solution)/shard_map/ppermute | solution.py:38
  28.9 6.9 %collective-permute-start.9 = (bf16[8,16384]{1,0:T(8,128)(2,1)S(1)}, bf16[8,16384]{1,0:T(8,128)(2,1)S(1)}, u32[]{:S(2)}, u32[]{:S(2)}) collective-permute-start(bf16[8,16384]{1,0:T(8,128)(2,1)S(1)} %pad_maximum_fusion.1.refs_0_), channel_id=1, source_target_pairs={{0,1},{1,0},{2,3},{3,2},{4,5},{5,4},{6,7},{7,6},{8,9},{9,8},{10,11... | collective-permute-start | bytes 786440 | tf_op jit(solution)/shard_map/ppermute | solution.py:38
  29.9 6.4 %collective-permute-start.8 = (bf16[8,16384]{1,0:T(8,128)(2,1)S(1)}, bf16[8,16384]{1,0:T(8,128)(2,1)S(1)}, u32[]{:S(2)}, u32[]{:S(2)}) collective-permute-start(bf16[8,16384]{1,0:T(8,128)(2,1)S(1)} %pad_maximum_fusion.1.refs_0_), channel_id=1, source_target_pairs={{0,16},{8,24},{16,0},{24,8},{1,17},{9,25},{17,1},{25,9},{2,18},{10... | collective-permute-start | bytes 786440 | tf_op jit(solution)/shard_map/ppermute | solution.py:38
  31.4 5.1 %collective-permute-start.17 = (bf16[8,16384]{1,0:T(8,128)(2,1)S(1)}, bf16[8,16384]{1,0:T(8,128)(2,1)S(1)}, u32[]{:S(2)}, u32[]{:S(2)}) collective-permute-start(bf16[8,16384]{1,0:T(8,128)(2,1)S(1)} %pad_maximum_fusion.refs_0_), channel_id=1, source_target_pairs={{0,8},{8,0},{16,24},{24,16},{1,9},{9,1},{17,25},{25,17},{2,10},{10... | collective-permute-start | bytes 786440 | tf_op jit(solution)/shard_map/ppermute | solution.py:75
  32.1 4.7 %collective-permute-start.19 = (bf16[8,16384]{1,0:T(8,128)(2,1)S(1)}, bf16[8,16384]{1,0:T(8,128)(2,1)S(1)}, u32[]{:S(2)}, u32[]{:S(2)}) collective-permute-start(bf16[8,16384]{1,0:T(8,128)(2,1)S(1)} %collective-permute-done.7.refs_2_), channel_id=1, source_target_pairs={{0,8},{8,0},{16,24},{24,16},{1,9},{9,1},{17,25},{25,17},{2,10},{10... | collective-permute-start | bytes 786440 | tf_op jit(solution)/shard_map/ppermute | solution.py:75
  33.1 5.3 %collective-permute-start.18 = (bf16[8,16384]{1,0:T(8,128)(2,1)S(1)}, bf16[8,16384]{1,0:T(8,128)(2,1)S(1)}, u32[]{:S(2)}, u32[]{:S(2)}) collective-permute-start(bf16[8,16384]{1,0:T(8,128)(2,1)S(1)} %collective-permute-done.6.refs_1_), channel_id=1, source_target_pairs={{0,8},{8,0},{16,24},{24,16},{1,9},{9,1},{17,25},{25,17},{2,10},{10... | collective-permute-start | bytes 786440 | tf_op jit(solution)/shard_map/ppermute | solution.py:75
  35.9 2.8 %collective-permute-start.21 = (bf16[8,8192]{1,0:T(8,128)(2,1)S(1)}, bf16[8,8192]{1,0:T(8,128)(2,1)S(1)}, u32[]{:S(2)}, u32[]{:S(2)}) collective-permute-start(bf16[8,8192]{1,0:T(8,128)(2,1)S(1)} %collective-permute-done.20.refs_6_), channel_id=1, source_target_pairs={{0,8},{8,0},{16,24},{24,16},{1,9},{9,1},{17,25},{25,17},{2,10},{10... | collective-permute-start | bytes 393224 | tf_op jit(solution)/shard_map/ppermute | solution.py:76
  36.3 2.4 %collective-permute-start.23 = (bf16[8,8192]{1,0:T(8,128)(2,1)S(1)}, bf16[8,8192]{1,0:T(8,128)(2,1)S(1)}, u32[]{:S(2)}, u32[]{:S(2)}) collective-permute-start(bf16[8,8192]{1,0:T(8,128)(2,1)S(1)} %collective-permute-done.22.refs_8_), channel_id=1, source_target_pairs={{0,8},{8,0},{16,24},{24,16},{1,9},{9,1},{17,25},{25,17},{2,10},{10... | collective-permute-start | bytes 393224 | tf_op jit(solution)/shard_map/ppermute | solution.py:76
  36.4 25.5 %collective-permute-start.10 = (bf16[8,16384]{1,0:T(8,128)(2,1)S(1)}, bf16[8,16384]{1,0:T(8,128)(2,1)S(1)}, u32[]{:S(2)}, u32[]{:S(2)}) collective-permute-start(bf16[8,16384]{1,0:T(8,128)(2,1)S(1)} %pad_maximum_fusion.1.refs_0_), channel_id=1, source_target_pairs={{0,8},{8,0},{16,24},{24,16},{1,9},{9,1},{17,25},{25,17},{2,10},{10... | collective-permute-start | bytes 786440 | tf_op jit(solution)/shard_map/ppermute | solution.py:75
  36.9 5.5 %collective-permute-start.13 = (bf16[8,8192]{1,0:T(8,128)(2,1)S(1)}, bf16[8,8192]{1,0:T(8,128)(2,1)S(1)}, u32[]{:S(2)}, u32[]{:S(2)}) collective-permute-start(bf16[8,8192]{1,0:T(8,128)(2,1)S(1)} %slice.16), channel_id=1, source_target_pairs={{0,16},{8,24},{16,0},{24,8},{1,17},{9,25},{17,1},{25,9},{2,18},{10... | collective-permute-start | bytes 393224 | tf_op jit(solution)/shard_map/ppermute | solution.py:38
  38.4 5.2 %collective-permute-start.15 = (bf16[8,8192]{1,0:T(8,128)(2,1)S(1)}, bf16[8,8192]{1,0:T(8,128)(2,1)S(1)}, u32[]{:S(2)}, u32[]{:S(2)}) collective-permute-start(bf16[8,8192]{1,0:T(8,128)(2,1)S(1)} %slice.17), channel_id=1, source_target_pairs={{0,1},{1,0},{2,3},{3,2},{4,5},{5,4},{6,7},{7,6},{8,9},{9,8},{10,11... | collective-permute-start | bytes 393224 | tf_op jit(solution)/shard_map/ppermute | solution.py:38
  38.7 23.3 %collective-permute-start.12 = (bf16[8,16384]{1,0:T(8,128)(2,1)S(1)}, bf16[8,16384]{1,0:T(8,128)(2,1)S(1)}, u32[]{:S(2)}, u32[]{:S(2)}) collective-permute-start(bf16[8,16384]{1,0:T(8,128)(2,1)S(1)} %collective-permute-done.9.refs_2_), channel_id=1, source_target_pairs={{0,8},{8,0},{16,24},{24,16},{1,9},{9,1},{17,25},{25,17},{2,10},{10... | collective-permute-start | bytes 786440 | tf_op jit(solution)/shard_map/ppermute | solution.py:75
  38.7 23.3 %collective-permute-start.11 = (bf16[8,16384]{1,0:T(8,128)(2,1)S(1)}, bf16[8,16384]{1,0:T(8,128)(2,1)S(1)}, u32[]{:S(2)}, u32[]{:S(2)}) collective-permute-start(bf16[8,16384]{1,0:T(8,128)(2,1)S(1)} %collective-permute-done.8.refs_1_), channel_id=1, source_target_pairs={{0,8},{8,0},{16,24},{24,16},{1,9},{9,1},{17,25},{25,17},{2,10},{10... | collective-permute-start | bytes 786440 | tf_op jit(solution)/shard_map/ppermute | solution.py:75
  42.4 19.5 %collective-permute-start.14 = (bf16[8,8192]{1,0:T(8,128)(2,1)S(1)}, bf16[8,8192]{1,0:T(8,128)(2,1)S(1)}, u32[]{:S(2)}, u32[]{:S(2)}) collective-permute-start(bf16[8,8192]{1,0:T(8,128)(2,1)S(1)} %collective-permute-done.13.refs_6_), channel_id=1, source_target_pairs={{0,8},{8,0},{16,24},{24,16},{1,9},{9,1},{17,25},{25,17},{2,10},{10... | collective-permute-start | bytes 393224 | tf_op jit(solution)/shard_map/ppermute | solution.py:76
  43.6 18.4 %collective-permute-start.16 = (bf16[8,8192]{1,0:T(8,128)(2,1)S(1)}, bf16[8,8192]{1,0:T(8,128)(2,1)S(1)}, u32[]{:S(2)}, u32[]{:S(2)}) collective-permute-start(bf16[8,8192]{1,0:T(8,128)(2,1)S(1)} %collective-permute-done.15.refs_8_), channel_id=1, source_target_pairs={{0,8},{8,0},{16,24},{24,16},{1,9},{9,1},{17,25},{25,17},{2,10},{10... | collective-permute-start | bytes 393224 | tf_op jit(solution)/shard_map/ppermute | solution.py:76
  43.6 0.7 copy-start
  44.3 0.7 copy-start.1

commit v2 on v1

v2 whole, which is shorter than its diff:
```python
import functools
import math

import jax
import jax.numpy as jnp
from jax import lax
from jax.experimental import pallas as pl
from jax.experimental.pallas import tpu as pltpu
from jax.sharding import PartitionSpec as P

BLOCK = 128
MXU = 256


def whiten_kernel(spectra_ref, *out_refs):
    freqs = spectra_ref.shape[0]
    power = None
    for freq in range(freqs):
        slab = spectra_ref[freq]
        term = jnp.sum(slab * slab, axis=1, keepdims=True)
        power = term if power is None else power + term
    floor = jnp.maximum(jnp.sqrt(power / freqs), 1.0)
    for freq in range(freqs):
        out_refs[freq][...] = (spectra_ref[freq] / floor).astype(jnp.bfloat16)


def whiten(spectra):
    freqs, windows, parts, channels = spectra.shape
    shape = jax.ShapeDtypeStruct((windows, parts, channels), jnp.bfloat16)
    slabs = pl.pallas_call(whiten_kernel, out_shape=[shape] * freqs, name="whiten")(spectra)
    return [slab.reshape(windows * parts, channels) for slab in slabs]


def shift(value, axis, step, inner=1):
    size = lax.axis_size(axis)
    stops = size // inner
    perm = [(at, (at // inner + step) % stops * inner + at % inner) for at in range(size)]
    return lax.ppermute(value, axis, perm)


def shift_plane(value, row_step, win_step, inner):
    row_size, win_size = lax.axis_size("row"), lax.axis_size("win")
    stops = row_size // inner
    perm = []
    for row in range(row_size):
        for win in range(win_size):
            to_row = (row // inner + row_step) % stops * inner + row % inner
            perm.append((row * win_size + win, to_row * win_size + (win + win_step) % win_size))
    return lax.ppermute(value, ("row", "win"), perm)


def gather_line(own):
    line = [own] + [shift(own, "col", step) for step in range(1, lax.axis_size("col"))]
    return jnp.concatenate(line, axis=0)


def row_cores():
    return 2 if lax.axis_size("row") % 2 == 0 else 1


def gather_cross(block):
    cores = row_cores()
    stops = lax.axis_size("row") // cores
    blocks = []
    for win_step in range(lax.axis_size("win")):
        for row_step in range(stops):
            if row_step + win_step > 0:
                blocks.append(shift_plane(block, row_step, win_step, cores))
    return blocks


def swap_cores(value):
    return lax.ppermute(value, "row", [(at, at ^ 1) for at in range(lax.axis_size("row"))])


def after(value, *earlier):
    return lax.optimization_barrier((value, *earlier))[0]


def stack_kernel(counts, freq, scale, pack, lists_hbm, *refs):
    piece_count, aliased = counts
    pieces = refs[:piece_count]
    out_ref, left_ref, right_ref, ring_ref, lists_ref, sems, list_sem = refs[
        piece_count + aliased :
    ]
    total = out_ref.shape[0]
    copies, _, width = left_ref.shape
    depth = right_ref.shape[1]
    slots, tiles, _, row_count, _ = ring_ref.shape
    chunks = pack // copies

    lists = pltpu.make_async_copy(lists_hbm, lists_ref, list_sem)
    lists.start()

    offset = lax.axis_index("win") * row_count
    pick_at = lax.broadcasted_iota(jnp.int32, (2 * row_count, 2 * BLOCK), 0)
    pick_lane = lax.broadcasted_iota(jnp.int32, (2 * row_count, 2 * BLOCK), 1)
    want = pick_at % row_count + offset + pick_at // row_count * BLOCK
    pick = (pick_lane == want).astype(jnp.bfloat16)
    turn_at = lax.broadcasted_iota(jnp.int32, (depth, depth), 0)
    turn_lane = lax.broadcasted_iota(jnp.int32, (depth, depth), 1)
    turn = jnp.where(
        turn_at % 2 == 1,
        jnp.where(turn_lane == turn_at - 1, -1.0, 0.0),
        jnp.where(turn_lane == turn_at + 1, 1.0, 0.0),
    ).astype(jnp.bfloat16)
    place = lax.broadcasted_iota(jnp.int32, (2 * row_count, width), 1) // depth

    def prepare(at, carry):
        here = pl.multiple_of(at * 2 * BLOCK, 2 * BLOCK)
        rows = jnp.concatenate([ref[:, pl.ds(here, 2 * BLOCK)] for ref in pieces], axis=0)
        turned = jnp.dot(turn, rows, preferred_element_type=jnp.float32).astype(jnp.bfloat16)
        left = lax.dot_general(
            pick,
            jnp.concatenate([rows] * copies, axis=0),
            (((1,), (1,)), ((), ())),
            preferred_element_type=jnp.float32,
        )
        where = pl.multiple_of(at * 2 * row_count, 2 * row_count)
        for copy in range(copies):
            only = left if copies == 1 else jnp.where(place == copy, left, 0.0)
            left_ref[copy, pl.ds(where, 2 * row_count), :] = only.astype(jnp.bfloat16)
        for half in range(2):
            lanes = slice(half * BLOCK, (half + 1) * BLOCK)
            right_ref[at * 2 + half, :, :BLOCK] = rows[:, lanes]
            right_ref[at * 2 + half, :, BLOCK:] = turned[:, lanes]
        return carry

    pairs = pieces[0].shape[1] // (2 * BLOCK)
    lax.fori_loop(0, pairs, prepare, 0, unroll=8 if pairs % 8 == 0 else 1)
    lists.wait()

    def send(step, slot, count=tiles):
        return pltpu.make_async_copy(
            ring_ref.at[slot, pl.ds(0, count)],
            out_ref.at[pl.ds(step * tiles, count), freq],
            sems.at[slot],
        )

    def compute(step, slot, count):
        for group in range(count // pack):
            lefts = []
            rights = []
            for member in range(pack):
                at = step * tiles + group * pack + member
                left_at = pl.multiple_of(lists_ref[at] * row_count, row_count)
                left = left_ref[member % copies, pl.ds(left_at, row_count), :]
                if chunks > 1:
                    chunk = member // copies
                    empty = jnp.zeros_like(left)
                    left = jnp.concatenate(
                        [left if spot == chunk else empty for spot in range(chunks)], axis=1
                    )
                lefts.append(left)
                rights.append(right_ref[lists_ref[total + at]])
            product = jnp.dot(
                jnp.concatenate(lefts, axis=0),
                jnp.concatenate(rights, axis=0),
                preferred_element_type=jnp.float32,
            )
            product = product * scale
            for member in range(pack):
                mine = product[member * row_count : (member + 1) * row_count]
                ring_ref[slot, group * pack + member, 0] = mine[:, :BLOCK]
                ring_ref[slot, group * pack + member, 1] = mine[:, BLOCK:]

    steps = total // tiles
    rest = total % tiles

    def stack(step, carry):
        slot = lax.rem(step, slots)

        @pl.when(step >= slots)
        def _():
            send(step - slots, slot).wait()

        compute(step, slot, tiles)
        send(step, slot).start()
        return carry

    lax.fori_loop(0, steps, stack, 0)
    sent = [(step, tiles) for step in range(max(0, steps - slots), steps)]
    if rest:
        if steps >= slots:
            send(sent[0][0], sent[0][0] % slots).wait()
            sent = sent[1:]
        compute(steps, steps % slots, rest)
        send(steps, steps % slots, rest).start()
        sent.append((steps, rest))
    for step, count in sent:
        send(step, step % slots, count).wait()


def stack_bin(freq, out_shape, lists, pieces, scale, so_far):
    channels = pieces[0].shape[1]
    depth = sum(value.shape[0] for value in pieces)
    tile_total, _, parts, row_count, _ = out_shape.shape
    pack = math.gcd(tile_total, max(1, MXU // depth))
    copies = min(pack, max(1, BLOCK // depth))
    tiles = max(pack, 24 // pack * pack)
    tiles = min(tiles, tile_total)
    blocks = channels // BLOCK
    vmem = pl.BlockSpec(memory_space=pltpu.VMEM)
    in_specs = [pl.BlockSpec(memory_space=pl.ANY)] + [vmem] * len(pieces)
    operands = [lists] + pieces
    aliases = {}
    if so_far is not None:
        in_specs.append(pl.BlockSpec(memory_space=pl.ANY))
        aliases = {len(operands): 0}
        operands.append(so_far)
    slots = 4
    scratch = [
        ((copies, blocks * row_count, copies * depth), jnp.bfloat16),
        ((blocks, depth, 2 * BLOCK), jnp.bfloat16),
        ((slots, tiles, parts, row_count, BLOCK), jnp.float32),
    ]
    used = [(value.shape, value.dtype) for value in pieces] + scratch
    vmem_bytes = sum(math.prod(shape) * jnp.dtype(kind).itemsize for shape, kind in used)
    product = tile_total * row_count * 2 * BLOCK
    return pl.pallas_call(
        functools.partial(stack_kernel, (len(pieces), len(aliases)), freq, scale, pack),
        out_shape=out_shape,
        in_specs=in_specs,
        out_specs=pl.BlockSpec(memory_space=pl.ANY),
        scratch_shapes=[pltpu.VMEM(*spec) for spec in scratch]
        + [pltpu.SMEM(lists.shape, jnp.int32)]
        + [pltpu.SemaphoreType.DMA((slots,)), pltpu.SemaphoreType.DMA],
        input_output_aliases=aliases,
        cost_estimate=pl.CostEstimate(
            flops=2 * product * depth, bytes_accessed=4 * product, transcendentals=0
        ),
        compiler_params=pltpu.CompilerParams(vmem_limit_bytes=vmem_bytes + 8 * 1024 * 1024),
        name="stack",
    )(*operands)


def on_device(spectra, tile_rows, tile_cols):
    window_total = (
        spectra.shape[2] * lax.axis_size("row") * lax.axis_size("col") * lax.axis_size("win")
    )
    scale = float(1.0 / window_total**0.5)
    slabs = whiten(spectra[0])
    row_count = BLOCK // lax.axis_size("win")
    out_shape = jax.ShapeDtypeStruct(
        (tile_rows.shape[0], len(slabs), 2, row_count, BLOCK), jnp.float32
    )
    lists = jnp.concatenate([tile_rows, tile_cols])
    out = None
    gate = None
    for freq, own in enumerate(slabs):
        if gate is not None:
            own = after(own, gate, lists)
        block = gather_line(own)
        swapped = [swap_cores(block)] if row_cores() == 2 else []
        gate = (swapped or [block])[0]
        sent = block if out is None else after(block, *arrived)
        arrived = gather_cross(sent)
        pieces = [block] + arrived
        if swapped:
            ready = arrived if out is None else after(tuple(arrived), out)
            swapped += [swap_cores(value) for value in ready]
        out = stack_bin(freq, out_shape, lists, pieces + swapped, scale, out)
    return out


def solution(mesh):
    in_specs = (P("win", None, ("row", "col"), None, None), P(("row", "col")), P(("row", "col")))
    out_specs = P(("row", "col"), None, None, "win", None)
    return jax.shard_map(
        on_device, mesh=mesh, in_specs=in_specs, out_specs=out_specs, check_vma=False
    )
```

time: 79.9 us -> 68.1 us (0.85)
  Pallas kernels: 36.2 us -> 31.3 us
  starting transfers between devices: 20.9 us -> 16.9 us
  waiting for transfers between devices: 18.1 us -> 16.5 us
  local copies, waits for them, and re-layouts: 1.41 us -> 0 us
    ppermute x14 -> x6, waiting for transfers between devices: 18.1 us -> 6.2 us  [shift(): return lax.ppermute(value, axis, perm)]
    ppermute x14 -> x6, starting transfers between devices: 19.8 us -> 8.13 us  [shift(): return lax.ppermute(value, axis, perm)]
    ppermute x10 -> x14, waiting for transfers between devices: 0.03 us -> 10.3 us  [the longest x6 8.9 us: shift_plane(): return lax.ppermute(value, ('row', 'win'), perm)]
    ppermute x10 -> x14, starting transfers between devices: 1.1 us -> 8.81 us  [the longest x6 7.11 us: shift_plane(): return lax.ppermute(value, ('row', 'win'), perm)]
    pallas_call x2, Pallas kernels: 34 us -> 29.1 us  [stack_bin(): pl.pallas_call(functools.partial(stack_kernel, (len(pieces), len(aliases)...]
    unnamed x4 -> x0, local copies, waits for them, and re-layouts: 1.37 us -> none
  transfers between devices with their start and end apart: 24 -> 20, of which waited for: 11 -> 9; matrix products, arithmetic and copies ran while one was open for 1% -> 3% of each run, Pallas kernels for 22% -> 21%
where the time goes in v2:
time: 68.1 us; the launch traced here: 67.8 us
  Pallas kernels  31.3 us (46%)
  starting transfers between devices  16.9 us (25%)
  waiting for transfers between devices  16.5 us (24%)
  other arithmetic  3.06 us (4%)
    pallas_call x2, Pallas kernels, stack_bin(): pl.pallas_call(functools.partial(stack_kernel, (len(pieces), len(aliases)...  29.1 us
    ppermute x6, waiting for transfers between devices, shift_plane(): return lax.ppermute(value, ('row', 'win'), perm)  8.9 us
    ppermute x6, starting transfers between devices, shift(): return lax.ppermute(value, axis, perm)  8.13 us
    ppermute x6, starting transfers between devices, shift_plane(): return lax.ppermute(value, ('row', 'win'), perm)  7.11 us
    ppermute x6, waiting for transfers between devices, shift(): return lax.ppermute(value, axis, perm)  6.2 us
    concatenate x2, other arithmetic, gather_line(): return jnp.concatenate(line, axis=0)  2.28 us
    pallas_call x1, Pallas kernels, whiten(): pl.pallas_call(whiten_kernel, out_shape=[shape] * freqs, name='whiten')  2.17 us
    ppermute x8, starting transfers between devices, swap_cores(): lax.ppermute(value, 'row', [(at, at ^ 1) for at in range(lax.axis_size('r...  1.7 us
  transfers between devices with their start and end apart: 20, of which 9 were waited for; matrix products, arithmetic and copies ran while one was open for 3% of the time, Pallas kernels for 21%

profile of v2, /device:TPU:0, one launch (start us, length us, event | category | flops | bytes accessed | tf_op | source)
XLA Modules:
  0.0 67.8 jit_solution(16182248546183145824)
XLA Ops:
  0.0 2.2 %whiten.1 = (bf16[1,2,16384]{2,1,0:T(2,128)(2,1)}, bf16[1,2,16384]{2,1,0:T(2,128)(2,1)}) custom-call(f32[2,1,2,16384]{3,2,1,0:T(2,128)} %bitcast.3), custom_call_target="tpu_custom_call" | custom-call | tf_op jit(solution)/shard_map/whiten/pallas_call | solution.py:30
  2.2 5.0 %collective-permute-start.2 = (bf16[2,16384]{1,0:T(2,128)(2,1)}, bf16[2,16384]{1,0:T(2,128)(2,1)S(1)}, u32[]{:S(2)}, u32[]{:S(2)}) collective-permute-start(bf16[2,16384]{1,0:T(2,128)(2,1)} %bitcast.8), channel_id=1, source_target_pairs={{0,6},{2,0},{4,2},{6,4},{1,7},{3,1},{5,3},{7,5},{8,14},{10,8},{12,... | collective-permute-start | bytes 196616 | tf_op jit(solution)/shard_map/ppermute | solution.py:38
  7.2 1.0 %collective-permute-start = (bf16[2,16384]{1,0:T(2,128)(2,1)}, bf16[2,16384]{1,0:T(2,128)(2,1)S(1)}, u32[]{:S(2)}, u32[]{:S(2)}) collective-permute-start(bf16[2,16384]{1,0:T(2,128)(2,1)} %bitcast.10), channel_id=1, source_target_pairs={{0,2},{2,4},{4,6},{6,0},{1,3},{3,5},{5,7},{7,1},{8,10},{10,12},{12... | collective-permute-start | bytes 196616 | tf_op jit(solution)/shard_map/ppermute | solution.py:38
  8.2 1.8 %collective-permute-done.2 = bf16[2,16384]{1,0:T(2,128)(2,1)S(1)} collective-permute-done((bf16[2,16384]{1,0:T(2,128)(2,1)}, bf16[2,16384]{1,0:T(2,128)(2,1)S(1)}, u32[]{:S(2)}, u32[]{:S(2)}) %collective-permute-start.2) | collective-permute-done | bytes 65568 | tf_op jit(solution)/shard_map/ppermute | solution.py:38
  10.0 3.9 %collective-permute-done.1 = bf16[2,16384]{1,0:T(2,128)(2,1)S(1)} collective-permute-done((bf16[2,16384]{1,0:T(2,128)(2,1)}, bf16[2,16384]{1,0:T(2,128)(2,1)S(1)}, u32[]{:S(2)}, u32[]{:S(2)}) %collective-permute-start.1) | collective-permute-done | bytes 65568 | tf_op jit(solution)/shard_map/ppermute | solution.py:38
  13.9 1.1 %pad_maximum_fusion.refs_0_ = bf16[8,16384]{1,0:T(8,128)(2,1)S(1)} fusion(bf16[2,16384]{1,0:T(2,128)(2,1)S(1)} %collective-permute-done.2, bf16[2,16384]{1,0:T(2,128)(2,1)S(1)} %collective-permute-done.1, bf16[2,16384]{1,0:T(2,128)(2,1)S(1)} %collective-permute-done, bf16[2,16384]{1,0:T(2,128)(2,1)} %bitcast.11), kind=kLoop, calls=%fused_computation | loop fusion | flops 1048576 | bytes 524288 | tf_op jit(solution)/shard_map/concatenate | solution.py:54
  15.0 0.1 collective-permute-start.3
  15.1 2.5 %collective-permute-start.9 = (bf16[8,16384]{1,0:T(8,128)(2,1)S(1)}, bf16[8,16384]{1,0:T(8,128)(2,1)S(1)}, u32[]{:S(2)}, u32[]{:S(2)}) collective-permute-start(bf16[8,16384]{1,0:T(8,128)(2,1)S(1)} %pad_maximum_fusion.refs_0_), channel_id=1, source_target_pairs={{0,17},{1,16},{8,25},{9,24},{16,1},{17,0},{24,9},{25,8},{2,19},{3,... | collective-permute-start | bytes 786440 | tf_op jit(solution)/shard_map/ppermute | solution.py:49
  17.6 0.5 collective-permute-start.8
  18.1 0.5 collective-permute-start.7
  18.7 0.8 %pad_add_fusion.lists_hbm = s32[1032]{0:T(1024)S(1)} fusion(s32[516]{0:T(1024)} %param.5, s32[516]{0:T(1024)} %param.4), kind=kLoop, calls=%fused_computation.2 | loop fusion | flops 1032 | bytes 8256 | tf_op jit(solution)/shard_map/concatenate | solution.py:247
  19.5 1.9 %collective-permute-start.6 = (bf16[2,16384]{1,0:T(2,128)(2,1)}, bf16[2,16384]{1,0:T(2,128)(2,1)S(1)}, u32[]{:S(2)}, u32[]{:S(2)}) collective-permute-start(bf16[2,16384]{1,0:T(2,128)(2,1)} %bitcast.4), channel_id=1, source_target_pairs={{0,6},{2,0},{4,2},{6,4},{1,7},{3,1},{5,3},{7,5},{8,14},{10,8},{12,... | collective-permute-start | bytes 196616 | tf_op jit(solution)/shard_map/ppermute | solution.py:38
  21.4 3.9 %collective-permute-done.9.refs_3_ = bf16[8,16384]{1,0:T(8,128)(2,1)S(1)} collective-permute-done((bf16[8,16384]{1,0:T(8,128)(2,1)S(1)}, bf16[8,16384]{1,0:T(8,128)(2,1)S(1)}, u32[]{:S(2)}, u32[]{:S(2)}) %collective-permute-start.9) | collective-permute-done | bytes 262176 | tf_op jit(solution)/shard_map/ppermute | solution.py:49
  25.2 0.2 collective-permute-start.4
  25.4 5.0 %collective-permute-done.8.refs_2_ = bf16[8,16384]{1,0:T(8,128)(2,1)S(1)} collective-permute-done((bf16[8,16384]{1,0:T(8,128)(2,1)S(1)}, bf16[8,16384]{1,0:T(8,128)(2,1)S(1)}, u32[]{:S(2)}, u32[]{:S(2)}) %collective-permute-start.8) | collective-permute-done | bytes 262176 | tf_op jit(solution)/shard_map/ppermute | solution.py:49
  30.4 0.0 collective-permute-start.16
  30.4 0.1 collective-permute-done.7.refs_1_
  30.5 0.4 collective-permute-start.15
  30.9 0.1 collective-permute-start.14
  31.0 0.5 collective-permute-done.4
  31.5 1.1 %pad_maximum_fusion.1.refs_0_ = bf16[8,16384]{1,0:T(8,128)(2,1)S(1)} fusion(bf16[2,16384]{1,0:T(2,128)(2,1)S(1)} %collective-permute-done.6, bf16[2,16384]{1,0:T(2,128)(2,1)S(1)} %collective-permute-done.5, bf16[2,16384]{1,0:T(2,128)(2,1)S(1)} %collective-permute-done.4, bf16[2,16384]{1,0:T(2,128)(2,1)} %bitcast.7), kind=kLoop, calls=%fused_computation.1 | loop fusion | flops 1048576 | bytes 524288 | tf_op jit(solution)/shard_map/concatenate | solution.py:54
  32.7 2.5 %collective-permute-start.12 = (bf16[8,16384]{1,0:T(8,128)(2,1)S(1)}, bf16[8,16384]{1,0:T(8,128)(2,1)S(1)}, u32[]{:S(2)}, u32[]{:S(2)}) collective-permute-start(bf16[8,16384]{1,0:T(8,128)(2,1)S(1)} %pad_maximum_fusion.1.refs_0_), channel_id=1, source_target_pairs={{0,17},{1,16},{8,25},{9,24},{16,1},{17,0},{24,9},{25,8},{2,19},{3,... | collective-permute-start | bytes 786440 | tf_op jit(solution)/shard_map/ppermute | solution.py:49
  35.2 0.5 collective-permute-start.11
  35.7 0.5 collective-permute-start.10
  36.2 14.5 %stack.2.refs_8_ = f32[516,2,2,64,128]{4,3,2,1,0:T(8,128)} custom-call(s32[1032]{0:T(1024)S(1)} %pad_add_fusion.lists_hbm, bf16[8,16384]{1,0:T(8,128)(2,1)S(1)} %pad_maximum_fusion.refs_0_, bf16[8,16384]{1,0:T(8,128)(2,1)S(1)} %collective-permute-done.7.refs_1_, bf16[8,16384]{1,0:T(8,128)(2,1)S(1)} %collective-permute-done.8.refs_2_, ...), custom_call_target="tpu_custom_call" | custom-call | flops 1082130432 | bytes 33816576 | tf_op jit(solution)/shard_map/stack/pallas_call | solution.py:220
  50.8 0.6 collective-permute-start.17
  51.4 0.1 collective-permute-start.18
  51.5 0.4 collective-permute-start.19
  51.9 0.6 collective-permute-done.17.refs_5_
  52.5 0.4 collective-permute-done.18.refs_6_
  52.9 0.4 collective-permute-done.19.refs_7_
  53.3 14.5 %stack.3 = f32[516,2,2,64,128]{4,3,2,1,0:T(8,128)} custom-call(s32[1032]{0:T(1024)S(1)} %pad_add_fusion.lists_hbm, bf16[8,16384]{1,0:T(8,128)(2,1)S(1)} %pad_maximum_fusion.1.refs_0_, bf16[8,16384]{1,0:T(8,128)(2,1)S(1)} %collective-permute-done.10.refs_1_, bf16[8,16384]{1,0:T(8,128)(2,1)S(1)} %collective-permute-done.11.refs_2_, ...), custom_call_target="tpu_custom_call", output_to_operand_aliasing={{}: (9, {})} | custom-call | flops 1082130432 | bytes 33816576 | tf_op jit(solution)/shard_map/stack/pallas_call | solution.py:220
  (14 shorter events, 0.0 us)
Async XLA Ops:
  2.2 7.9 %collective-permute-start.2 = (bf16[2,16384]{1,0:T(2,128)(2,1)}, bf16[2,16384]{1,0:T(2,128)(2,1)S(1)}, u32[]{:S(2)}, u32[]{:S(2)}) collective-permute-start(bf16[2,16384]{1,0:T(2,128)(2,1)} %bitcast.8), channel_id=1, source_target_pairs={{0,6},{2,0},{4,2},{6,4},{1,7},{3,1},{5,3},{7,5},{8,14},{10,8},{12,... | collective-permute-start | bytes 196616 | tf_op jit(solution)/shard_map/ppermute | solution.py:38
  7.2 6.7 %collective-permute-start.1 = (bf16[2,16384]{1,0:T(2,128)(2,1)}, bf16[2,16384]{1,0:T(2,128)(2,1)S(1)}, u32[]{:S(2)}, u32[]{:S(2)}) collective-permute-start(bf16[2,16384]{1,0:T(2,128)(2,1)} %bitcast.9), channel_id=1, source_target_pairs={{0,4},{2,6},{4,0},{6,2},{1,5},{3,7},{5,1},{7,3},{8,12},{10,14},{12... | collective-permute-start | bytes 196616 | tf_op jit(solution)/shard_map/ppermute | solution.py:38
  7.2 6.7 %collective-permute-start = (bf16[2,16384]{1,0:T(2,128)(2,1)}, bf16[2,16384]{1,0:T(2,128)(2,1)S(1)}, u32[]{:S(2)}, u32[]{:S(2)}) collective-permute-start(bf16[2,16384]{1,0:T(2,128)(2,1)} %bitcast.10), channel_id=1, source_target_pairs={{0,2},{2,4},{4,6},{6,0},{1,3},{3,5},{5,7},{7,1},{8,10},{10,12},{12... | collective-permute-start | bytes 196616 | tf_op jit(solution)/shard_map/ppermute | solution.py:38
  15.0 4.4 %collective-permute-start.3 = (bf16[8,16384]{1,0:T(8,128)(2,1)S(1)}, bf16[8,16384]{1,0:T(8,128)(2,1)S(1)}, u32[]{:S(2)}, u32[]{:S(2)}) collective-permute-start(bf16[8,16384]{1,0:T(8,128)(2,1)S(1)} %pad_maximum_fusion.refs_0_), channel_id=1, source_target_pairs={{0,8},{8,0},{16,24},{24,16},{1,9},{9,1},{17,25},{25,17},{2,10},{10... | collective-permute-start | bytes 786440 | tf_op jit(solution)/shard_map/ppermute | solution.py:73
  15.1 10.1 %collective-permute-start.9 = (bf16[8,16384]{1,0:T(8,128)(2,1)S(1)}, bf16[8,16384]{1,0:T(8,128)(2,1)S(1)}, u32[]{:S(2)}, u32[]{:S(2)}) collective-permute-start(bf16[8,16384]{1,0:T(8,128)(2,1)S(1)} %pad_maximum_fusion.refs_0_), channel_id=1, source_target_pairs={{0,17},{1,16},{8,25},{9,24},{16,1},{17,0},{24,9},{25,8},{2,19},{3,... | collective-permute-start | bytes 786440 | tf_op jit(solution)/shard_map/ppermute | solution.py:49
  17.6 12.7 %collective-permute-start.8 = (bf16[8,16384]{1,0:T(8,128)(2,1)S(1)}, bf16[8,16384]{1,0:T(8,128)(2,1)S(1)}, u32[]{:S(2)}, u32[]{:S(2)}) collective-permute-start(bf16[8,16384]{1,0:T(8,128)(2,1)S(1)} %pad_maximum_fusion.refs_0_), channel_id=1, source_target_pairs={{0,1},{1,0},{8,9},{9,8},{16,17},{17,16},{24,25},{25,24},{2,3},{3,2... | collective-permute-start | bytes 786440 | tf_op jit(solution)/shard_map/ppermute | solution.py:49
  18.1 12.3 %collective-permute-start.7 = (bf16[8,16384]{1,0:T(8,128)(2,1)S(1)}, bf16[8,16384]{1,0:T(8,128)(2,1)S(1)}, u32[]{:S(2)}, u32[]{:S(2)}) collective-permute-start(bf16[8,16384]{1,0:T(8,128)(2,1)S(1)} %pad_maximum_fusion.refs_0_), channel_id=1, source_target_pairs={{0,16},{1,17},{8,24},{9,25},{16,0},{17,1},{24,8},{25,9},{2,18},{3,... | collective-permute-start | bytes 786440 | tf_op jit(solution)/shard_map/ppermute | solution.py:49
  19.5 11.4 %collective-permute-start.6 = (bf16[2,16384]{1,0:T(2,128)(2,1)}, bf16[2,16384]{1,0:T(2,128)(2,1)S(1)}, u32[]{:S(2)}, u32[]{:S(2)}) collective-permute-start(bf16[2,16384]{1,0:T(2,128)(2,1)} %bitcast.4), channel_id=1, source_target_pairs={{0,6},{2,0},{4,2},{6,4},{1,7},{3,1},{5,3},{7,5},{8,14},{10,8},{12,... | collective-permute-start | bytes 196616 | tf_op jit(solution)/shard_map/ppermute | solution.py:38
  21.4 9.6 %collective-permute-start.5 = (bf16[2,16384]{1,0:T(2,128)(2,1)}, bf16[2,16384]{1,0:T(2,128)(2,1)S(1)}, u32[]{:S(2)}, u32[]{:S(2)}) collective-permute-start(bf16[2,16384]{1,0:T(2,128)(2,1)} %bitcast.5), channel_id=1, source_target_pairs={{0,4},{2,6},{4,0},{6,2},{1,5},{3,7},{5,1},{7,3},{8,12},{10,14},{12... | collective-permute-start | bytes 196616 | tf_op jit(solution)/shard_map/ppermute | solution.py:38
  25.2 6.3 %collective-permute-start.4 = (bf16[2,16384]{1,0:T(2,128)(2,1)}, bf16[2,16384]{1,0:T(2,128)(2,1)S(1)}, u32[]{:S(2)}, u32[]{:S(2)}) collective-permute-start(bf16[2,16384]{1,0:T(2,128)(2,1)} %bitcast.6), channel_id=1, source_target_pairs={{0,2},{2,4},{4,6},{6,0},{1,3},{3,5},{5,7},{7,1},{8,10},{10,12},{12... | collective-permute-start | bytes 196616 | tf_op jit(solution)/shard_map/ppermute | solution.py:38
  30.4 5.3 %collective-permute-start.16 = (bf16[8,16384]{1,0:T(8,128)(2,1)S(1)}, bf16[8,16384]{1,0:T(8,128)(2,1)S(1)}, u32[]{:S(2)}, u32[]{:S(2)}) collective-permute-start(bf16[8,16384]{1,0:T(8,128)(2,1)S(1)} %collective-permute-done.9.refs_3_), channel_id=1, source_target_pairs={{0,8},{8,0},{16,24},{24,16},{1,9},{9,1},{17,25},{25,17},{2,10},{10... | collective-permute-start | bytes 786440 | tf_op jit(solution)/shard_map/ppermute | solution.py:73
  30.5 5.8 %collective-permute-start.15 = (bf16[8,16384]{1,0:T(8,128)(2,1)S(1)}, bf16[8,16384]{1,0:T(8,128)(2,1)S(1)}, u32[]{:S(2)}, u32[]{:S(2)}) collective-permute-start(bf16[8,16384]{1,0:T(8,128)(2,1)S(1)} %collective-permute-done.8.refs_2_), channel_id=1, source_target_pairs={{0,8},{8,0},{16,24},{24,16},{1,9},{9,1},{17,25},{25,17},{2,10},{10... | collective-permute-start | bytes 786440 | tf_op jit(solution)/shard_map/ppermute | solution.py:73
  30.9 5.3 %collective-permute-start.14 = (bf16[8,16384]{1,0:T(8,128)(2,1)S(1)}, bf16[8,16384]{1,0:T(8,128)(2,1)S(1)}, u32[]{:S(2)}, u32[]{:S(2)}) collective-permute-start(bf16[8,16384]{1,0:T(8,128)(2,1)S(1)} %collective-permute-done.7.refs_1_), channel_id=1, source_target_pairs={{0,8},{8,0},{16,24},{24,16},{1,9},{9,1},{17,25},{25,17},{2,10},{10... | collective-permute-start | bytes 786440 | tf_op jit(solution)/shard_map/ppermute | solution.py:73
  32.7 18.1 %collective-permute-start.12 = (bf16[8,16384]{1,0:T(8,128)(2,1)S(1)}, bf16[8,16384]{1,0:T(8,128)(2,1)S(1)}, u32[]{:S(2)}, u32[]{:S(2)}) collective-permute-start(bf16[8,16384]{1,0:T(8,128)(2,1)S(1)} %pad_maximum_fusion.1.refs_0_), channel_id=1, source_target_pairs={{0,17},{1,16},{8,25},{9,24},{16,1},{17,0},{24,9},{25,8},{2,19},{3,... | collective-permute-start | bytes 786440 | tf_op jit(solution)/shard_map/ppermute | solution.py:49
  35.2 15.6 %collective-permute-start.11 = (bf16[8,16384]{1,0:T(8,128)(2,1)S(1)}, bf16[8,16384]{1,0:T(8,128)(2,1)S(1)}, u32[]{:S(2)}, u32[]{:S(2)}) collective-permute-start(bf16[8,16384]{1,0:T(8,128)(2,1)S(1)} %pad_maximum_fusion.1.refs_0_), channel_id=1, source_target_pairs={{0,1},{1,0},{8,9},{9,8},{16,17},{17,16},{24,25},{25,24},{2,3},{3,2... | collective-permute-start | bytes 786440 | tf_op jit(solution)/shard_map/ppermute | solution.py:49
  35.7 15.1 %collective-permute-start.10 = (bf16[8,16384]{1,0:T(8,128)(2,1)S(1)}, bf16[8,16384]{1,0:T(8,128)(2,1)S(1)}, u32[]{:S(2)}, u32[]{:S(2)}) collective-permute-start(bf16[8,16384]{1,0:T(8,128)(2,1)S(1)} %pad_maximum_fusion.1.refs_0_), channel_id=1, source_target_pairs={{0,16},{1,17},{8,24},{9,25},{16,0},{17,1},{24,8},{25,9},{2,18},{3,... | collective-permute-start | bytes 786440 | tf_op jit(solution)/shard_map/ppermute | solution.py:49
  36.2 15.7 %collective-permute-start.13 = (bf16[8,16384]{1,0:T(8,128)(2,1)S(1)}, bf16[8,16384]{1,0:T(8,128)(2,1)S(1)}, u32[]{:S(2)}, u32[]{:S(2)}) collective-permute-start(bf16[8,16384]{1,0:T(8,128)(2,1)S(1)} %pad_maximum_fusion.1.refs_0_), channel_id=1, source_target_pairs={{0,8},{8,0},{16,24},{24,16},{1,9},{9,1},{17,25},{25,17},{2,10},{10... | collective-permute-start | bytes 786440 | tf_op jit(solution)/shard_map/ppermute | solution.py:73
  50.8 1.7 %collective-permute-start.17 = (bf16[8,16384]{1,0:T(8,128)(2,1)S(1)}, bf16[8,16384]{1,0:T(8,128)(2,1)S(1)}, u32[]{:S(2)}, u32[]{:S(2)}) collective-permute-start(bf16[8,16384]{1,0:T(8,128)(2,1)S(1)} %collective-permute-done.10.refs_1_), channel_id=1, source_target_pairs={{0,8},{8,0},{16,24},{24,16},{1,9},{9,1},{17,25},{25,17},{2,10},{10... | collective-permute-start | bytes 786440 | tf_op jit(solution)/shard_map/ppermute | solution.py:73
  51.4 1.5 %collective-permute-start.18 = (bf16[8,16384]{1,0:T(8,128)(2,1)S(1)}, bf16[8,16384]{1,0:T(8,128)(2,1)S(1)}, u32[]{:S(2)}, u32[]{:S(2)}) collective-permute-start(bf16[8,16384]{1,0:T(8,128)(2,1)S(1)} %collective-permute-done.11.refs_2_), channel_id=1, source_target_pairs={{0,8},{8,0},{16,24},{24,16},{1,9},{9,1},{17,25},{25,17},{2,10},{10... | collective-permute-start | bytes 786440 | tf_op jit(solution)/shard_map/ppermute | solution.py:73
  51.5 1.8 %collective-permute-start.19 = (bf16[8,16384]{1,0:T(8,128)(2,1)S(1)}, bf16[8,16384]{1,0:T(8,128)(2,1)S(1)}, u32[]{:S(2)}, u32[]{:S(2)}) collective-permute-start(bf16[8,16384]{1,0:T(8,128)(2,1)S(1)} %collective-permute-done.12.refs_3_), channel_id=1, source_target_pairs={{0,8},{8,0},{16,24},{24,16},{1,9},{9,1},{17,25},{25,17},{2,10},{10... | collective-permute-start | bytes 786440 | tf_op jit(solution)/shard_map/ppermute | solution.py:73

commit v3 on v2

--- a/solution.py
+++ b/solution.py
@@ -19,9 +19,9 @@
         slab = spectra_ref[freq]
         term = jnp.sum(slab * slab, axis=1, keepdims=True)
         power = term if power is None else power + term
-    floor = jnp.maximum(jnp.sqrt(power / freqs), 1.0)
+    factor = jnp.minimum(lax.rsqrt(power / freqs), 1.0)
     for freq in range(freqs):
-        out_refs[freq][...] = (spectra_ref[freq] / floor).astype(jnp.bfloat16)
+        out_refs[freq][...] = (spectra_ref[freq] * factor).astype(jnp.bfloat16)
 
 
 def whiten(spectra):
@@ -58,15 +58,31 @@
     return 2 if lax.axis_size("row") % 2 == 0 else 1
 
 
-def gather_cross(block):
+def gather_direct(block, earlier):
     cores = row_cores()
-    stops = lax.axis_size("row") // cores
+    sent = after(block, *earlier)
     blocks = []
     for win_step in range(lax.axis_size("win")):
-        for row_step in range(stops):
+        for row_step in range(lax.axis_size("row") // cores):
             if row_step + win_step > 0:
-                blocks.append(shift_plane(block, row_step, win_step, cores))
+                blocks.append(shift_plane(sent, row_step, win_step, cores))
     return blocks
+
+
+def gather_relayed(block):
+    cores = row_cores()
+    half = block.shape[1] // 2
+    along_row = [
+        shift(block, "row", step, cores) for step in range(1, lax.axis_size("row") // cores)
+    ]
+    along_win = [shift(block, "win", step) for step in range(1, lax.axis_size("win"))]
+    lows = []
+    highs = []
+    for row_step, from_row in enumerate(along_row, 1):
+        for win_step, from_win in enumerate(along_win, 1):
+            lows.append(shift(from_win[:, :half], "row", row_step, cores))
+            highs.append(shift(from_row[:, half:], "win", win_step))
+    return along_row + along_win, lows, highs
 
 
 def swap_cores(value):
@@ -78,8 +94,11 @@
 
 
 def stack_kernel(counts, freq, scale, pack, lists_hbm, *refs):
-    piece_count, aliased = counts
-    pieces = refs[:piece_count]
+    whole_count, half_count, aliased = counts
+    whole = refs[:whole_count]
+    lows = refs[whole_count : whole_count + half_count]
+    piece_count = whole_count + 2 * half_count
+    highs = refs[whole_count + half_count : piece_count]
     out_ref, left_ref, right_ref, ring_ref, lists_ref, sems, list_sem = refs[
         piece_count + aliased :
     ]
@@ -106,9 +125,12 @@
     ).astype(jnp.bfloat16)
     place = lax.broadcasted_iota(jnp.int32, (2 * row_count, width), 1) // depth
 
-    def prepare(at, carry):
-        here = pl.multiple_of(at * 2 * BLOCK, 2 * BLOCK)
-        rows = jnp.concatenate([ref[:, pl.ds(here, 2 * BLOCK)] for ref in pieces], axis=0)
+    def prepare(first, halves, at, carry):
+        near = pl.ds(pl.multiple_of(at * 2 * BLOCK, 2 * BLOCK), 2 * BLOCK)
+        at = at + first
+        here = pl.ds(pl.multiple_of(at * 2 * BLOCK, 2 * BLOCK), 2 * BLOCK)
+        pieces = [ref[:, here] for ref in whole] + [ref[:, near] for ref in halves]
+        rows = jnp.concatenate(pieces, axis=0)
         turned = jnp.dot(turn, rows, preferred_element_type=jnp.float32).astype(jnp.bfloat16)
         left = lax.dot_general(
             pick,
@@ -126,8 +148,12 @@
             right_ref[at * 2 + half, :, BLOCK:] = turned[:, lanes]
         return carry
 
-    pairs = pieces[0].shape[1] // (2 * BLOCK)
-    lax.fori_loop(0, pairs, prepare, 0, unroll=8 if pairs % 8 == 0 else 1)
+    pairs = whole[0].shape[1] // (2 * BLOCK)
+    runs = [(0, lows), (pairs // 2, highs)] if half_count else [(0, [])]
+    for first, halves in runs:
+        count = pairs // len(runs)
+        body = functools.partial(prepare, first, halves)
+        lax.fori_loop(0, count, body, 0, unroll=8 if count % 8 == 0 else 1)
     lists.wait()
 
     def send(step, slot, count=tiles):
@@ -191,13 +217,14 @@
         send(step, step % slots, count).wait()
 
 
-def stack_bin(freq, out_shape, lists, pieces, scale, so_far):
-    channels = pieces[0].shape[1]
-    depth = sum(value.shape[0] for value in pieces)
+def stack_bin(freq, out_shape, lists, whole, lows, highs, scale, so_far):
+    pieces = whole + lows + highs
+    channels = whole[0].shape[1]
+    depth = sum(value.shape[0] for value in whole + lows)
     tile_total, _, parts, row_count, _ = out_shape.shape
     pack = math.gcd(tile_total, max(1, MXU // depth))
     copies = min(pack, max(1, BLOCK // depth))
-    tiles = max(pack, 24 // pack * pack)
+    tiles = max(pack, 48 // pack * pack)
     tiles = min(tiles, tile_total)
     blocks = channels // BLOCK
     vmem = pl.BlockSpec(memory_space=pltpu.VMEM)
@@ -208,7 +235,7 @@
         in_specs.append(pl.BlockSpec(memory_space=pl.ANY))
         aliases = {len(operands): 0}
         operands.append(so_far)
-    slots = 4
+    slots = 3
     scratch = [
         ((copies, blocks * row_count, copies * depth), jnp.bfloat16),
         ((blocks, depth, 2 * BLOCK), jnp.bfloat16),
@@ -218,7 +245,7 @@
     vmem_bytes = sum(math.prod(shape) * jnp.dtype(kind).itemsize for shape, kind in used)
     product = tile_total * row_count * 2 * BLOCK
     return pl.pallas_call(
-        functools.partial(stack_kernel, (len(pieces), len(aliases)), freq, scale, pack),
+        functools.partial(stack_kernel, (len(whole), len(lows), len(aliases)), freq, scale, pack),
         out_shape=out_shape,
         in_specs=in_specs,
         out_specs=pl.BlockSpec(memory_space=pl.ANY),
@@ -245,21 +272,28 @@
         (tile_rows.shape[0], len(slabs), 2, row_count, BLOCK), jnp.float32
     )
     lists = jnp.concatenate([tile_rows, tile_cols])
+    swap = swap_cores if row_cores() == 2 else None
     out = None
-    gate = None
     for freq, own in enumerate(slabs):
-        if gate is not None:
+        if freq > 0:
             own = after(own, gate, lists)
         block = gather_line(own)
-        swapped = [swap_cores(block)] if row_cores() == 2 else []
-        gate = (swapped or [block])[0]
-        sent = block if out is None else after(block, *arrived)
-        arrived = gather_cross(sent)
-        pieces = [block] + arrived
-        if swapped:
+        whole = [block]
+        if swap:
+            whole.append(swap(block))
+        gate = whole[-1]
+        if freq == 0:
+            arrived, lows, highs = gather_relayed(block)
+            last = lows + highs if lows else arrived
+        else:
+            arrived, lows, highs = gather_direct(block, last), [], []
+            last = arrived
+        if swap:
             ready = arrived if out is None else after(tuple(arrived), out)
-            swapped += [swap_cores(value) for value in ready]
-        out = stack_bin(freq, out_shape, lists, pieces + swapped, scale, out)
+            whole += [swap(value) for value in ready]
+            lows = lows + [swap(value) for value in lows]
+            highs = highs + [swap(value) for value in highs]
+        out = stack_bin(freq, out_shape, lists, whole + arrived, lows, highs, scale, out)
     return out
 
 

time: 68.1 us -> 67.8 us (level)
  waiting for transfers between devices: 16.5 us -> 11.4 us
  starting transfers between devices: 16.9 us -> 21.2 us
    ppermute x6 -> x3, waiting for transfers between devices: 8.9 us -> 0.01 us  [shift_plane(): return lax.ppermute(value, ('row', 'win'), perm)]
    ppermute x6 -> x10, starting transfers between devices: 8.13 us -> 16.1 us  [shift(): return lax.ppermute(value, axis, perm)]
    ppermute x6 -> x3, starting transfers between devices: 7.11 us -> 3.49 us  [shift_plane(): return lax.ppermute(value, ('row', 'win'), perm)]
    ppermute x6 -> x10, waiting for transfers between devices: 6.2 us -> 9.05 us  [shift(): return lax.ppermute(value, axis, perm)]
    ppermute x8 -> x9, waiting for transfers between devices: 1.41 us -> 2.34 us  [swap_cores(): lax.ppermute(value, 'row', [(at, at ^ 1) for at in range(lax.axis_size('r...]
    ppermute x8 -> x9, starting transfers between devices: 1.7 us -> 1.62 us  [swap_cores(): lax.ppermute(value, 'row', [(at, at ^ 1) for at in range(lax.axis_size('r...]
  transfers between devices with their start and end apart: 20 -> 22, of which waited for: 9 -> 9; matrix products, arithmetic and copies ran while one was open for 3% -> 3% of each run, Pallas kernels for 21% -> 22%
where the time goes in v3:
time: 67.8 us; the launch traced here: 67.5 us
  Pallas kernels  31.8 us (47%)
  starting transfers between devices  21.2 us (31%)
  waiting for transfers between devices  11.4 us (17%)
  other arithmetic  3.06 us (5%)
    pallas_call x2, Pallas kernels, stack_bin(): pl.pallas_call(functools.partial(stack_kernel, (len(whole), len(lows), le...  29.7 us
    ppermute x10, starting transfers between devices, shift(): return lax.ppermute(value, axis, perm)  16.1 us
    ppermute x10, waiting for transfers between devices, shift(): return lax.ppermute(value, axis, perm)  9.05 us
    ppermute x3, starting transfers between devices, shift_plane(): return lax.ppermute(value, ('row', 'win'), perm)  3.49 us
    ppermute x9, waiting for transfers between devices, swap_cores(): lax.ppermute(value, 'row', [(at, at ^ 1) for at in range(lax.axis_size('r...  2.34 us
    concatenate x2, other arithmetic, gather_line(): return jnp.concatenate(line, axis=0)  2.28 us
    pallas_call x1, Pallas kernels, whiten(): pl.pallas_call(whiten_kernel, out_shape=[shape] * freqs, name='whiten')  2.06 us
    ppermute x9, starting transfers between devices, swap_cores(): lax.ppermute(value, 'row', [(at, at ^ 1) for at in range(lax.axis_size('r...  1.62 us
  transfers between devices with their start and end apart: 22, of which 9 were waited for; matrix products, arithmetic and copies ran while one was open for 3% of the time, Pallas kernels for 22%

profile of v3, /device:TPU:0, one launch (start us, length us, event | category | flops | bytes accessed | tf_op | source)
XLA Modules:
  0.0 67.5 jit_solution(3709875297224441211)
XLA Ops:
  0.0 2.1 %whiten.1 = (bf16[1,2,16384]{2,1,0:T(2,128)(2,1)}, bf16[1,2,16384]{2,1,0:T(2,128)(2,1)}) custom-call(f32[2,1,2,16384]{3,2,1,0:T(2,128)} %bitcast.3), custom_call_target="tpu_custom_call" | custom-call | tf_op jit(solution)/shard_map/whiten/pallas_call | solution.py:30
  2.1 5.0 %collective-permute-start.2 = (bf16[2,16384]{1,0:T(2,128)(2,1)}, bf16[2,16384]{1,0:T(2,128)(2,1)S(1)}, u32[]{:S(2)}, u32[]{:S(2)}) collective-permute-start(bf16[2,16384]{1,0:T(2,128)(2,1)} %bitcast.8), channel_id=1, source_target_pairs={{0,6},{2,0},{4,2},{6,4},{1,7},{3,1},{5,3},{7,5},{8,14},{10,8},{12,... | collective-permute-start | bytes 196616 | tf_op jit(solution)/shard_map/ppermute | solution.py:38
  7.1 1.0 %collective-permute-start = (bf16[2,16384]{1,0:T(2,128)(2,1)}, bf16[2,16384]{1,0:T(2,128)(2,1)S(1)}, u32[]{:S(2)}, u32[]{:S(2)}) collective-permute-start(bf16[2,16384]{1,0:T(2,128)(2,1)} %bitcast.10), channel_id=1, source_target_pairs={{0,2},{2,4},{4,6},{6,0},{1,3},{3,5},{5,7},{7,1},{8,10},{10,12},{12... | collective-permute-start | bytes 196616 | tf_op jit(solution)/shard_map/ppermute | solution.py:38
  8.1 1.8 %collective-permute-done.2 = bf16[2,16384]{1,0:T(2,128)(2,1)S(1)} collective-permute-done((bf16[2,16384]{1,0:T(2,128)(2,1)}, bf16[2,16384]{1,0:T(2,128)(2,1)S(1)}, u32[]{:S(2)}, u32[]{:S(2)}) %collective-permute-start.2) | collective-permute-done | bytes 65568 | tf_op jit(solution)/shard_map/ppermute | solution.py:38
  9.9 3.9 %collective-permute-done.1 = bf16[2,16384]{1,0:T(2,128)(2,1)S(1)} collective-permute-done((bf16[2,16384]{1,0:T(2,128)(2,1)}, bf16[2,16384]{1,0:T(2,128)(2,1)S(1)}, u32[]{:S(2)}, u32[]{:S(2)}) %collective-permute-start.1) | collective-permute-done | bytes 65568 | tf_op jit(solution)/shard_map/ppermute | solution.py:38
  13.8 1.1 %pad_maximum_fusion.refs_0_ = bf16[8,16384]{1,0:T(8,128)(2,1)S(1)} fusion(bf16[2,16384]{1,0:T(2,128)(2,1)S(1)} %collective-permute-done.2, bf16[2,16384]{1,0:T(2,128)(2,1)S(1)} %collective-permute-done.1, bf16[2,16384]{1,0:T(2,128)(2,1)S(1)} %collective-permute-done, bf16[2,16384]{1,0:T(2,128)(2,1)} %bitcast.11), kind=kLoop, calls=%fused_computation | loop fusion | flops 1048576 | bytes 524288 | tf_op jit(solution)/shard_map/concatenate | solution.py:54
  14.9 0.1 collective-permute-start.3
  15.0 1.6 %collective-permute-start.10 = (bf16[8,16384]{1,0:T(8,128)(2,1)S(1)}, bf16[8,16384]{1,0:T(8,128)(2,1)S(1)}, u32[]{:S(2)}, u32[]{:S(2)}) collective-permute-start(bf16[8,16384]{1,0:T(8,128)(2,1)S(1)} %pad_maximum_fusion.refs_0_), channel_id=1, source_target_pairs={{0,16},{8,24},{16,0},{24,8},{1,17},{9,25},{17,1},{25,9},{2,18},{10... | collective-permute-start | bytes 786440 | tf_op jit(solution)/shard_map/ppermute | solution.py:38
  16.6 1.5 %collective-permute-start.8 = (bf16[8,16384]{1,0:T(8,128)(2,1)S(1)}, bf16[8,16384]{1,0:T(8,128)(2,1)S(1)}, u32[]{:S(2)}, u32[]{:S(2)}) collective-permute-start(bf16[8,16384]{1,0:T(8,128)(2,1)S(1)} %pad_maximum_fusion.refs_0_), channel_id=1, source_target_pairs={{0,1},{1,0},{2,3},{3,2},{4,5},{5,4},{6,7},{7,6},{8,9},{9,8},{10,11... | collective-permute-start | bytes 786440 | tf_op jit(solution)/shard_map/ppermute | solution.py:38
  18.1 0.8 %pad_add_fusion.lists_hbm = s32[1032]{0:T(1024)S(1)} fusion(s32[516]{0:T(1024)} %param.5, s32[516]{0:T(1024)} %param.4), kind=kLoop, calls=%fused_computation.2 | loop fusion | flops 1032 | bytes 8256 | tf_op jit(solution)/shard_map/concatenate | solution.py:274
  18.9 1.9 %collective-permute-start.6 = (bf16[2,16384]{1,0:T(2,128)(2,1)}, bf16[2,16384]{1,0:T(2,128)(2,1)S(1)}, u32[]{:S(2)}, u32[]{:S(2)}) collective-permute-start(bf16[2,16384]{1,0:T(2,128)(2,1)} %bitcast.4), channel_id=1, source_target_pairs={{0,6},{2,0},{4,2},{6,4},{1,7},{3,1},{5,3},{7,5},{8,14},{10,8},{12,... | collective-permute-start | bytes 196616 | tf_op jit(solution)/shard_map/ppermute | solution.py:38
  20.8 1.9 %collective-permute-start.4 = (bf16[2,16384]{1,0:T(2,128)(2,1)}, bf16[2,16384]{1,0:T(2,128)(2,1)S(1)}, u32[]{:S(2)}, u32[]{:S(2)}) collective-permute-start(bf16[2,16384]{1,0:T(2,128)(2,1)} %bitcast.6), channel_id=1, source_target_pairs={{0,2},{2,4},{4,6},{6,0},{1,3},{3,5},{5,7},{7,1},{8,10},{10,12},{12... | collective-permute-start | bytes 196616 | tf_op jit(solution)/shard_map/ppermute | solution.py:38
  22.7 1.1 %collective-permute-done.10.refs_4_ = bf16[8,16384]{1,0:T(8,128)(2,1)S(1)} collective-permute-done((bf16[8,16384]{1,0:T(8,128)(2,1)S(1)}, bf16[8,16384]{1,0:T(8,128)(2,1)S(1)}, u32[]{:S(2)}, u32[]{:S(2)}) %collective-permute-start.10) | collective-permute-done | bytes 262176 | tf_op jit(solution)/shard_map/ppermute | solution.py:38
  23.8 1.6 %collective-permute-start.11 = (bf16[8,8192]{1,0:T(8,128)(2,1)S(1)}, bf16[8,8192]{1,0:T(8,128)(2,1)S(1)}, u32[]{:S(2)}, u32[]{:S(2)}) collective-permute-start(bf16[8,8192]{1,0:T(8,128)(2,1)S(1)} %slice.9), channel_id=1, source_target_pairs={{0,1},{1,0},{2,3},{3,2},{4,5},{5,4},{6,7},{7,6},{8,9},{9,8},{10,11... | collective-permute-start | bytes 393224 | tf_op jit(solution)/shard_map/ppermute | solution.py:38
  25.4 1.6 %collective-permute-start.9 = (bf16[8,8192]{1,0:T(8,128)(2,1)S(1)}, bf16[8,8192]{1,0:T(8,128)(2,1)S(1)}, u32[]{:S(2)}, u32[]{:S(2)}) collective-permute-start(bf16[8,8192]{1,0:T(8,128)(2,1)S(1)} %slice.8), channel_id=1, source_target_pairs={{0,16},{8,24},{16,0},{24,8},{1,17},{9,25},{17,1},{25,9},{2,18},{10... | collective-permute-start | bytes 393224 | tf_op jit(solution)/shard_map/ppermute | solution.py:38
  26.9 1.1 %collective-permute-done.5 = bf16[2,16384]{1,0:T(2,128)(2,1)S(1)} collective-permute-done((bf16[2,16384]{1,0:T(2,128)(2,1)}, bf16[2,16384]{1,0:T(2,128)(2,1)S(1)}, u32[]{:S(2)}, u32[]{:S(2)}) %collective-permute-start.5) | collective-permute-done | bytes 65568 | tf_op jit(solution)/shard_map/ppermute | solution.py:38
  28.0 1.1 %pad_maximum_fusion.1.refs_0_ = bf16[8,16384]{1,0:T(8,128)(2,1)S(1)} fusion(bf16[2,16384]{1,0:T(2,128)(2,1)S(1)} %collective-permute-done.6, bf16[2,16384]{1,0:T(2,128)(2,1)S(1)} %collective-permute-done.5, bf16[2,16384]{1,0:T(2,128)(2,1)S(1)} %collective-permute-done.4, bf16[2,16384]{1,0:T(2,128)(2,1)} %bitcast.7), kind=kLoop, calls=%fused_computation.1 | loop fusion | flops 1048576 | bytes 524288 | tf_op jit(solution)/shard_map/concatenate | solution.py:54
  29.1 1.3 %collective-permute-done.9.refs_6_ = bf16[8,8192]{1,0:T(8,128)(2,1)S(1)} collective-permute-done((bf16[8,8192]{1,0:T(8,128)(2,1)S(1)}, bf16[8,8192]{1,0:T(8,128)(2,1)S(1)}, u32[]{:S(2)}, u32[]{:S(2)}) %collective-permute-start.9) | collective-permute-done | bytes 131104 | tf_op jit(solution)/shard_map/ppermute | solution.py:38
  30.4 1.4 %collective-permute-start.14 = (bf16[8,16384]{1,0:T(8,128)(2,1)S(1)}, bf16[8,16384]{1,0:T(8,128)(2,1)S(1)}, u32[]{:S(2)}, u32[]{:S(2)}) collective-permute-start(bf16[8,16384]{1,0:T(8,128)(2,1)S(1)} %pad_maximum_fusion.1.refs_0_), channel_id=1, source_target_pairs={{0,17},{1,16},{8,25},{9,24},{16,1},{17,0},{24,9},{25,8},{2,19},{3,... | collective-permute-start | bytes 786440 | tf_op jit(solution)/shard_map/ppermute | solution.py:49
  31.8 1.5 %collective-permute-start.13 = (bf16[8,16384]{1,0:T(8,128)(2,1)S(1)}, bf16[8,16384]{1,0:T(8,128)(2,1)S(1)}, u32[]{:S(2)}, u32[]{:S(2)}) collective-permute-start(bf16[8,16384]{1,0:T(8,128)(2,1)S(1)} %pad_maximum_fusion.1.refs_0_), channel_id=1, source_target_pairs={{0,1},{1,0},{8,9},{9,8},{16,17},{17,16},{24,25},{25,24},{2,3},{3,2... | collective-permute-start | bytes 786440 | tf_op jit(solution)/shard_map/ppermute | solution.py:49
  33.3 0.5 collective-permute-start.12
  33.9 0.5 collective-permute-start.17
  34.4 0.8 %collective-permute-done.18.refs_9_ = bf16[8,8192]{1,0:T(8,128)(2,1)S(1)} collective-permute-done((bf16[8,8192]{1,0:T(8,128)(2,1)S(1)}, bf16[8,8192]{1,0:T(8,128)(2,1)S(1)}, u32[]{:S(2)}, u32[]{:S(2)}) %collective-permute-start.18) | collective-permute-done | bytes 131104 | tf_op jit(solution)/shard_map/ppermute | solution.py:89
  35.2 0.1 collective-permute-start.7
  35.4 14.9 %stack.2.refs_8_ = f32[516,2,2,64,128]{4,3,2,1,0:T(8,128)} custom-call(s32[1032]{0:T(1024)S(1)} %pad_add_fusion.lists_hbm, bf16[8,16384]{1,0:T(8,128)(2,1)S(1)} %pad_maximum_fusion.refs_0_, bf16[8,16384]{1,0:T(8,128)(2,1)S(1)} %collective-permute-done.3.refs_1_, bf16[8,16384]{1,0:T(8,128)(2,1)S(1)} %collective-permute-done.15.refs_2_, ...), custom_call_target="tpu_custom_call" | custom-call | flops 1082130432 | bytes 33816576 | tf_op jit(solution)/shard_map/stack/pallas_call | solution.py:247
  50.3 0.4 collective-permute-start.19
  50.7 0.2 collective-permute-start.20
  50.9 0.3 collective-permute-start.21
  51.2 0.7 %collective-permute-done.19.refs_2_ = bf16[8,16384]{1,0:T(8,128)(2,1)S(1)} collective-permute-done((bf16[8,16384]{1,0:T(8,128)(2,1)S(1)}, bf16[8,16384]{1,0:T(8,128)(2,1)S(1)}, u32[]{:S(2)}, u32[]{:S(2)}) %collective-permute-start.19) | collective-permute-done | bytes 262176 | tf_op jit(solution)/shard_map/ppermute | solution.py:89
  51.9 0.4 collective-permute-done.20.refs_3_
  52.3 0.4 collective-permute-done.21.refs_4_
  52.7 14.8 %stack.3 = f32[516,2,2,64,128]{4,3,2,1,0:T(8,128)} custom-call(s32[1032]{0:T(1024)S(1)} %pad_add_fusion.lists_hbm, bf16[8,16384]{1,0:T(8,128)(2,1)S(1)} %pad_maximum_fusion.1.refs_0_, bf16[8,16384]{1,0:T(8,128)(2,1)S(1)} %collective-permute-done.7.refs_1_, bf16[8,16384]{1,0:T(8,128)(2,1)S(1)} %collective-permute-done.19.refs_2_, ...), custom_call_target="tpu_custom_call", output_to_operand_aliasing={{}: (9, {})} | custom-call | flops 1082130432 | bytes 33816576 | tf_op jit(solution)/shard_map/stack/pallas_call | solution.py:247
  (20 shorter events, 0.1 us)
Async XLA Ops:
  2.1 7.9 %collective-permute-start.2 = (bf16[2,16384]{1,0:T(2,128)(2,1)}, bf16[2,16384]{1,0:T(2,128)(2,1)S(1)}, u32[]{:S(2)}, u32[]{:S(2)}) collective-permute-start(bf16[2,16384]{1,0:T(2,128)(2,1)} %bitcast.8), channel_id=1, source_target_pairs={{0,6},{2,0},{4,2},{6,4},{1,7},{3,1},{5,3},{7,5},{8,14},{10,8},{12,... | collective-permute-start | bytes 196616 | tf_op jit(solution)/shard_map/ppermute | solution.py:38
  7.1 6.7 %collective-permute-start.1 = (bf16[2,16384]{1,0:T(2,128)(2,1)}, bf16[2,16384]{1,0:T(2,128)(2,1)S(1)}, u32[]{:S(2)}, u32[]{:S(2)}) collective-permute-start(bf16[2,16384]{1,0:T(2,128)(2,1)} %bitcast.9), channel_id=1, source_target_pairs={{0,4},{2,6},{4,0},{6,2},{1,5},{3,7},{5,1},{7,3},{8,12},{10,14},{12... | collective-permute-start | bytes 196616 | tf_op jit(solution)/shard_map/ppermute | solution.py:38
  7.1 6.7 %collective-permute-start = (bf16[2,16384]{1,0:T(2,128)(2,1)}, bf16[2,16384]{1,0:T(2,128)(2,1)S(1)}, u32[]{:S(2)}, u32[]{:S(2)}) collective-permute-start(bf16[2,16384]{1,0:T(2,128)(2,1)} %bitcast.10), channel_id=1, source_target_pairs={{0,2},{2,4},{4,6},{6,0},{1,3},{3,5},{5,7},{7,1},{8,10},{10,12},{12... | collective-permute-start | bytes 196616 | tf_op jit(solution)/shard_map/ppermute | solution.py:38
  14.9 3.9 %collective-permute-start.3 = (bf16[8,16384]{1,0:T(8,128)(2,1)S(1)}, bf16[8,16384]{1,0:T(8,128)(2,1)S(1)}, u32[]{:S(2)}, u32[]{:S(2)}) collective-permute-start(bf16[8,16384]{1,0:T(8,128)(2,1)S(1)} %pad_maximum_fusion.refs_0_), channel_id=1, source_target_pairs={{0,8},{8,0},{16,24},{24,16},{1,9},{9,1},{17,25},{25,17},{2,10},{10... | collective-permute-start | bytes 786440 | tf_op jit(solution)/shard_map/ppermute | solution.py:89
  15.0 8.7 %collective-permute-start.10 = (bf16[8,16384]{1,0:T(8,128)(2,1)S(1)}, bf16[8,16384]{1,0:T(8,128)(2,1)S(1)}, u32[]{:S(2)}, u32[]{:S(2)}) collective-permute-start(bf16[8,16384]{1,0:T(8,128)(2,1)S(1)} %pad_maximum_fusion.refs_0_), channel_id=1, source_target_pairs={{0,16},{8,24},{16,0},{24,8},{1,17},{9,25},{17,1},{25,9},{2,18},{10... | collective-permute-start | bytes 786440 | tf_op jit(solution)/shard_map/ppermute | solution.py:38
  16.6 8.8 %collective-permute-start.8 = (bf16[8,16384]{1,0:T(8,128)(2,1)S(1)}, bf16[8,16384]{1,0:T(8,128)(2,1)S(1)}, u32[]{:S(2)}, u32[]{:S(2)}) collective-permute-start(bf16[8,16384]{1,0:T(8,128)(2,1)S(1)} %pad_maximum_fusion.refs_0_), channel_id=1, source_target_pairs={{0,1},{1,0},{2,3},{3,2},{4,5},{5,4},{6,7},{7,6},{8,9},{9,8},{10,11... | collective-permute-start | bytes 786440 | tf_op jit(solution)/shard_map/ppermute | solution.py:38
  18.9 8.0 %collective-permute-start.6 = (bf16[2,16384]{1,0:T(2,128)(2,1)}, bf16[2,16384]{1,0:T(2,128)(2,1)S(1)}, u32[]{:S(2)}, u32[]{:S(2)}) collective-permute-start(bf16[2,16384]{1,0:T(2,128)(2,1)} %bitcast.4), channel_id=1, source_target_pairs={{0,6},{2,0},{4,2},{6,4},{1,7},{3,1},{5,3},{7,5},{8,14},{10,8},{12,... | collective-permute-start | bytes 196616 | tf_op jit(solution)/shard_map/ppermute | solution.py:38
  20.8 7.2 %collective-permute-start.5 = (bf16[2,16384]{1,0:T(2,128)(2,1)}, bf16[2,16384]{1,0:T(2,128)(2,1)S(1)}, u32[]{:S(2)}, u32[]{:S(2)}) collective-permute-start(bf16[2,16384]{1,0:T(2,128)(2,1)} %bitcast.5), channel_id=1, source_target_pairs={{0,4},{2,6},{4,0},{6,2},{1,5},{3,7},{5,1},{7,3},{8,12},{10,14},{12... | collective-permute-start | bytes 196616 | tf_op jit(solution)/shard_map/ppermute | solution.py:38
  20.8 7.2 %collective-permute-start.4 = (bf16[2,16384]{1,0:T(2,128)(2,1)}, bf16[2,16384]{1,0:T(2,128)(2,1)S(1)}, u32[]{:S(2)}, u32[]{:S(2)}) collective-permute-start(bf16[2,16384]{1,0:T(2,128)(2,1)} %bitcast.6), channel_id=1, source_target_pairs={{0,2},{2,4},{4,6},{6,0},{1,3},{3,5},{5,7},{7,1},{8,10},{10,12},{12... | collective-permute-start | bytes 196616 | tf_op jit(solution)/shard_map/ppermute | solution.py:38
  23.8 5.4 %collective-permute-start.11 = (bf16[8,8192]{1,0:T(8,128)(2,1)S(1)}, bf16[8,8192]{1,0:T(8,128)(2,1)S(1)}, u32[]{:S(2)}, u32[]{:S(2)}) collective-permute-start(bf16[8,8192]{1,0:T(8,128)(2,1)S(1)} %slice.9), channel_id=1, source_target_pairs={{0,1},{1,0},{2,3},{3,2},{4,5},{5,4},{6,7},{7,6},{8,9},{9,8},{10,11... | collective-permute-start | bytes 393224 | tf_op jit(solution)/shard_map/ppermute | solution.py:38
  25.4 5.0 %collective-permute-start.9 = (bf16[8,8192]{1,0:T(8,128)(2,1)S(1)}, bf16[8,8192]{1,0:T(8,128)(2,1)S(1)}, u32[]{:S(2)}, u32[]{:S(2)}) collective-permute-start(bf16[8,8192]{1,0:T(8,128)(2,1)S(1)} %slice.8), channel_id=1, source_target_pairs={{0,16},{8,24},{16,0},{24,8},{1,17},{9,25},{17,1},{25,9},{2,18},{10... | collective-permute-start | bytes 393224 | tf_op jit(solution)/shard_map/ppermute | solution.py:38
  26.9 7.0 %collective-permute-start.15 = (bf16[8,16384]{1,0:T(8,128)(2,1)S(1)}, bf16[8,16384]{1,0:T(8,128)(2,1)S(1)}, u32[]{:S(2)}, u32[]{:S(2)}) collective-permute-start(bf16[8,16384]{1,0:T(8,128)(2,1)S(1)} %collective-permute-done.10.refs_4_), channel_id=1, source_target_pairs={{0,8},{8,0},{16,24},{24,16},{1,9},{9,1},{17,25},{25,17},{2,10},{10... | collective-permute-start | bytes 786440 | tf_op jit(solution)/shard_map/ppermute | solution.py:89
  28.0 5.9 %collective-permute-start.16 = (bf16[8,16384]{1,0:T(8,128)(2,1)S(1)}, bf16[8,16384]{1,0:T(8,128)(2,1)S(1)}, u32[]{:S(2)}, u32[]{:S(2)}) collective-permute-start(bf16[8,16384]{1,0:T(8,128)(2,1)S(1)} %collective-permute-done.8.refs_5_), channel_id=1, source_target_pairs={{0,8},{8,0},{16,24},{24,16},{1,9},{9,1},{17,25},{25,17},{2,10},{10... | collective-permute-start | bytes 786440 | tf_op jit(solution)/shard_map/ppermute | solution.py:89
  30.4 19.9 %collective-permute-start.14 = (bf16[8,16384]{1,0:T(8,128)(2,1)S(1)}, bf16[8,16384]{1,0:T(8,128)(2,1)S(1)}, u32[]{:S(2)}, u32[]{:S(2)}) collective-permute-start(bf16[8,16384]{1,0:T(8,128)(2,1)S(1)} %pad_maximum_fusion.1.refs_0_), channel_id=1, source_target_pairs={{0,17},{1,16},{8,25},{9,24},{16,1},{17,0},{24,9},{25,8},{2,19},{3,... | collective-permute-start | bytes 786440 | tf_op jit(solution)/shard_map/ppermute | solution.py:49
  31.8 18.5 %collective-permute-start.13 = (bf16[8,16384]{1,0:T(8,128)(2,1)S(1)}, bf16[8,16384]{1,0:T(8,128)(2,1)S(1)}, u32[]{:S(2)}, u32[]{:S(2)}) collective-permute-start(bf16[8,16384]{1,0:T(8,128)(2,1)S(1)} %pad_maximum_fusion.1.refs_0_), channel_id=1, source_target_pairs={{0,1},{1,0},{8,9},{9,8},{16,17},{17,16},{24,25},{25,24},{2,3},{3,2... | collective-permute-start | bytes 786440 | tf_op jit(solution)/shard_map/ppermute | solution.py:49
  33.3 17.0 %collective-permute-start.12 = (bf16[8,16384]{1,0:T(8,128)(2,1)S(1)}, bf16[8,16384]{1,0:T(8,128)(2,1)S(1)}, u32[]{:S(2)}, u32[]{:S(2)}) collective-permute-start(bf16[8,16384]{1,0:T(8,128)(2,1)S(1)} %pad_maximum_fusion.1.refs_0_), channel_id=1, source_target_pairs={{0,16},{1,17},{8,24},{9,25},{16,0},{17,1},{24,8},{25,9},{2,18},{3,... | collective-permute-start | bytes 786440 | tf_op jit(solution)/shard_map/ppermute | solution.py:49
  33.9 1.3 %collective-permute-start.18 = (bf16[8,8192]{1,0:T(8,128)(2,1)S(1)}, bf16[8,8192]{1,0:T(8,128)(2,1)S(1)}, u32[]{:S(2)}, u32[]{:S(2)}) collective-permute-start(bf16[8,8192]{1,0:T(8,128)(2,1)S(1)} %collective-permute-done.11.refs_8_), channel_id=1, source_target_pairs={{0,8},{8,0},{16,24},{24,16},{1,9},{9,1},{17,25},{25,17},{2,10},{10... | collective-permute-start | bytes 393224 | tf_op jit(solution)/shard_map/ppermute | solution.py:89
  33.9 1.5 %collective-permute-start.17 = (bf16[8,8192]{1,0:T(8,128)(2,1)S(1)}, bf16[8,8192]{1,0:T(8,128)(2,1)S(1)}, u32[]{:S(2)}, u32[]{:S(2)}) collective-permute-start(bf16[8,8192]{1,0:T(8,128)(2,1)S(1)} %collective-permute-done.9.refs_6_), channel_id=1, source_target_pairs={{0,8},{8,0},{16,24},{24,16},{1,9},{9,1},{17,25},{25,17},{2,10},{10... | collective-permute-start | bytes 393224 | tf_op jit(solution)/shard_map/ppermute | solution.py:89
  35.2 16.0 %collective-permute-start.7 = (bf16[8,16384]{1,0:T(8,128)(2,1)S(1)}, bf16[8,16384]{1,0:T(8,128)(2,1)S(1)}, u32[]{:S(2)}, u32[]{:S(2)}) collective-permute-start(bf16[8,16384]{1,0:T(8,128)(2,1)S(1)} %pad_maximum_fusion.1.refs_0_), channel_id=1, source_target_pairs={{0,8},{8,0},{16,24},{24,16},{1,9},{9,1},{17,25},{25,17},{2,10},{10... | collective-permute-start | bytes 786440 | tf_op jit(solution)/shard_map/ppermute | solution.py:89
  50.3 1.6 %collective-permute-start.19 = (bf16[8,16384]{1,0:T(8,128)(2,1)S(1)}, bf16[8,16384]{1,0:T(8,128)(2,1)S(1)}, u32[]{:S(2)}, u32[]{:S(2)}) collective-permute-start(bf16[8,16384]{1,0:T(8,128)(2,1)S(1)} %collective-permute-done.12.refs_5_), channel_id=1, source_target_pairs={{0,8},{8,0},{16,24},{24,16},{1,9},{9,1},{17,25},{25,17},{2,10},{10... | collective-permute-start | bytes 786440 | tf_op jit(solution)/shard_map/ppermute | solution.py:89
  50.7 1.6 %collective-permute-start.20 = (bf16[8,16384]{1,0:T(8,128)(2,1)S(1)}, bf16[8,16384]{1,0:T(8,128)(2,1)S(1)}, u32[]{:S(2)}, u32[]{:S(2)}) collective-permute-start(bf16[8,16384]{1,0:T(8,128)(2,1)S(1)} %collective-permute-done.13.refs_6_), channel_id=1, source_target_pairs={{0,8},{8,0},{16,24},{24,16},{1,9},{9,1},{17,25},{25,17},{2,10},{10... | collective-permute-start | bytes 786440 | tf_op jit(solution)/shard_map/ppermute | solution.py:89
  50.9 1.8 %collective-permute-start.21 = (bf16[8,16384]{1,0:T(8,128)(2,1)S(1)}, bf16[8,16384]{1,0:T(8,128)(2,1)S(1)}, u32[]{:S(2)}, u32[]{:S(2)}) collective-permute-start(bf16[8,16384]{1,0:T(8,128)(2,1)S(1)} %collective-permute-done.14.refs_7_), channel_id=1, source_target_pairs={{0,8},{8,0},{16,24},{24,16},{1,9},{9,1},{17,25},{25,17},{2,10},{10... | collective-permute-start | bytes 786440 | tf_op jit(solution)/shard_map/ppermute | solution.py:89

commit v4 on v3

--- a/solution.py
+++ b/solution.py
@@ -31,22 +31,9 @@
     return [slab.reshape(windows * parts, channels) for slab in slabs]
 
 
-def shift(value, axis, step, inner=1):
+def shift(value, axis, step):
     size = lax.axis_size(axis)
-    stops = size // inner
-    perm = [(at, (at // inner + step) % stops * inner + at % inner) for at in range(size)]
-    return lax.ppermute(value, axis, perm)
-
-
-def shift_plane(value, row_step, win_step, inner):
-    row_size, win_size = lax.axis_size("row"), lax.axis_size("win")
-    stops = row_size // inner
-    perm = []
-    for row in range(row_size):
-        for win in range(win_size):
-            to_row = (row // inner + row_step) % stops * inner + row % inner
-            perm.append((row * win_size + win, to_row * win_size + (win + win_step) % win_size))
-    return lax.ppermute(value, ("row", "win"), perm)
+    return lax.ppermute(value, axis, [(at, (at + step) % size) for at in range(size)])
 
 
 def gather_line(own):
@@ -54,43 +41,39 @@
     return jnp.concatenate(line, axis=0)
 
 
-def row_cores():
-    return 2 if lax.axis_size("row") % 2 == 0 else 1
-
-
-def gather_direct(block, earlier):
-    cores = row_cores()
-    sent = after(block, *earlier)
-    blocks = []
-    for win_step in range(lax.axis_size("win")):
-        for row_step in range(lax.axis_size("row") // cores):
-            if row_step + win_step > 0:
-                blocks.append(shift_plane(sent, row_step, win_step, cores))
-    return blocks
+def gather_chips(own):
+    return lax.all_gather(own, ("chip", "col", "win"), axis=0, tiled=True)
+
+
+def by_column(tile_rows, tile_cols):
+    total = tile_rows.shape[0]
+    place = jnp.arange(total, dtype=jnp.int32)
+    key = tile_cols * total + place
+    rank = jnp.sum((key[None, :] < key[:, None]).astype(jnp.int32), axis=1)
+    hit = rank[None, :] == place[:, None]
+    return jnp.concatenate(
+        [
+            jnp.sum(jnp.where(hit, values[None, :], 0), axis=1)
+            for values in (tile_rows, tile_cols, place)
+        ]
+    )
 
 
 def gather_relayed(block):
-    cores = row_cores()
     half = block.shape[1] // 2
-    along_row = [
-        shift(block, "row", step, cores) for step in range(1, lax.axis_size("row") // cores)
-    ]
+    along_chip = [shift(block, "chip", step) for step in range(1, lax.axis_size("chip"))]
     along_win = [shift(block, "win", step) for step in range(1, lax.axis_size("win"))]
     lows = []
     highs = []
-    for row_step, from_row in enumerate(along_row, 1):
+    for chip_step, from_chip in enumerate(along_chip, 1):
         for win_step, from_win in enumerate(along_win, 1):
-            lows.append(shift(from_win[:, :half], "row", row_step, cores))
-            highs.append(shift(from_row[:, half:], "win", win_step))
-    return along_row + along_win, lows, highs
-
-
-def swap_cores(value):
-    return lax.ppermute(value, "row", [(at, at ^ 1) for at in range(lax.axis_size("row"))])
-
-
-def after(value, *earlier):
-    return lax.optimization_barrier((value, *earlier))[0]
+            lows.append(shift(from_win[:, :half], "chip", chip_step))
+            highs.append(shift(from_chip[:, half:], "win", win_step))
+    return along_chip + along_win, lows, highs
+
+
+def swap_cores(values):
+    return [shift(value, "core", 1) for value in values] if lax.axis_size("core") == 2 else []
 
 
 def stack_kernel(counts, freq, scale, pack, lists_hbm, *refs):
@@ -125,9 +108,8 @@
     ).astype(jnp.bfloat16)
     place = lax.broadcasted_iota(jnp.int32, (2 * row_count, width), 1) // depth
 
-    def prepare(first, halves, at, carry):
-        near = pl.ds(pl.multiple_of(at * 2 * BLOCK, 2 * BLOCK), 2 * BLOCK)
-        at = at + first
+    def prepare(halves, first, at):
+        near = pl.ds(pl.multiple_of((at - first) * 2 * BLOCK, 2 * BLOCK), 2 * BLOCK)
         here = pl.ds(pl.multiple_of(at * 2 * BLOCK, 2 * BLOCK), 2 * BLOCK)
         pieces = [ref[:, here] for ref in whole] + [ref[:, near] for ref in halves]
         rows = jnp.concatenate(pieces, axis=0)
@@ -146,22 +128,39 @@
             lanes = slice(half * BLOCK, (half + 1) * BLOCK)
             right_ref[at * 2 + half, :, :BLOCK] = rows[:, lanes]
             right_ref[at * 2 + half, :, BLOCK:] = turned[:, lanes]
-        return carry
 
     pairs = whole[0].shape[1] // (2 * BLOCK)
-    runs = [(0, lows), (pairs // 2, highs)] if half_count else [(0, [])]
-    for first, halves in runs:
-        count = pairs // len(runs)
-        body = functools.partial(prepare, first, halves)
-        lax.fori_loop(0, count, body, 0, unroll=8 if count % 8 == 0 else 1)
+    span = math.gcd(pairs // 2, 8)
+    parts = pairs // span
+
+    def prepare_to(done, need):
+        def part(halves, first, at, carry):
+            for pair in range(span):
+                prepare(halves, first, at * span + pair)
+            return carry
+
+        if not half_count:
+            lax.fori_loop(done, need, functools.partial(part, [], 0), 0)
+            return
+        middle = parts // 2
+        lax.fori_loop(done, jnp.minimum(need, middle), functools.partial(part, lows, 0), 0)
+        first = functools.partial(part, highs, middle * span)
+        lax.fori_loop(jnp.maximum(done, middle), need, first, 0)
+
+    prepare_to(0, 1)
     lists.wait()
 
-    def send(step, slot, count=tiles):
-        return pltpu.make_async_copy(
-            ring_ref.at[slot, pl.ds(0, count)],
-            out_ref.at[pl.ds(step * tiles, count), freq],
-            sems.at[slot],
-        )
+    def send(step, slot, count):
+        for tile in range(count):
+            to = lists_ref[2 * total + step * tiles + tile]
+            pltpu.make_async_copy(
+                ring_ref.at[slot, tile], out_ref.at[to, freq], sems.at[slot]
+            ).start()
+
+    def sent(slot, count):
+        pltpu.make_async_copy(
+            ring_ref.at[slot, pl.ds(0, count)], out_ref.at[pl.ds(0, count), freq], sems.at[slot]
+        ).wait()
 
     def compute(step, slot, count):
         for group in range(count // pack):
@@ -193,28 +192,35 @@
     steps = total // tiles
     rest = total % tiles
 
-    def stack(step, carry):
+    def needed(last):
+        return lists_ref[total + last] // (2 * span) + 1
+
+    def stack(step, done):
         slot = lax.rem(step, slots)
+        need = jnp.maximum(needed(step * tiles + tiles - 1), done)
+        prepare_to(done, need)
 
         @pl.when(step >= slots)
         def _():
-            send(step - slots, slot).wait()
+            sent(slot, tiles)
 
         compute(step, slot, tiles)
-        send(step, slot).start()
-        return carry
-
-    lax.fori_loop(0, steps, stack, 0)
-    sent = [(step, tiles) for step in range(max(0, steps - slots), steps)]
+        send(step, slot, tiles)
+        return need
+
+    done = lax.fori_loop(0, steps, stack, jnp.int32(1))
+    flying = [(step % slots, tiles) for step in range(max(0, steps - slots), steps)]
     if rest:
+        prepare_to(done, needed(total - 1))
+        slot = steps % slots
         if steps >= slots:
-            send(sent[0][0], sent[0][0] % slots).wait()
-            sent = sent[1:]
-        compute(steps, steps % slots, rest)
-        send(steps, steps % slots, rest).start()
-        sent.append((steps, rest))
-    for step, count in sent:
-        send(step, step % slots, count).wait()
+            sent(slot, tiles)
+            flying = flying[1:]
+        compute(steps, slot, rest)
+        send(steps, slot, rest)
+        flying.append((slot, rest))
+    for slot, count in flying:
+        sent(slot, count)
 
 
 def stack_bin(freq, out_shape, lists, whole, lows, highs, scale, so_far):
@@ -224,7 +230,7 @@
     tile_total, _, parts, row_count, _ = out_shape.shape
     pack = math.gcd(tile_total, max(1, MXU // depth))
     copies = min(pack, max(1, BLOCK // depth))
-    tiles = max(pack, 48 // pack * pack)
+    tiles = max(pack, 24 // pack * pack)
     tiles = min(tiles, tile_total)
     blocks = channels // BLOCK
     vmem = pl.BlockSpec(memory_space=pltpu.VMEM)
@@ -235,7 +241,7 @@
         in_specs.append(pl.BlockSpec(memory_space=pl.ANY))
         aliases = {len(operands): 0}
         operands.append(so_far)
-    slots = 3
+    slots = 4
     scratch = [
         ((copies, blocks * row_count, copies * depth), jnp.bfloat16),
         ((blocks, depth, 2 * BLOCK), jnp.bfloat16),
@@ -262,8 +268,8 @@
 
 
 def on_device(spectra, tile_rows, tile_cols):
-    window_total = (
-        spectra.shape[2] * lax.axis_size("row") * lax.axis_size("col") * lax.axis_size("win")
+    window_total = spectra.shape[2] * math.prod(
+        lax.axis_size(axis) for axis in ("chip", "core", "col", "win")
     )
     scale = float(1.0 / window_total**0.5)
     slabs = whiten(spectra[0])
@@ -271,35 +277,29 @@
     out_shape = jax.ShapeDtypeStruct(
         (tile_rows.shape[0], len(slabs), 2, row_count, BLOCK), jnp.float32
     )
-    lists = jnp.concatenate([tile_rows, tile_cols])
-    swap = swap_cores if row_cores() == 2 else None
-    out = None
-    for freq, own in enumerate(slabs):
-        if freq > 0:
-            own = after(own, gate, lists)
-        block = gather_line(own)
-        whole = [block]
-        if swap:
-            whole.append(swap(block))
-        gate = whole[-1]
-        if freq == 0:
-            arrived, lows, highs = gather_relayed(block)
-            last = lows + highs if lows else arrived
-        else:
-            arrived, lows, highs = gather_direct(block, last), [], []
-            last = arrived
-        if swap:
-            ready = arrived if out is None else after(tuple(arrived), out)
-            whole += [swap(value) for value in ready]
-            lows = lows + [swap(value) for value in lows]
-            highs = highs + [swap(value) for value in highs]
-        out = stack_bin(freq, out_shape, lists, whole + arrived, lows, highs, scale, out)
+    lists = by_column(tile_rows, tile_cols)
+    block = gather_line(slabs[0])
+    arrived, lows, highs = gather_relayed(block)
+    whole = [block] + swap_cores([block]) + arrived + swap_cores(arrived)
+    lows = lows + swap_cores(lows)
+    highs = highs + swap_cores(highs)
+    later = [gather_chips(own) for own in slabs[1:]]
+    out = stack_bin(0, out_shape, lists, whole, lows, highs, scale, None)
+    for freq, rows in enumerate(later, 1):
+        rows = lax.optimization_barrier((rows, out))[0]
+        out = stack_bin(freq, out_shape, lists, [rows] + swap_cores([rows]), [], [], scale, out)
     return out
 
 
 def solution(mesh):
-    in_specs = (P("win", None, ("row", "col"), None, None), P(("row", "col")), P(("row", "col")))
-    out_specs = P(("row", "col"), None, None, "win", None)
+    rows, cols, wins = (mesh.shape[axis] for axis in ("row", "col", "win"))
+    cores = 2 if rows % 2 == 0 else 1
+    mesh = jax.sharding.Mesh(
+        mesh.devices.reshape(rows // cores, cores, cols, wins), ("chip", "core", "col", "win")
+    )
+    devices = ("chip", "core", "col")
+    in_specs = (P("win", None, devices, None, None), P(devices), P(devices))
+    out_specs = P(devices, None, None, "win", None)
     return jax.shard_map(
         on_device, mesh=mesh, in_specs=in_specs, out_specs=out_specs, check_vma=False
     )

time: 67.8 us -> 104 us (1.53)
  waiting for transfers between devices: 11.4 us -> 41.1 us
  between operations: 0.08 us -> 13.5 us
  starting transfers between devices: 21.2 us -> 12.9 us
  local copies, waits for them, and re-layouts: 0.02 us -> 4.44 us
  Pallas kernels: 31.8 us -> 29.9 us
    all_gather x0 -> x1, waiting for transfers between devices: none -> 25.3 us  [gather_chips(): return lax.all_gather(own, ('chip', 'col', 'win'), axis=0, tiled=True)]
    ppermute x22 -> x13, starting transfers between devices: 21.2 us -> 12.9 us  [shift(): lax.ppermute(value, axis, [(at, (at + step) % size) for at in range(size)])]
    ppermute x22 -> x13, waiting for transfers between devices: 11.4 us -> 15.7 us  [shift(): lax.ppermute(value, axis, [(at, (at + step) % size) for at in range(size)])]
    unnamed x0 -> x5, local copies, waits for them, and re-layouts: none -> 2.75 us
    pallas_call x2, Pallas kernels: 29.7 us -> 27.8 us  [stack_bin(): pl.pallas_call(functools.partial(stack_kernel, (len(whole), len(lows), le...]
    pallas_call x0 -> x1, local copies, waits for them, and re-layouts: none -> 1.59 us  [whiten(): pl.pallas_call(whiten_kernel, out_shape=[shape] * freqs, name='whiten')]
    concatenate x2 -> x1, other arithmetic: 2.28 us -> 1.14 us  [gather_line(): return jnp.concatenate(line, axis=0)]
    reduce_sum x0 -> x2, other arithmetic: none -> 1.06 us  [the longest x1 0.76 us: by_column(): jnp.sum(jnp.where(hit, values[None, :], 0), axis=1)]
  transfers between devices with their start and end apart: 22 -> 14, of which waited for: 9 -> 8; matrix products, arithmetic and copies ran while one was open for 3% -> 4% of each run, Pallas kernels for 22% -> 13%
where the time goes in v4:
time: 104 us
  waiting for transfers between devices  41.1 us (40%)
  Pallas kernels  29.9 us (29%)
  between operations  13.5 us (13%)
  starting transfers between devices  12.9 us (12%)
  local copies, waits for them, and re-layouts  4.44 us (4%)
  other arithmetic  2.21 us (2%)
    pallas_call x2, Pallas kernels, stack_bin(): pl.pallas_call(functools.partial(stack_kernel, (len(whole), len(lows), le...  27.8 us
    all_gather x1, waiting for transfers between devices, gather_chips(): return lax.all_gather(own, ('chip', 'col', 'win'), axis=0, tiled=True)  25.3 us
    ppermute x13, waiting for transfers between devices, shift(): lax.ppermute(value, axis, [(at, (at + step) % size) for at in range(size)])  15.7 us
    ppermute x13, starting transfers between devices, shift(): lax.ppermute(value, axis, [(at, (at + step) % size) for at in range(size)])  12.9 us
    unnamed x5, local copies, waits for them, and re-layouts  2.75 us
    pallas_call x1, Pallas kernels, whiten(): pl.pallas_call(whiten_kernel, out_shape=[shape] * freqs, name='whiten')  2.09 us
  transfers between devices with their start and end apart: 14, of which 8 were waited for; matrix products, arithmetic and copies ran while one was open for 4% of the time, Pallas kernels for 13%

profile of v4, /device:TPU:0, one launch (start us, length us, event | category | flops | bytes accessed | tf_op | source)
XLA Modules:
  0.0 104.0 jit_solution(6478168716018563641)
XLA Ops:
  6.5 2.1 %whiten.1 = (bf16[1,2,16384]{2,1,0:T(2,128)(2,1)}, bf16[1,2,16384]{2,1,0:T(2,128)(2,1)}) custom-call(f32[2,1,2,16384]{3,2,1,0:T(2,128)} %bitcast.7), custom_call_target="tpu_custom_call" | custom-call | tf_op jit(solution)/shard_map/whiten/pallas_call | solution.py:30
  8.6 5.0 %collective-permute-start.2 = (bf16[2,16384]{1,0:T(2,128)(2,1)}, bf16[2,16384]{1,0:T(2,128)(2,1)S(1)}, u32[]{:S(2)}, u32[]{:S(2)}) collective-permute-start(bf16[2,16384]{1,0:T(2,128)(2,1)} %bitcast.8), channel_id=1, source_target_pairs={{0,6},{2,0},{4,2},{6,4},{1,7},{3,1},{5,3},{7,5},{8,14},{10,8},{12,... | collective-permute-start | bytes 196616 | tf_op jit(solution)/shard_map/ppermute | solution.py:36
  13.7 1.0 collective-permute-start
  14.7 1.6 %copy.7 = bf16[1,2,16384]{2,0,1:T(2,128)(2,1)} copy(bf16[1,2,16384]{2,1,0:T(2,128)(2,1)} %get-tuple-element.8) | data formatting | bytes 131072 | tf_op jit(solution)/shard_map/whiten/pallas_call | solution.py:30
  16.3 0.0 all-gather.3.cloned.1.call-update
  16.3 0.2 collective-permute-done.2
  16.5 3.9 %collective-permute-done.1 = bf16[2,16384]{1,0:T(2,128)(2,1)S(1)} collective-permute-done((bf16[2,16384]{1,0:T(2,128)(2,1)}, bf16[2,16384]{1,0:T(2,128)(2,1)S(1)}, u32[]{:S(2)}, u32[]{:S(2)}) %collective-permute-start.1) | collective-permute-done | bytes 65568 | tf_op jit(solution)/shard_map/ppermute | solution.py:36
  20.4 1.1 %pad_maximum_fusion.refs_0_ = bf16[8,16384]{1,0:T(8,128)(2,1)S(1)} fusion(bf16[2,16384]{1,0:T(2,128)(2,1)S(1)} %collective-permute-done.2, bf16[2,16384]{1,0:T(2,128)(2,1)S(1)} %collective-permute-done.1, bf16[2,16384]{1,0:T(2,128)(2,1)S(1)} %collective-permute-done, bf16[2,16384]{1,0:T(2,128)(2,1)} %bitcast.11), kind=kLoop, calls=%fused_computation.6 | loop fusion | flops 1048576 | bytes 524288 | tf_op jit(solution)/shard_map/concatenate | solution.py:41
  21.5 1.6 %collective-permute-start.5 = (bf16[8,16384]{1,0:T(8,128)(2,1)S(1)}, bf16[8,16384]{1,0:T(8,128)(2,1)S(1)}, u32[]{:S(2)}, u32[]{:S(2)}) collective-permute-start(bf16[8,16384]{1,0:T(8,128)(2,1)S(1)} %pad_maximum_fusion.refs_0_), channel_id=1, source_target_pairs={{0,1},{1,0},{2,3},{3,2},{4,5},{5,4},{6,7},{7,6},{8,9},{9,8},{10,11... | collective-permute-start | bytes 786440 | tf_op jit(solution)/shard_map/ppermute | solution.py:36
  23.1 1.5 %collective-permute-start.4 = (bf16[8,16384]{1,0:T(8,128)(2,1)S(1)}, bf16[8,16384]{1,0:T(8,128)(2,1)S(1)}, u32[]{:S(2)}, u32[]{:S(2)}) collective-permute-start(bf16[8,16384]{1,0:T(8,128)(2,1)S(1)} %pad_maximum_fusion.refs_0_), channel_id=1, source_target_pairs={{0,16},{16,0},{1,17},{17,1},{2,18},{18,2},{3,19},{19,3},{4,20},{20... | collective-permute-start | bytes 786440 | tf_op jit(solution)/shard_map/ppermute | solution.py:36
  24.6 6.0 %collective-permute-done.5.refs_3_ = bf16[8,16384]{1,0:T(8,128)(2,1)S(1)} collective-permute-done((bf16[8,16384]{1,0:T(8,128)(2,1)S(1)}, bf16[8,16384]{1,0:T(8,128)(2,1)S(1)}, u32[]{:S(2)}, u32[]{:S(2)}) %collective-permute-start.5) | collective-permute-done | bytes 262176 | tf_op jit(solution)/shard_map/ppermute | solution.py:36
  30.6 1.6 %collective-permute-start.8 = (bf16[8,8192]{1,0:T(8,128)(2,1)S(1)}, bf16[8,8192]{1,0:T(8,128)(2,1)S(1)}, u32[]{:S(2)}, u32[]{:S(2)}) collective-permute-start(bf16[8,8192]{1,0:T(8,128)(2,1)S(1)} %slice.8), channel_id=1, source_target_pairs={{0,16},{16,0},{1,17},{17,1},{2,18},{18,2},{3,19},{19,3},{4,20},{20... | collective-permute-start | bytes 393224 | tf_op jit(solution)/shard_map/ppermute | solution.py:36
  32.1 0.0 collective-permute-done.4.refs_2_
  32.1 1.6 %collective-permute-start.10 = (bf16[8,8192]{1,0:T(8,128)(2,1)S(1)}, bf16[8,8192]{1,0:T(8,128)(2,1)S(1)}, u32[]{:S(2)}, u32[]{:S(2)}) collective-permute-start(bf16[8,8192]{1,0:T(8,128)(2,1)S(1)} %slice.9), channel_id=1, source_target_pairs={{0,1},{1,0},{2,3},{3,2},{4,5},{5,4},{6,7},{7,6},{8,9},{9,8},{10,11... | collective-permute-start | bytes 393224 | tf_op jit(solution)/shard_map/ppermute | solution.py:36
  33.7 0.0 collective-permute-start.3
  33.7 0.5 collective-permute-start.7
  34.2 0.1 collective-permute-start.6
  34.3 0.3 convert_reduce_fusion
  34.6 1.0 collective-permute-done.8.refs_6_
  35.6 0.0 collective-permute-start.9
  35.6 1.6 %collective-permute-done.10.refs_8_ = bf16[8,8192]{1,0:T(8,128)(2,1)S(1)} collective-permute-done((bf16[8,8192]{1,0:T(8,128)(2,1)S(1)}, bf16[8,8192]{1,0:T(8,128)(2,1)S(1)}, u32[]{:S(2)}, u32[]{:S(2)}) %collective-permute-start.10) | collective-permute-done | bytes 131104 | tf_op jit(solution)/shard_map/ppermute | solution.py:36
  37.2 0.8 select_reduce_fusion
  37.9 0.1 concatenate.6.lists_hbm
  38.0 0.0 collective-permute-done.3.refs_1_
  38.0 0.0 collective-permute-done.7.refs_5_
  38.1 0.5 collective-permute-done.11.refs_9_
  38.5 14.0 %stack.2.refs_2_ = f32[516,2,2,64,128]{4,3,2,1,0:T(8,128)} custom-call(s32[1548]{0:T(1024)S(1)} %concatenate.6.lists_hbm, bf16[8,16384]{1,0:T(8,128)(2,1)S(1)} %pad_maximum_fusion.refs_0_, bf16[8,16384]{1,0:T(8,128)(2,1)S(1)} %collective-permute-done.3.refs_1_, bf16[8,16384]{1,0:T(8,128)(2,1)S(1)} %collective-permute-done.4.refs_2_, ...), custom_call_target="tpu_custom_call" | custom-call | flops 1082130432 | bytes 33816576 | tf_op jit(solution)/shard_map/stack/pallas_call | solution.py:253
  52.5 25.3 %all-gather.3.cloned.1.call-done = bf16[1,32,16384]{2,0,1:T(2,128)(2,1)} async-done(((bf16[1,2,16384]{2,0,1:T(2,128)(2,1)}), bf16[1,32,16384]{2,0,1:T(2,128)(2,1)}) %all-gather.3.cloned.1.call-update) | async-done | bytes 1048592 | tf_op jit(solution)/shard_map/all_gather | solution.py:45
  77.9 2.7 %copy.10 = bf16[1,32,16384]{2,1,0:T(8,128)(2,1)S(1)} copy(bf16[1,32,16384]{2,0,1:T(2,128)(2,1)} %all-gather.3.cloned.1.call-done) | data formatting | bytes 2097152
  80.6 0.1 collective-permute-start.12
  80.7 2.6 %collective-permute-done.12.refs_1_ = bf16[32,16384]{1,0:T(8,128)(2,1)S(1)} collective-permute-done((bf16[32,16384]{1,0:T(8,128)(2,1)S(1)}, bf16[32,16384]{1,0:T(8,128)(2,1)S(1)}, u32[]{:S(2)}, u32[]{:S(2)}) %collective-permute-start.12) | collective-permute-done | bytes 1048608 | tf_op jit(solution)/shard_map/ppermute | solution.py:36
  83.4 13.8 %stack.3 = f32[516,2,2,64,128]{4,3,2,1,0:T(8,128)} custom-call(s32[1548]{0:T(1024)S(1)} %concatenate.6.lists_hbm, bf16[32,16384]{1,0:T(8,128)(2,1)S(1)} %bitcast.6, bf16[32,16384]{1,0:T(8,128)(2,1)S(1)} %collective-permute-done.12.refs_1_, f32[516,2,2,64,128]{4,3,2,1,0:T(8,128)} %stack.2.refs_2_), custom_call_target="tpu_custom_call", output_to_operand_aliasing={{}: (3, {})} | custom-call | flops 1082130432 | bytes 33816576 | tf_op jit(solution)/shard_map/stack/pallas_call | solution.py:253
  (13 shorter events, 0.0 us)
Async XLA Ops:
  6.5 27.2 %copy-start = (s32[516]{0:T(1024)S(1)}, s32[516]{0:T(1024)}, u32[]{:S(2)}) copy-start(s32[516]{0:T(1024)} %param.5) | copy-start | bytes 6196
  6.5 30.6 %copy-start.1 = (s32[516]{0:T(1024)S(1)}, s32[516]{0:T(1024)}, u32[]{:S(2)}) copy-start(s32[516]{0:T(1024)} %param.4) | copy-start | bytes 6196
  6.5 71.4 %all-gather.3.cloned.1.call-start = ((), (), s32[]{:S(2)}) async-start(), calls=%async_computation | async-start | bytes 2228224 | tf_op jit(solution)/shard_map/all_gather | solution.py:45
  8.6 7.9 %collective-permute-start.2 = (bf16[2,16384]{1,0:T(2,128)(2,1)}, bf16[2,16384]{1,0:T(2,128)(2,1)S(1)}, u32[]{:S(2)}, u32[]{:S(2)}) collective-permute-start(bf16[2,16384]{1,0:T(2,128)(2,1)} %bitcast.8), channel_id=1, source_target_pairs={{0,6},{2,0},{4,2},{6,4},{1,7},{3,1},{5,3},{7,5},{8,14},{10,8},{12,... | collective-permute-start | bytes 196616 | tf_op jit(solution)/shard_map/ppermute | solution.py:36
  13.7 6.7 %collective-permute-start.1 = (bf16[2,16384]{1,0:T(2,128)(2,1)}, bf16[2,16384]{1,0:T(2,128)(2,1)S(1)}, u32[]{:S(2)}, u32[]{:S(2)}) collective-permute-start(bf16[2,16384]{1,0:T(2,128)(2,1)} %bitcast.9), channel_id=1, source_target_pairs={{0,4},{2,6},{4,0},{6,2},{1,5},{3,7},{5,1},{7,3},{8,12},{10,14},{12... | collective-permute-start | bytes 196616 | tf_op jit(solution)/shard_map/ppermute | solution.py:36
  13.7 6.7 %collective-permute-start = (bf16[2,16384]{1,0:T(2,128)(2,1)}, bf16[2,16384]{1,0:T(2,128)(2,1)S(1)}, u32[]{:S(2)}, u32[]{:S(2)}) collective-permute-start(bf16[2,16384]{1,0:T(2,128)(2,1)} %bitcast.10), channel_id=1, source_target_pairs={{0,2},{2,4},{4,6},{6,0},{1,3},{3,5},{5,7},{7,1},{8,10},{10,12},{12... | collective-permute-start | bytes 196616 | tf_op jit(solution)/shard_map/ppermute | solution.py:36
  21.5 9.0 %collective-permute-start.5 = (bf16[8,16384]{1,0:T(8,128)(2,1)S(1)}, bf16[8,16384]{1,0:T(8,128)(2,1)S(1)}, u32[]{:S(2)}, u32[]{:S(2)}) collective-permute-start(bf16[8,16384]{1,0:T(8,128)(2,1)S(1)} %pad_maximum_fusion.refs_0_), channel_id=1, source_target_pairs={{0,1},{1,0},{2,3},{3,2},{4,5},{5,4},{6,7},{7,6},{8,9},{9,8},{10,11... | collective-permute-start | bytes 786440 | tf_op jit(solution)/shard_map/ppermute | solution.py:36
  23.1 9.0 %collective-permute-start.4 = (bf16[8,16384]{1,0:T(8,128)(2,1)S(1)}, bf16[8,16384]{1,0:T(8,128)(2,1)S(1)}, u32[]{:S(2)}, u32[]{:S(2)}) collective-permute-start(bf16[8,16384]{1,0:T(8,128)(2,1)S(1)} %pad_maximum_fusion.refs_0_), channel_id=1, source_target_pairs={{0,16},{16,0},{1,17},{17,1},{2,18},{18,2},{3,19},{19,3},{4,20},{20... | collective-permute-start | bytes 786440 | tf_op jit(solution)/shard_map/ppermute | solution.py:36
  30.6 5.0 %collective-permute-start.8 = (bf16[8,8192]{1,0:T(8,128)(2,1)S(1)}, bf16[8,8192]{1,0:T(8,128)(2,1)S(1)}, u32[]{:S(2)}, u32[]{:S(2)}) collective-permute-start(bf16[8,8192]{1,0:T(8,128)(2,1)S(1)} %slice.8), channel_id=1, source_target_pairs={{0,16},{16,0},{1,17},{17,1},{2,18},{18,2},{3,19},{19,3},{4,20},{20... | collective-permute-start | bytes 393224 | tf_op jit(solution)/shard_map/ppermute | solution.py:36
  32.1 5.0 %collective-permute-start.10 = (bf16[8,8192]{1,0:T(8,128)(2,1)S(1)}, bf16[8,8192]{1,0:T(8,128)(2,1)S(1)}, u32[]{:S(2)}, u32[]{:S(2)}) collective-permute-start(bf16[8,8192]{1,0:T(8,128)(2,1)S(1)} %slice.9), channel_id=1, source_target_pairs={{0,1},{1,0},{2,3},{3,2},{4,5},{5,4},{6,7},{7,6},{8,9},{9,8},{10,11... | collective-permute-start | bytes 393224 | tf_op jit(solution)/shard_map/ppermute | solution.py:36
  33.7 4.3 %collective-permute-start.3 = (bf16[8,16384]{1,0:T(8,128)(2,1)S(1)}, bf16[8,16384]{1,0:T(8,128)(2,1)S(1)}, u32[]{:S(2)}, u32[]{:S(2)}) collective-permute-start(bf16[8,16384]{1,0:T(8,128)(2,1)S(1)} %pad_maximum_fusion.refs_0_), channel_id=1, source_target_pairs={{0,8},{8,0},{1,9},{9,1},{2,10},{10,2},{3,11},{11,3},{4,12},{12,4},... | collective-permute-start | bytes 786440 | tf_op jit(solution)/shard_map/ppermute | solution.py:36
  33.7 4.3 %collective-permute-start.7 = (bf16[8,16384]{1,0:T(8,128)(2,1)S(1)}, bf16[8,16384]{1,0:T(8,128)(2,1)S(1)}, u32[]{:S(2)}, u32[]{:S(2)}) collective-permute-start(bf16[8,16384]{1,0:T(8,128)(2,1)S(1)} %collective-permute-done.5.refs_3_), channel_id=1, source_target_pairs={{0,8},{8,0},{1,9},{9,1},{2,10},{10,2},{3,11},{11,3},{4,12},{12,4},... | collective-permute-start | bytes 786440 | tf_op jit(solution)/shard_map/ppermute | solution.py:36
  34.2 3.8 %collective-permute-start.6 = (bf16[8,16384]{1,0:T(8,128)(2,1)S(1)}, bf16[8,16384]{1,0:T(8,128)(2,1)S(1)}, u32[]{:S(2)}, u32[]{:S(2)}) collective-permute-start(bf16[8,16384]{1,0:T(8,128)(2,1)S(1)} %collective-permute-done.4.refs_2_), channel_id=1, source_target_pairs={{0,8},{8,0},{1,9},{9,1},{2,10},{10,2},{3,11},{11,3},{4,12},{12,4},... | collective-permute-start | bytes 786440 | tf_op jit(solution)/shard_map/ppermute | solution.py:36
  35.6 2.4 %collective-permute-start.9 = (bf16[8,8192]{1,0:T(8,128)(2,1)S(1)}, bf16[8,8192]{1,0:T(8,128)(2,1)S(1)}, u32[]{:S(2)}, u32[]{:S(2)}) collective-permute-start(bf16[8,8192]{1,0:T(8,128)(2,1)S(1)} %collective-permute-done.8.refs_6_), channel_id=1, source_target_pairs={{0,8},{8,0},{1,9},{9,1},{2,10},{10,2},{3,11},{11,3},{4,12},{12,4},... | collective-permute-start | bytes 393224 | tf_op jit(solution)/shard_map/ppermute | solution.py:36
  37.2 1.3 %collective-permute-start.11 = (bf16[8,8192]{1,0:T(8,128)(2,1)S(1)}, bf16[8,8192]{1,0:T(8,128)(2,1)S(1)}, u32[]{:S(2)}, u32[]{:S(2)}) collective-permute-start(bf16[8,8192]{1,0:T(8,128)(2,1)S(1)} %collective-permute-done.10.refs_8_), channel_id=1, source_target_pairs={{0,8},{8,0},{1,9},{9,1},{2,10},{10,2},{3,11},{11,3},{4,12},{12,4},... | collective-permute-start | bytes 393224 | tf_op jit(solution)/shard_map/ppermute | solution.py:36
  80.6 2.7 %collective-permute-start.12 = (bf16[32,16384]{1,0:T(8,128)(2,1)S(1)}, bf16[32,16384]{1,0:T(8,128)(2,1)S(1)}, u32[]{:S(2)}, u32[]{:S(2)}) collective-permute-start(bf16[32,16384]{1,0:T(8,128)(2,1)S(1)} %bitcast.5), channel_id=1, source_target_pairs={{0,8},{8,0},{1,9},{9,1},{2,10},{10,2},{3,11},{11,3},{4,12},{12,4},... | collective-permute-start | bytes 3145736 | tf_op jit(solution)/shard_map/ppermute | solution.py:36
Sparse Core Ops, SparseCore 0:
  16.4 61.4 all-gather.2

commit v5 on v4

--- a/solution.py
+++ b/solution.py
@@ -12,23 +12,29 @@
 MXU = 256
 
 
-def whiten_kernel(spectra_ref, *out_refs):
+def whiten_kernel(freq, spectra_ref, out_ref):
     freqs = spectra_ref.shape[0]
     power = None
-    for freq in range(freqs):
-        slab = spectra_ref[freq]
+    for at in range(freqs):
+        slab = spectra_ref[at]
         term = jnp.sum(slab * slab, axis=1, keepdims=True)
         power = term if power is None else power + term
     factor = jnp.minimum(lax.rsqrt(power / freqs), 1.0)
-    for freq in range(freqs):
-        out_refs[freq][...] = (spectra_ref[freq] * factor).astype(jnp.bfloat16)
-
-
-def whiten(spectra):
-    freqs, windows, parts, channels = spectra.shape
-    shape = jax.ShapeDtypeStruct((windows, parts, channels), jnp.bfloat16)
-    slabs = pl.pallas_call(whiten_kernel, out_shape=[shape] * freqs, name="whiten")(spectra)
-    return [slab.reshape(windows * parts, channels) for slab in slabs]
+    out_ref[...] = (spectra_ref[freq] * factor).astype(jnp.bfloat16)
+
+
+def whiten(spectra, freq):
+    _, windows, parts, channels = spectra.shape
+    slab = pl.pallas_call(
+        functools.partial(whiten_kernel, freq),
+        out_shape=jax.ShapeDtypeStruct((windows, parts, channels), jnp.bfloat16),
+        name="whiten",
+    )(spectra)
+    return slab.reshape(windows * parts, channels)
+
+
+def after(value, *earlier):
+    return lax.optimization_barrier((value, *earlier))[0]
 
 
 def shift(value, axis, step):
@@ -41,8 +47,18 @@
     return jnp.concatenate(line, axis=0)
 
 
-def gather_chips(own):
-    return lax.all_gather(own, ("chip", "col", "win"), axis=0, tiled=True)
+def gather_direct(block):
+    chips, wins = lax.axis_size("chip"), lax.axis_size("win")
+    blocks = []
+    for step in range(1, chips * wins):
+        chip_step, win_step = step % chips, step // chips
+        perm = []
+        for chip in range(chips):
+            for win in range(wins):
+                to = (chip + chip_step) % chips * wins + (win + win_step) % wins
+                perm.append((chip * wins + win, to))
+        blocks.append(lax.ppermute(block, ("chip", "win"), perm))
+    return blocks
 
 
 def by_column(tile_rows, tile_cols):
@@ -150,9 +166,9 @@
     prepare_to(0, 1)
     lists.wait()
 
-    def send(step, slot, count):
-        for tile in range(count):
-            to = lists_ref[2 * total + step * tiles + tile]
+    def send(first, slot, tiles_here):
+        for tile in tiles_here:
+            to = lists_ref[2 * total + first + tile]
             pltpu.make_async_copy(
                 ring_ref.at[slot, tile], out_ref.at[to, freq], sems.at[slot]
             ).start()
@@ -162,12 +178,12 @@
             ring_ref.at[slot, pl.ds(0, count)], out_ref.at[pl.ds(0, count), freq], sems.at[slot]
         ).wait()
 
-    def compute(step, slot, count):
+    def compute(first, slot, count, between):
         for group in range(count // pack):
             lefts = []
             rights = []
             for member in range(pack):
-                at = step * tiles + group * pack + member
+                at = first + group * pack + member
                 left_at = pl.multiple_of(lists_ref[at] * row_count, row_count)
                 left = left_ref[member % copies, pl.ds(left_at, row_count), :]
                 if chunks > 1:
@@ -188,38 +204,54 @@
                 mine = product[member * row_count : (member + 1) * row_count]
                 ring_ref[slot, group * pack + member, 0] = mine[:, :BLOCK]
                 ring_ref[slot, group * pack + member, 1] = mine[:, BLOCK:]
-
-    steps = total // tiles
-    rest = total % tiles
+            between(group)
 
     def needed(last):
         return lists_ref[total + last] // (2 * span) + 1
 
-    def stack(step, done):
+    start = total % tiles or tiles
+    steps = (total - start) // tiles
+    groups = tiles // pack
+
+    def first_of(step):
+        return start + (step - 1) * tiles
+
+    done = jnp.maximum(needed(start - 1), 1)
+    prepare_to(1, done)
+    compute(0, 0, start, lambda group: None)
+    send(0, 0, range(start))
+
+    def stack(step, done, opening):
+        first = first_of(step)
         slot = lax.rem(step, slots)
-        need = jnp.maximum(needed(step * tiles + tiles - 1), done)
+        before = lax.rem(step + slots - 1, slots)
+        need = jnp.maximum(needed(first + tiles - 1), done)
         prepare_to(done, need)
 
-        @pl.when(step >= slots)
+        @pl.when(step > slots)
         def _():
             sent(slot, tiles)
 
-        compute(step, slot, tiles)
-        send(step, slot, tiles)
+        if opening:
+            compute(first, slot, tiles, lambda group: None)
+            return need
+
+        @pl.when(step == slots)
+        def _():
+            sent(slot, start)
+
+        def between(group):
+            send(first - tiles, before, range(group * pack, (group + 1) * pack))
+
+        compute(first, slot, tiles, between)
         return need
 
-    done = lax.fori_loop(0, steps, stack, jnp.int32(1))
-    flying = [(step % slots, tiles) for step in range(max(0, steps - slots), steps)]
-    if rest:
-        prepare_to(done, needed(total - 1))
-        slot = steps % slots
-        if steps >= slots:
-            sent(slot, tiles)
-            flying = flying[1:]
-        compute(steps, slot, rest)
-        send(steps, slot, rest)
-        flying.append((slot, rest))
-    for slot, count in flying:
+    if steps:
+        done = stack(1, done, True)
+        lax.fori_loop(2, steps + 1, lambda step, done: stack(step, done, False), done)
+        send(first_of(steps), steps % slots, range(tiles))
+    flying = [(step % slots, tiles if step else start) for step in range(steps + 1)]
+    for slot, count in flying[-slots:]:
         sent(slot, count)
 
 
@@ -249,7 +281,6 @@
     ]
     used = [(value.shape, value.dtype) for value in pieces] + scratch
     vmem_bytes = sum(math.prod(shape) * jnp.dtype(kind).itemsize for shape, kind in used)
-    product = tile_total * row_count * 2 * BLOCK
     return pl.pallas_call(
         functools.partial(stack_kernel, (len(whole), len(lows), len(aliases)), freq, scale, pack),
         out_shape=out_shape,
@@ -259,9 +290,7 @@
         + [pltpu.SMEM(lists.shape, jnp.int32)]
         + [pltpu.SemaphoreType.DMA((slots,)), pltpu.SemaphoreType.DMA],
         input_output_aliases=aliases,
-        cost_estimate=pl.CostEstimate(
-            flops=2 * product * depth, bytes_accessed=4 * product, transcendentals=0
-        ),
+        cost_estimate=pl.CostEstimate(flops=0, bytes_accessed=0, transcendentals=0),
         compiler_params=pltpu.CompilerParams(vmem_limit_bytes=vmem_bytes + 8 * 1024 * 1024),
         name="stack",
     )(*operands)
@@ -272,22 +301,30 @@
         lax.axis_size(axis) for axis in ("chip", "core", "col", "win")
     )
     scale = float(1.0 / window_total**0.5)
-    slabs = whiten(spectra[0])
+    freqs = spectra.shape[1]
     row_count = BLOCK // lax.axis_size("win")
     out_shape = jax.ShapeDtypeStruct(
-        (tile_rows.shape[0], len(slabs), 2, row_count, BLOCK), jnp.float32
+        (tile_rows.shape[0], freqs, 2, row_count, BLOCK), jnp.float32
     )
     lists = by_column(tile_rows, tile_cols)
-    block = gather_line(slabs[0])
+    block = gather_line(whiten(spectra[0], 0))
+    swapped = swap_cores([block])
     arrived, lows, highs = gather_relayed(block)
-    whole = [block] + swap_cores([block]) + arrived + swap_cores(arrived)
+    whole = [block] + swapped + arrived + swap_cores(arrived)
     lows = lows + swap_cores(lows)
     highs = highs + swap_cores(highs)
-    later = [gather_chips(own) for own in slabs[1:]]
+    later = []
+    for freq in range(1, freqs):
+        own = after(whiten(spectra[0], freq), *swapped)
+        block = gather_line(own)
+        swapped = swap_cores([block])
+        arrived = gather_direct(after(block, *arrived))
+        later.append(([block] + swapped, arrived))
     out = stack_bin(0, out_shape, lists, whole, lows, highs, scale, None)
-    for freq, rows in enumerate(later, 1):
-        rows = lax.optimization_barrier((rows, out))[0]
-        out = stack_bin(freq, out_shape, lists, [rows] + swap_cores([rows]), [], [], scale, out)
+    for freq, (whole, arrived) in enumerate(later, 1):
+        arrived = list(after(tuple(arrived), out))
+        whole = whole + arrived + swap_cores(arrived)
+        out = stack_bin(freq, out_shape, lists, whole, [], [], scale, out)
     return out
 
 

time: 104 us -> 67.3 us (0.65)
  waiting for transfers between devices: 41.1 us -> 9.43 us
  between operations: 13.5 us -> 0.1 us
  starting transfers between devices: 12.9 us -> 20.5 us
  local copies, waits for them, and re-layouts: 4.44 us -> 0.1 us
  Pallas kernels: 29.9 us -> 32.8 us
  other arithmetic: 2.21 us -> 4.03 us
    all_gather x1 -> x0, waiting for transfers between devices: 25.3 us -> none  [gather_chips(): return lax.all_gather(own, ('chip', 'col', 'win'), axis=0, tiled=True)]
    ppermute x13 -> x19, waiting for transfers between devices: 15.7 us -> 9.42 us  [shift(): lax.ppermute(value, axis, [(at, (at + step) % size) for at in range(size)])]
    ppermute x13 -> x19, starting transfers between devices: 12.9 us -> 17 us  [shift(): lax.ppermute(value, axis, [(at, (at + step) % size) for at in range(size)])]
    ppermute x0 -> x3, starting transfers between devices: none -> 3.55 us  [gather_direct(): blocks.append(lax.ppermute(block, ('chip', 'win'), perm))]
    unnamed x5 -> x4, local copies, waits for them, and re-layouts: 2.75 us -> 0.01 us
    pallas_call x1 -> x2, Pallas kernels: 2.09 us -> 4.08 us  [whiten(): pl.pallas_call(functools.partial(whiten_kernel, freq), out_shape=jax.Shap...]
    pallas_call x1 -> x0, local copies, waits for them, and re-layouts: 1.59 us -> none  [whiten(): pl.pallas_call(whiten_kernel, out_shape=[shape] * freqs, name='whiten')]
    concatenate x1 -> x2, other arithmetic: 1.14 us -> 2.28 us  [gather_line(): return jnp.concatenate(line, axis=0)]
  transfers between devices with their start and end apart: 14 -> 22, of which waited for: 8 -> 6; matrix products, arithmetic and copies ran while one was open for 4% -> 4% of each run, Pallas kernels for 13% -> 24%
where the time goes in v5:
time: 67.3 us; the launch traced here: 67 us
  Pallas kernels  32.8 us (49%)
  starting transfers between devices  20.5 us (30%)
  waiting for transfers between devices  9.43 us (14%)
  other arithmetic  4.03 us (6%)
    pallas_call x2, Pallas kernels, stack_bin(): pl.pallas_call(functools.partial(stack_kernel, (len(whole), len(lows), le...  28.7 us
    ppermute x19, starting transfers between devices, shift(): lax.ppermute(value, axis, [(at, (at + step) % size) for at in range(size)])  17 us
    ppermute x19, waiting for transfers between devices, shift(): lax.ppermute(value, axis, [(at, (at + step) % size) for at in range(size)])  9.42 us
    pallas_call x2, Pallas kernels, whiten(): pl.pallas_call(functools.partial(whiten_kernel, freq), out_shape=jax.Shap...  4.08 us
    ppermute x3, starting transfers between devices, gather_direct(): blocks.append(lax.ppermute(block, ('chip', 'win'), perm))  3.55 us
    concatenate x2, other arithmetic, gather_line(): return jnp.concatenate(line, axis=0)  2.28 us
  transfers between devices with their start and end apart: 22, of which 6 were waited for; matrix products, arithmetic and copies ran while one was open for 4% of the time, Pallas kernels for 24%

profile of v5, /device:TPU:0, one launch (start us, length us, event | category | flops | bytes accessed | tf_op | source)
XLA Modules:
  0.0 67.0 jit_solution(2336192156208653067)
XLA Ops:
  0.0 2.1 %whiten.3 = bf16[1,2,16384]{2,1,0:T(2,128)(2,1)} custom-call(f32[2,1,2,16384]{3,2,1,0:T(2,128)} %bitcast.3), custom_call_target="tpu_custom_call" | custom-call | tf_op jit(solution)/shard_map/whiten/pallas_call | solution.py:28
  2.1 5.0 %collective-permute-start.2 = (bf16[2,16384]{1,0:T(2,128)(2,1)}, bf16[2,16384]{1,0:T(2,128)(2,1)S(1)}, u32[]{:S(2)}, u32[]{:S(2)}) collective-permute-start(bf16[2,16384]{1,0:T(2,128)(2,1)} %bitcast.9), channel_id=1, source_target_pairs={{0,6},{2,0},{4,2},{6,4},{1,7},{3,1},{5,3},{7,5},{8,14},{10,8},{12,... | collective-permute-start | bytes 196616 | tf_op jit(solution)/shard_map/ppermute | solution.py:42
  7.1 1.0 %collective-permute-start = (bf16[2,16384]{1,0:T(2,128)(2,1)}, bf16[2,16384]{1,0:T(2,128)(2,1)S(1)}, u32[]{:S(2)}, u32[]{:S(2)}) collective-permute-start(bf16[2,16384]{1,0:T(2,128)(2,1)} %bitcast.11), channel_id=1, source_target_pairs={{0,2},{2,4},{4,6},{6,0},{1,3},{3,5},{5,7},{7,1},{8,10},{10,12},{12... | collective-permute-start | bytes 196616 | tf_op jit(solution)/shard_map/ppermute | solution.py:42
  8.1 1.8 %collective-permute-done.2 = bf16[2,16384]{1,0:T(2,128)(2,1)S(1)} collective-permute-done((bf16[2,16384]{1,0:T(2,128)(2,1)}, bf16[2,16384]{1,0:T(2,128)(2,1)S(1)}, u32[]{:S(2)}, u32[]{:S(2)}) %collective-permute-start.2) | collective-permute-done | bytes 65568 | tf_op jit(solution)/shard_map/ppermute | solution.py:42
  9.9 3.9 %collective-permute-done.1 = bf16[2,16384]{1,0:T(2,128)(2,1)S(1)} collective-permute-done((bf16[2,16384]{1,0:T(2,128)(2,1)}, bf16[2,16384]{1,0:T(2,128)(2,1)S(1)}, u32[]{:S(2)}, u32[]{:S(2)}) %collective-permute-start.1) | collective-permute-done | bytes 65568 | tf_op jit(solution)/shard_map/ppermute | solution.py:42
  13.8 1.1 %pad_maximum_fusion.refs_0_ = bf16[8,16384]{1,0:T(8,128)(2,1)S(1)} fusion(bf16[2,16384]{1,0:T(2,128)(2,1)S(1)} %collective-permute-done.2, bf16[2,16384]{1,0:T(2,128)(2,1)S(1)} %collective-permute-done.1, bf16[2,16384]{1,0:T(2,128)(2,1)S(1)} %collective-permute-done, bf16[2,16384]{1,0:T(2,128)(2,1)} %bitcast.12), kind=kLoop, calls=%fused_computation.5 | loop fusion | flops 1048576 | bytes 524288 | tf_op jit(solution)/shard_map/concatenate | solution.py:47
  15.0 1.6 %collective-permute-start.9 = (bf16[8,16384]{1,0:T(8,128)(2,1)S(1)}, bf16[8,16384]{1,0:T(8,128)(2,1)S(1)}, u32[]{:S(2)}, u32[]{:S(2)}) collective-permute-start(bf16[8,16384]{1,0:T(8,128)(2,1)S(1)} %pad_maximum_fusion.refs_0_), channel_id=1, source_target_pairs={{0,1},{1,0},{2,3},{3,2},{4,5},{5,4},{6,7},{7,6},{8,9},{9,8},{10,11... | collective-permute-start | bytes 786440 | tf_op jit(solution)/shard_map/ppermute | solution.py:42
  16.6 1.5 %collective-permute-start.8 = (bf16[8,16384]{1,0:T(8,128)(2,1)S(1)}, bf16[8,16384]{1,0:T(8,128)(2,1)S(1)}, u32[]{:S(2)}, u32[]{:S(2)}) collective-permute-start(bf16[8,16384]{1,0:T(8,128)(2,1)S(1)} %pad_maximum_fusion.refs_0_), channel_id=1, source_target_pairs={{0,16},{16,0},{1,17},{17,1},{2,18},{18,2},{3,19},{19,3},{4,20},{20... | collective-permute-start | bytes 786440 | tf_op jit(solution)/shard_map/ppermute | solution.py:42
  18.1 2.0 %whiten.2 = bf16[1,2,16384]{2,1,0:T(2,128)(2,1)} custom-call(f32[2,1,2,16384]{3,2,1,0:T(2,128)} %bitcast.4), custom_call_target="tpu_custom_call" | custom-call | tf_op jit(solution)/shard_map/whiten/pallas_call | solution.py:28
  20.1 1.9 %collective-permute-start.6 = (bf16[2,16384]{1,0:T(2,128)(2,1)}, bf16[2,16384]{1,0:T(2,128)(2,1)S(1)}, u32[]{:S(2)}, u32[]{:S(2)}) collective-permute-start(bf16[2,16384]{1,0:T(2,128)(2,1)} %bitcast.5), channel_id=1, source_target_pairs={{0,6},{2,0},{4,2},{6,4},{1,7},{3,1},{5,3},{7,5},{8,14},{10,8},{12,... | collective-permute-start | bytes 196616 | tf_op jit(solution)/shard_map/ppermute | solution.py:42
  22.0 1.9 %collective-permute-start.4 = (bf16[2,16384]{1,0:T(2,128)(2,1)}, bf16[2,16384]{1,0:T(2,128)(2,1)S(1)}, u32[]{:S(2)}, u32[]{:S(2)}) collective-permute-start(bf16[2,16384]{1,0:T(2,128)(2,1)} %bitcast.7), channel_id=1, source_target_pairs={{0,2},{2,4},{4,6},{6,0},{1,3},{3,5},{5,7},{7,1},{8,10},{10,12},{12... | collective-permute-start | bytes 196616 | tf_op jit(solution)/shard_map/ppermute | solution.py:42
  23.9 0.7 %iota_add_fusion = s32[516]{0:T(1024)S(1)} fusion(s32[516]{0:T(1024)} %param.5), kind=kLoop, calls=%fused_computation.7 | loop fusion | flops 1032 | bytes 4128 | tf_op jit(solution)/shard_map/add | solution.py:67
  24.6 0.7 %collective-permute-start.15 = (bf16[8,8192]{1,0:T(8,128)(2,1)S(1)}, bf16[8,8192]{1,0:T(8,128)(2,1)S(1)}, u32[]{:S(2)}, u32[]{:S(2)}) collective-permute-start(bf16[8,8192]{1,0:T(8,128)(2,1)S(1)} %slice.8), channel_id=1, source_target_pairs={{0,16},{16,0},{1,17},{17,1},{2,18},{18,2},{3,19},{19,3},{4,20},{20... | collective-permute-start | bytes 393224 | tf_op jit(solution)/shard_map/ppermute | solution.py:42
  25.3 1.6 %collective-permute-start.17 = (bf16[8,8192]{1,0:T(8,128)(2,1)S(1)}, bf16[8,8192]{1,0:T(8,128)(2,1)S(1)}, u32[]{:S(2)}, u32[]{:S(2)}) collective-permute-start(bf16[8,8192]{1,0:T(8,128)(2,1)S(1)} %slice.9), channel_id=1, source_target_pairs={{0,1},{1,0},{2,3},{3,2},{4,5},{5,4},{6,7},{7,6},{8,9},{9,8},{10,11... | collective-permute-start | bytes 393224 | tf_op jit(solution)/shard_map/ppermute | solution.py:42
  26.9 2.3 %collective-permute-done.5 = bf16[2,16384]{1,0:T(2,128)(2,1)S(1)} collective-permute-done((bf16[2,16384]{1,0:T(2,128)(2,1)}, bf16[2,16384]{1,0:T(2,128)(2,1)S(1)}, u32[]{:S(2)}, u32[]{:S(2)}) %collective-permute-start.5) | collective-permute-done | bytes 65568 | tf_op jit(solution)/shard_map/ppermute | solution.py:42
  29.2 1.1 %pad_maximum_fusion.1.refs_0_ = bf16[8,16384]{1,0:T(8,128)(2,1)S(1)} fusion(bf16[2,16384]{1,0:T(2,128)(2,1)S(1)} %collective-permute-done.6, bf16[2,16384]{1,0:T(2,128)(2,1)S(1)} %collective-permute-done.5, bf16[2,16384]{1,0:T(2,128)(2,1)S(1)} %collective-permute-done.4, bf16[2,16384]{1,0:T(2,128)(2,1)} %bitcast.8), kind=kLoop, calls=%fused_computation.6 | loop fusion | flops 1048576 | bytes 524288 | tf_op jit(solution)/shard_map/concatenate | solution.py:47
  30.4 0.5 collective-permute-start.12
  30.9 1.5 %collective-permute-start.11 = (bf16[8,16384]{1,0:T(8,128)(2,1)S(1)}, bf16[8,16384]{1,0:T(8,128)(2,1)S(1)}, u32[]{:S(2)}, u32[]{:S(2)}) collective-permute-start(bf16[8,16384]{1,0:T(8,128)(2,1)S(1)} %pad_maximum_fusion.1.refs_0_), channel_id=1, source_target_pairs={{0,1},{1,0},{16,17},{17,16},{2,3},{3,2},{18,19},{19,18},{4,5},{5,4... | collective-permute-start | bytes 786440 | tf_op jit(solution)/shard_map/ppermute | solution.py:60
  32.4 1.5 %collective-permute-start.10 = (bf16[8,16384]{1,0:T(8,128)(2,1)S(1)}, bf16[8,16384]{1,0:T(8,128)(2,1)S(1)}, u32[]{:S(2)}, u32[]{:S(2)}) collective-permute-start(bf16[8,16384]{1,0:T(8,128)(2,1)S(1)} %pad_maximum_fusion.1.refs_0_), channel_id=1, source_target_pairs={{0,16},{1,17},{16,0},{17,1},{2,18},{3,19},{18,2},{19,3},{4,20},{5,... | collective-permute-start | bytes 786440 | tf_op jit(solution)/shard_map/ppermute | solution.py:60
  33.9 0.3 convert_reduce_fusion
  34.3 0.5 collective-permute-start.18
  34.8 0.8 %select_reduce_fusion = (s32[516]{0:T(1024)S(1)}, s32[516]{0:T(1024)S(1)}, s32[516]{0:T(1024)S(1)}) fusion(s32[516]{0:T(1024)S(1)} %convert_reduce_fusion, s32[516]{0:T(1024)S(1)} %copy-done, s32[516]{0:T(1024)S(1)} %copy-done.1), kind=kLoop, calls=%fused_computation | loop fusion | flops 1862244 | bytes 12384 | tf_op jit(solution)/shard_map/reduce_sum | solution.py:72
  35.6 0.1 concatenate.9.lists_hbm
  35.7 0.2 collective-permute-start.7
  35.8 14.4 %stack.2.refs_8_ = f32[516,2,2,64,128]{4,3,2,1,0:T(8,128)} custom-call(s32[1548]{0:T(1024)S(1)} %concatenate.9.lists_hbm, bf16[8,16384]{1,0:T(8,128)(2,1)S(1)} %pad_maximum_fusion.refs_0_, bf16[8,16384]{1,0:T(8,128)(2,1)S(1)} %collective-permute-done.3.refs_1_, bf16[8,16384]{1,0:T(8,128)(2,1)S(1)} %collective-permute-done.8.refs_2_, ...), custom_call_target="tpu_custom_call" | custom-call | tf_op jit(solution)/shard_map/stack/pallas_call | solution.py:284
  50.3 0.5 collective-permute-start.19
  50.7 0.1 collective-permute-start.20
  50.8 0.4 collective-permute-start.21
  51.3 0.6 collective-permute-done.19.refs_5_
  51.9 0.4 collective-permute-done.20.refs_6_
  52.3 0.4 collective-permute-done.21.refs_7_
  52.7 14.3 %stack.3 = f32[516,2,2,64,128]{4,3,2,1,0:T(8,128)} custom-call(s32[1548]{0:T(1024)S(1)} %concatenate.9.lists_hbm, bf16[8,16384]{1,0:T(8,128)(2,1)S(1)} %pad_maximum_fusion.1.refs_0_, bf16[8,16384]{1,0:T(8,128)(2,1)S(1)} %collective-permute-done.7.refs_1_, bf16[8,16384]{1,0:T(8,128)(2,1)S(1)} %collective-permute-done.10.refs_2_, ...), custom_call_target="tpu_custom_call", output_to_operand_aliasing={{}: (9, {})} | custom-call | tf_op jit(solution)/shard_map/stack/pallas_call | solution.py:284
  (28 shorter events, 0.2 us)
Async XLA Ops:
  0.0 34.8 %copy-start = (s32[516]{0:T(1024)S(1)}, s32[516]{0:T(1024)}, u32[]{:S(2)}) copy-start(s32[516]{0:T(1024)} %param.5) | copy-start | bytes 6196
  0.0 34.8 %copy-start.1 = (s32[516]{0:T(1024)S(1)}, s32[516]{0:T(1024)}, u32[]{:S(2)}) copy-start(s32[516]{0:T(1024)} %param.4) | copy-start | bytes 6196
  2.1 7.9 %collective-permute-start.2 = (bf16[2,16384]{1,0:T(2,128)(2,1)}, bf16[2,16384]{1,0:T(2,128)(2,1)S(1)}, u32[]{:S(2)}, u32[]{:S(2)}) collective-permute-start(bf16[2,16384]{1,0:T(2,128)(2,1)} %bitcast.9), channel_id=1, source_target_pairs={{0,6},{2,0},{4,2},{6,4},{1,7},{3,1},{5,3},{7,5},{8,14},{10,8},{12,... | collective-permute-start | bytes 196616 | tf_op jit(solution)/shard_map/ppermute | solution.py:42
  7.1 6.7 %collective-permute-start.1 = (bf16[2,16384]{1,0:T(2,128)(2,1)}, bf16[2,16384]{1,0:T(2,128)(2,1)S(1)}, u32[]{:S(2)}, u32[]{:S(2)}) collective-permute-start(bf16[2,16384]{1,0:T(2,128)(2,1)} %bitcast.10), channel_id=1, source_target_pairs={{0,4},{2,6},{4,0},{6,2},{1,5},{3,7},{5,1},{7,3},{8,12},{10,14},{12... | collective-permute-start | bytes 196616 | tf_op jit(solution)/shard_map/ppermute | solution.py:42
  7.1 6.7 %collective-permute-start = (bf16[2,16384]{1,0:T(2,128)(2,1)}, bf16[2,16384]{1,0:T(2,128)(2,1)S(1)}, u32[]{:S(2)}, u32[]{:S(2)}) collective-permute-start(bf16[2,16384]{1,0:T(2,128)(2,1)} %bitcast.11), channel_id=1, source_target_pairs={{0,2},{2,4},{4,6},{6,0},{1,3},{3,5},{5,7},{7,1},{8,10},{10,12},{12... | collective-permute-start | bytes 196616 | tf_op jit(solution)/shard_map/ppermute | solution.py:42
  14.9 5.2 %collective-permute-start.3 = (bf16[8,16384]{1,0:T(8,128)(2,1)S(1)}, bf16[8,16384]{1,0:T(8,128)(2,1)S(1)}, u32[]{:S(2)}, u32[]{:S(2)}) collective-permute-start(bf16[8,16384]{1,0:T(8,128)(2,1)S(1)} %pad_maximum_fusion.refs_0_), channel_id=1, source_target_pairs={{0,8},{8,0},{1,9},{9,1},{2,10},{10,2},{3,11},{11,3},{4,12},{12,4},... | collective-permute-start | bytes 786440 | tf_op jit(solution)/shard_map/ppermute | solution.py:42
  15.0 9.6 %collective-permute-start.9 = (bf16[8,16384]{1,0:T(8,128)(2,1)S(1)}, bf16[8,16384]{1,0:T(8,128)(2,1)S(1)}, u32[]{:S(2)}, u32[]{:S(2)}) collective-permute-start(bf16[8,16384]{1,0:T(8,128)(2,1)S(1)} %pad_maximum_fusion.refs_0_), channel_id=1, source_target_pairs={{0,1},{1,0},{2,3},{3,2},{4,5},{5,4},{6,7},{7,6},{8,9},{9,8},{10,11... | collective-permute-start | bytes 786440 | tf_op jit(solution)/shard_map/ppermute | solution.py:42
  16.6 8.7 %collective-permute-start.8 = (bf16[8,16384]{1,0:T(8,128)(2,1)S(1)}, bf16[8,16384]{1,0:T(8,128)(2,1)S(1)}, u32[]{:S(2)}, u32[]{:S(2)}) collective-permute-start(bf16[8,16384]{1,0:T(8,128)(2,1)S(1)} %pad_maximum_fusion.refs_0_), channel_id=1, source_target_pairs={{0,16},{16,0},{1,17},{17,1},{2,18},{18,2},{3,19},{19,3},{4,20},{20... | collective-permute-start | bytes 786440 | tf_op jit(solution)/shard_map/ppermute | solution.py:42
  20.1 6.8 %collective-permute-start.6 = (bf16[2,16384]{1,0:T(2,128)(2,1)}, bf16[2,16384]{1,0:T(2,128)(2,1)S(1)}, u32[]{:S(2)}, u32[]{:S(2)}) collective-permute-start(bf16[2,16384]{1,0:T(2,128)(2,1)} %bitcast.5), channel_id=1, source_target_pairs={{0,6},{2,0},{4,2},{6,4},{1,7},{3,1},{5,3},{7,5},{8,14},{10,8},{12,... | collective-permute-start | bytes 196616 | tf_op jit(solution)/shard_map/ppermute | solution.py:42
  22.0 7.2 %collective-permute-start.5 = (bf16[2,16384]{1,0:T(2,128)(2,1)}, bf16[2,16384]{1,0:T(2,128)(2,1)S(1)}, u32[]{:S(2)}, u32[]{:S(2)}) collective-permute-start(bf16[2,16384]{1,0:T(2,128)(2,1)} %bitcast.6), channel_id=1, source_target_pairs={{0,4},{2,6},{4,0},{6,2},{1,5},{3,7},{5,1},{7,3},{8,12},{10,14},{12... | collective-permute-start | bytes 196616 | tf_op jit(solution)/shard_map/ppermute | solution.py:42
  22.0 7.2 %collective-permute-start.4 = (bf16[2,16384]{1,0:T(2,128)(2,1)}, bf16[2,16384]{1,0:T(2,128)(2,1)S(1)}, u32[]{:S(2)}, u32[]{:S(2)}) collective-permute-start(bf16[2,16384]{1,0:T(2,128)(2,1)} %bitcast.7), channel_id=1, source_target_pairs={{0,2},{2,4},{4,6},{6,0},{1,3},{3,5},{5,7},{7,1},{8,10},{10,12},{12... | collective-permute-start | bytes 196616 | tf_op jit(solution)/shard_map/ppermute | solution.py:42
  24.6 6.3 %collective-permute-start.15 = (bf16[8,8192]{1,0:T(8,128)(2,1)S(1)}, bf16[8,8192]{1,0:T(8,128)(2,1)S(1)}, u32[]{:S(2)}, u32[]{:S(2)}) collective-permute-start(bf16[8,8192]{1,0:T(8,128)(2,1)S(1)} %slice.8), channel_id=1, source_target_pairs={{0,16},{16,0},{1,17},{17,1},{2,18},{18,2},{3,19},{19,3},{4,20},{20... | collective-permute-start | bytes 393224 | tf_op jit(solution)/shard_map/ppermute | solution.py:42
  25.3 7.1 %collective-permute-start.17 = (bf16[8,8192]{1,0:T(8,128)(2,1)S(1)}, bf16[8,8192]{1,0:T(8,128)(2,1)S(1)}, u32[]{:S(2)}, u32[]{:S(2)}) collective-permute-start(bf16[8,8192]{1,0:T(8,128)(2,1)S(1)} %slice.9), channel_id=1, source_target_pairs={{0,1},{1,0},{2,3},{3,2},{4,5},{5,4},{6,7},{7,6},{8,9},{9,8},{10,11... | collective-permute-start | bytes 393224 | tf_op jit(solution)/shard_map/ppermute | solution.py:42
  26.9 7.3 %collective-permute-start.14 = (bf16[8,16384]{1,0:T(8,128)(2,1)S(1)}, bf16[8,16384]{1,0:T(8,128)(2,1)S(1)}, u32[]{:S(2)}, u32[]{:S(2)}) collective-permute-start(bf16[8,16384]{1,0:T(8,128)(2,1)S(1)} %collective-permute-done.9.refs_3_), channel_id=1, source_target_pairs={{0,8},{8,0},{1,9},{9,1},{2,10},{10,2},{3,11},{11,3},{4,12},{12,4},... | collective-permute-start | bytes 786440 | tf_op jit(solution)/shard_map/ppermute | solution.py:42
  29.2 5.1 %collective-permute-start.13 = (bf16[8,16384]{1,0:T(8,128)(2,1)S(1)}, bf16[8,16384]{1,0:T(8,128)(2,1)S(1)}, u32[]{:S(2)}, u32[]{:S(2)}) collective-permute-start(bf16[8,16384]{1,0:T(8,128)(2,1)S(1)} %collective-permute-done.8.refs_2_), channel_id=1, source_target_pairs={{0,8},{8,0},{1,9},{9,1},{2,10},{10,2},{3,11},{11,3},{4,12},{12,4},... | collective-permute-start | bytes 786440 | tf_op jit(solution)/shard_map/ppermute | solution.py:42
  30.4 19.9 %collective-permute-start.12 = (bf16[8,16384]{1,0:T(8,128)(2,1)S(1)}, bf16[8,16384]{1,0:T(8,128)(2,1)S(1)}, u32[]{:S(2)}, u32[]{:S(2)}) collective-permute-start(bf16[8,16384]{1,0:T(8,128)(2,1)S(1)} %pad_maximum_fusion.1.refs_0_), channel_id=1, source_target_pairs={{0,17},{1,16},{16,1},{17,0},{2,19},{3,18},{18,3},{19,2},{4,21},{5,... | collective-permute-start | bytes 786440 | tf_op jit(solution)/shard_map/ppermute | solution.py:60
  30.9 19.3 %collective-permute-start.11 = (bf16[8,16384]{1,0:T(8,128)(2,1)S(1)}, bf16[8,16384]{1,0:T(8,128)(2,1)S(1)}, u32[]{:S(2)}, u32[]{:S(2)}) collective-permute-start(bf16[8,16384]{1,0:T(8,128)(2,1)S(1)} %pad_maximum_fusion.1.refs_0_), channel_id=1, source_target_pairs={{0,1},{1,0},{16,17},{17,16},{2,3},{3,2},{18,19},{19,18},{4,5},{5,4... | collective-permute-start | bytes 786440 | tf_op jit(solution)/shard_map/ppermute | solution.py:60
  32.4 17.8 %collective-permute-start.10 = (bf16[8,16384]{1,0:T(8,128)(2,1)S(1)}, bf16[8,16384]{1,0:T(8,128)(2,1)S(1)}, u32[]{:S(2)}, u32[]{:S(2)}) collective-permute-start(bf16[8,16384]{1,0:T(8,128)(2,1)S(1)} %pad_maximum_fusion.1.refs_0_), channel_id=1, source_target_pairs={{0,16},{1,17},{16,0},{17,1},{2,18},{3,19},{18,2},{19,3},{4,20},{5,... | collective-permute-start | bytes 786440 | tf_op jit(solution)/shard_map/ppermute | solution.py:60
  34.2 1.4 %collective-permute-start.16 = (bf16[8,8192]{1,0:T(8,128)(2,1)S(1)}, bf16[8,8192]{1,0:T(8,128)(2,1)S(1)}, u32[]{:S(2)}, u32[]{:S(2)}) collective-permute-start(bf16[8,8192]{1,0:T(8,128)(2,1)S(1)} %collective-permute-done.15.refs_6_), channel_id=1, source_target_pairs={{0,8},{8,0},{1,9},{9,1},{2,10},{10,2},{3,11},{11,3},{4,12},{12,4},... | collective-permute-start | bytes 393224 | tf_op jit(solution)/shard_map/ppermute | solution.py:42
  34.3 1.5 %collective-permute-start.18 = (bf16[8,8192]{1,0:T(8,128)(2,1)S(1)}, bf16[8,8192]{1,0:T(8,128)(2,1)S(1)}, u32[]{:S(2)}, u32[]{:S(2)}) collective-permute-start(bf16[8,8192]{1,0:T(8,128)(2,1)S(1)} %collective-permute-done.17.refs_8_), channel_id=1, source_target_pairs={{0,8},{8,0},{1,9},{9,1},{2,10},{10,2},{3,11},{11,3},{4,12},{12,4},... | collective-permute-start | bytes 393224 | tf_op jit(solution)/shard_map/ppermute | solution.py:42
  35.7 15.6 %collective-permute-start.7 = (bf16[8,16384]{1,0:T(8,128)(2,1)S(1)}, bf16[8,16384]{1,0:T(8,128)(2,1)S(1)}, u32[]{:S(2)}, u32[]{:S(2)}) collective-permute-start(bf16[8,16384]{1,0:T(8,128)(2,1)S(1)} %pad_maximum_fusion.1.refs_0_), channel_id=1, source_target_pairs={{0,8},{8,0},{1,9},{9,1},{2,10},{10,2},{3,11},{11,3},{4,12},{12,4},... | collective-permute-start | bytes 786440 | tf_op jit(solution)/shard_map/ppermute | solution.py:42
  50.3 1.6 %collective-permute-start.19 = (bf16[8,16384]{1,0:T(8,128)(2,1)S(1)}, bf16[8,16384]{1,0:T(8,128)(2,1)S(1)}, u32[]{:S(2)}, u32[]{:S(2)}) collective-permute-start(bf16[8,16384]{1,0:T(8,128)(2,1)S(1)} %collective-permute-done.10.refs_2_), channel_id=1, source_target_pairs={{0,8},{8,0},{1,9},{9,1},{2,10},{10,2},{3,11},{11,3},{4,12},{12,4},... | collective-permute-start | bytes 786440 | tf_op jit(solution)/shard_map/ppermute | solution.py:42
  50.7 1.5 %collective-permute-start.20 = (bf16[8,16384]{1,0:T(8,128)(2,1)S(1)}, bf16[8,16384]{1,0:T(8,128)(2,1)S(1)}, u32[]{:S(2)}, u32[]{:S(2)}) collective-permute-start(bf16[8,16384]{1,0:T(8,128)(2,1)S(1)} %collective-permute-done.11.refs_3_), channel_id=1, source_target_pairs={{0,8},{8,0},{1,9},{9,1},{2,10},{10,2},{3,11},{11,3},{4,12},{12,4},... | collective-permute-start | bytes 786440 | tf_op jit(solution)/shard_map/ppermute | solution.py:42
  50.8 1.8 %collective-permute-start.21 = (bf16[8,16384]{1,0:T(8,128)(2,1)S(1)}, bf16[8,16384]{1,0:T(8,128)(2,1)S(1)}, u32[]{:S(2)}, u32[]{:S(2)}) collective-permute-start(bf16[8,16384]{1,0:T(8,128)(2,1)S(1)} %collective-permute-done.12.refs_4_), channel_id=1, source_target_pairs={{0,8},{8,0},{1,9},{9,1},{2,10},{10,2},{3,11},{11,3},{4,12},{12,4},... | collective-permute-start | bytes 786440 | tf_op jit(solution)/shard_map/ppermute | solution.py:42

commit v6 on v4

--- a/solution.py
+++ b/solution.py
@@ -31,6 +31,10 @@
     return [slab.reshape(windows * parts, channels) for slab in slabs]
 
 
+def after(value, *earlier):
+    return lax.optimization_barrier((value, *earlier))[0]
+
+
 def shift(value, axis, step):
     size = lax.axis_size(axis)
     return lax.ppermute(value, axis, [(at, (at + step) % size) for at in range(size)])
@@ -41,8 +45,19 @@
     return jnp.concatenate(line, axis=0)
 
 
-def gather_chips(own):
-    return lax.all_gather(own, ("chip", "col", "win"), axis=0, tiled=True)
+def gather_direct(block, near, far):
+    chips, wins = lax.axis_size("chip"), lax.axis_size("win")
+    blocks = []
+    for step in range(1, chips * wins):
+        chip_step, win_step = step % chips, step // chips
+        perm = []
+        for chip in range(chips):
+            for win in range(wins):
+                to = (chip + chip_step) % chips * wins + (win + win_step) % wins
+                perm.append((chip * wins + win, to))
+        sent = after(block, *(far if chip_step and win_step else near))
+        blocks.append(lax.ppermute(sent, ("chip", "win"), perm))
+    return blocks
 
 
 def by_column(tile_rows, tile_cols):
@@ -150,9 +165,9 @@
     prepare_to(0, 1)
     lists.wait()
 
-    def send(step, slot, count):
-        for tile in range(count):
-            to = lists_ref[2 * total + step * tiles + tile]
+    def send(first, slot, tiles_here):
+        for tile in tiles_here:
+            to = lists_ref[2 * total + first + tile]
             pltpu.make_async_copy(
                 ring_ref.at[slot, tile], out_ref.at[to, freq], sems.at[slot]
             ).start()
@@ -162,12 +177,12 @@
             ring_ref.at[slot, pl.ds(0, count)], out_ref.at[pl.ds(0, count), freq], sems.at[slot]
         ).wait()
 
-    def compute(step, slot, count):
+    def compute(first, slot, count):
         for group in range(count // pack):
             lefts = []
             rights = []
             for member in range(pack):
-                at = step * tiles + group * pack + member
+                at = first + group * pack + member
                 left_at = pl.multiple_of(lists_ref[at] * row_count, row_count)
                 left = left_ref[member % copies, pl.ds(left_at, row_count), :]
                 if chunks > 1:
@@ -189,35 +204,36 @@
                 ring_ref[slot, group * pack + member, 0] = mine[:, :BLOCK]
                 ring_ref[slot, group * pack + member, 1] = mine[:, BLOCK:]
 
+    def needed(last):
+        return lists_ref[total + last] // (2 * span) + 1
+
     steps = total // tiles
     rest = total % tiles
 
-    def needed(last):
-        return lists_ref[total + last] // (2 * span) + 1
-
     def stack(step, done):
+        first = step * tiles
         slot = lax.rem(step, slots)
-        need = jnp.maximum(needed(step * tiles + tiles - 1), done)
+        need = jnp.maximum(needed(first + tiles - 1), done)
         prepare_to(done, need)
 
         @pl.when(step >= slots)
         def _():
             sent(slot, tiles)
 
-        compute(step, slot, tiles)
-        send(step, slot, tiles)
+        compute(first, slot, tiles)
+        send(first, slot, range(tiles))
         return need
 
     done = lax.fori_loop(0, steps, stack, jnp.int32(1))
-    flying = [(step % slots, tiles) for step in range(max(0, steps - slots), steps)]
+    flying = [(step % slots, tiles) for step in range(steps)][-slots:]
     if rest:
         prepare_to(done, needed(total - 1))
         slot = steps % slots
         if steps >= slots:
             sent(slot, tiles)
             flying = flying[1:]
-        compute(steps, slot, rest)
-        send(steps, slot, rest)
+        compute(steps * tiles, slot, rest)
+        send(steps * tiles, slot, range(rest))
         flying.append((slot, rest))
     for slot, count in flying:
         sent(slot, count)
@@ -249,7 +265,6 @@
     ]
     used = [(value.shape, value.dtype) for value in pieces] + scratch
     vmem_bytes = sum(math.prod(shape) * jnp.dtype(kind).itemsize for shape, kind in used)
-    product = tile_total * row_count * 2 * BLOCK
     return pl.pallas_call(
         functools.partial(stack_kernel, (len(whole), len(lows), len(aliases)), freq, scale, pack),
         out_shape=out_shape,
@@ -259,9 +274,7 @@
         + [pltpu.SMEM(lists.shape, jnp.int32)]
         + [pltpu.SemaphoreType.DMA((slots,)), pltpu.SemaphoreType.DMA],
         input_output_aliases=aliases,
-        cost_estimate=pl.CostEstimate(
-            flops=2 * product * depth, bytes_accessed=4 * product, transcendentals=0
-        ),
+        cost_estimate=pl.CostEstimate(flops=0, bytes_accessed=0, transcendentals=0),
         compiler_params=pltpu.CompilerParams(vmem_limit_bytes=vmem_bytes + 8 * 1024 * 1024),
         name="stack",
     )(*operands)
@@ -272,22 +285,33 @@
         lax.axis_size(axis) for axis in ("chip", "core", "col", "win")
     )
     scale = float(1.0 / window_total**0.5)
-    slabs = whiten(spectra[0])
+    freqs = spectra.shape[1]
     row_count = BLOCK // lax.axis_size("win")
     out_shape = jax.ShapeDtypeStruct(
-        (tile_rows.shape[0], len(slabs), 2, row_count, BLOCK), jnp.float32
+        (tile_rows.shape[0], freqs, 2, row_count, BLOCK), jnp.float32
     )
     lists = by_column(tile_rows, tile_cols)
+    slabs = whiten(spectra[0])
     block = gather_line(slabs[0])
+    block, lists = lax.optimization_barrier((block, lists))
+    swapped = swap_cores([block])
     arrived, lows, highs = gather_relayed(block)
-    whole = [block] + swap_cores([block]) + arrived + swap_cores(arrived)
+    near, far = arrived, lows + highs
+    whole = [block] + swapped + arrived + swap_cores(arrived)
     lows = lows + swap_cores(lows)
     highs = highs + swap_cores(highs)
-    later = [gather_chips(own) for own in slabs[1:]]
+    later = []
+    for own in slabs[1:]:
+        block = gather_line(after(own, *swapped))
+        swapped = swap_cores([block])
+        arrived = gather_direct(block, near, far)
+        near, far = arrived, arrived
+        later.append(([block] + swapped, arrived))
     out = stack_bin(0, out_shape, lists, whole, lows, highs, scale, None)
-    for freq, rows in enumerate(later, 1):
-        rows = lax.optimization_barrier((rows, out))[0]
-        out = stack_bin(freq, out_shape, lists, [rows] + swap_cores([rows]), [], [], scale, out)
+    for freq, (whole, arrived) in enumerate(later, 1):
+        arrived = list(after(tuple(arrived), out))
+        whole = whole + arrived + swap_cores(arrived)
+        out = stack_bin(freq, out_shape, lists, whole, [], [], scale, out)
     return out
 
 

time: 104 us -> 64.3 us (0.62)
  waiting for transfers between devices: 41.1 us -> 7.6 us
  between operations: 13.5 us -> 0.08 us
  starting transfers between devices: 12.9 us -> 21.5 us
  local copies, waits for them, and re-layouts: 4.44 us -> 0.1 us
  other arithmetic: 2.21 us -> 4.74 us
    all_gather x1 -> x0, waiting for transfers between devices: 25.3 us -> none  [gather_chips(): return lax.all_gather(own, ('chip', 'col', 'win'), axis=0, tiled=True)]
    ppermute x13 -> x19, waiting for transfers between devices: 15.7 us -> 7.59 us  [shift(): lax.ppermute(value, axis, [(at, (at + step) % size) for at in range(size)])]
    ppermute x13 -> x19, starting transfers between devices: 12.9 us -> 17.9 us  [shift(): lax.ppermute(value, axis, [(at, (at + step) % size) for at in range(size)])]
    ppermute x0 -> x3, starting transfers between devices: none -> 3.55 us  [gather_direct(): blocks.append(lax.ppermute(sent, ('chip', 'win'), perm))]
    unnamed x5 -> x0, local copies, waits for them, and re-layouts: 2.75 us -> none
    pallas_call x1 -> x0, local copies, waits for them, and re-layouts: 1.59 us -> none  [whiten(): pl.pallas_call(whiten_kernel, out_shape=[shape] * freqs, name='whiten')]
    concatenate x1 -> x2, other arithmetic: 1.14 us -> 2.28 us  [gather_line(): return jnp.concatenate(line, axis=0)]
  transfers between devices with their start and end apart: 14 -> 22, of which waited for: 8 -> 7; matrix products, arithmetic and copies ran while one was open for 4% -> 6% of each run, Pallas kernels for 13% -> 22%
where the time goes in v6:
time: 64.3 us; the launch traced here: 63.9 us
  Pallas kernels  29.9 us (47%)
  starting transfers between devices  21.5 us (33%)
  waiting for transfers between devices  7.6 us (12%)
  other arithmetic  4.74 us (7%)
    pallas_call x2, Pallas kernels, stack_bin(): pl.pallas_call(functools.partial(stack_kernel, (len(whole), len(lows), le...  27.9 us
    ppermute x19, starting transfers between devices, shift(): lax.ppermute(value, axis, [(at, (at + step) % size) for at in range(size)])  17.9 us
    ppermute x19, waiting for transfers between devices, shift(): lax.ppermute(value, axis, [(at, (at + step) % size) for at in range(size)])  7.59 us
    ppermute x3, starting transfers between devices, gather_direct(): blocks.append(lax.ppermute(sent, ('chip', 'win'), perm))  3.55 us
    concatenate x2, other arithmetic, gather_line(): return jnp.concatenate(line, axis=0)  2.28 us
    pallas_call x1, Pallas kernels, whiten(): pl.pallas_call(whiten_kernel, out_shape=[shape] * freqs, name='whiten')  2.07 us
    reduce_sum x1, other arithmetic, by_column(): jnp.sum(jnp.where(hit, values[None, :], 0), axis=1)  1.46 us
  transfers between devices with their start and end apart: 22, of which 7 were waited for; matrix products, arithmetic and copies ran while one was open for 6% of the time, Pallas kernels for 22%

profile of v6, /device:TPU:0, one launch (start us, length us, event | category | flops | bytes accessed | tf_op | source)
XLA Modules:
  0.0 63.9 jit_solution(17414973641683159742)
XLA Ops:
  0.0 2.1 %whiten.1 = (bf16[1,2,16384]{2,1,0:T(2,128)(2,1)}, bf16[1,2,16384]{2,1,0:T(2,128)(2,1)}) custom-call(f32[2,1,2,16384]{3,2,1,0:T(2,128)} %bitcast.3), custom_call_target="tpu_custom_call" | custom-call | tf_op jit(solution)/shard_map/whiten/pallas_call | solution.py:30
  2.1 5.0 %collective-permute-start.2 = (bf16[2,16384]{1,0:T(2,128)(2,1)}, bf16[2,16384]{1,0:T(2,128)(2,1)S(1)}, u32[]{:S(2)}, u32[]{:S(2)}) collective-permute-start(bf16[2,16384]{1,0:T(2,128)(2,1)} %bitcast.8), channel_id=1, source_target_pairs={{0,6},{2,0},{4,2},{6,4},{1,7},{3,1},{5,3},{7,5},{8,14},{10,8},{12,... | collective-permute-start | bytes 196616 | tf_op jit(solution)/shard_map/ppermute | solution.py:40
  7.1 1.0 %collective-permute-start = (bf16[2,16384]{1,0:T(2,128)(2,1)}, bf16[2,16384]{1,0:T(2,128)(2,1)S(1)}, u32[]{:S(2)}, u32[]{:S(2)}) collective-permute-start(bf16[2,16384]{1,0:T(2,128)(2,1)} %bitcast.10), channel_id=1, source_target_pairs={{0,2},{2,4},{4,6},{6,0},{1,3},{3,5},{5,7},{7,1},{8,10},{10,12},{12... | collective-permute-start | bytes 196616 | tf_op jit(solution)/shard_map/ppermute | solution.py:40
  8.1 0.7 %iota_add_fusion = s32[516]{0:T(1024)S(1)} fusion(s32[516]{0:T(1024)} %param.5), kind=kLoop, calls=%fused_computation.7 | loop fusion | flops 1032 | bytes 4128 | tf_op jit(solution)/shard_map/add | solution.py:66
  8.8 0.3 convert_reduce_fusion
  9.1 1.5 %select_reduce_fusion = (s32[516]{0:T(1024)S(1)}, s32[516]{0:T(1024)S(1)}, s32[516]{0:T(1024)S(1)}) fusion(s32[516]{0:T(1024)S(1)} %convert_reduce_fusion, s32[516]{0:T(1024)} %param.5, s32[516]{0:T(1024)} %param.4), kind=kLoop, calls=%fused_computation | loop fusion | flops 1862244 | bytes 12384 | tf_op jit(solution)/shard_map/reduce_sum | solution.py:71
  10.7 3.1 %collective-permute-done.1 = bf16[2,16384]{1,0:T(2,128)(2,1)S(1)} collective-permute-done((bf16[2,16384]{1,0:T(2,128)(2,1)}, bf16[2,16384]{1,0:T(2,128)(2,1)S(1)}, u32[]{:S(2)}, u32[]{:S(2)}) %collective-permute-start.1) | collective-permute-done | bytes 65568 | tf_op jit(solution)/shard_map/ppermute | solution.py:40
  13.8 1.1 %pad_maximum_fusion.refs_0_ = bf16[8,16384]{1,0:T(8,128)(2,1)S(1)} fusion(bf16[2,16384]{1,0:T(2,128)(2,1)S(1)} %collective-permute-done.2, bf16[2,16384]{1,0:T(2,128)(2,1)S(1)} %collective-permute-done.1, bf16[2,16384]{1,0:T(2,128)(2,1)S(1)} %collective-permute-done, bf16[2,16384]{1,0:T(2,128)(2,1)} %bitcast.11), kind=kLoop, calls=%fused_computation.5 | loop fusion | flops 1048576 | bytes 524288 | tf_op jit(solution)/shard_map/concatenate | solution.py:45
  15.0 1.6 %collective-permute-start.9 = (bf16[8,16384]{1,0:T(8,128)(2,1)S(1)}, bf16[8,16384]{1,0:T(8,128)(2,1)S(1)}, u32[]{:S(2)}, u32[]{:S(2)}) collective-permute-start(bf16[8,16384]{1,0:T(8,128)(2,1)S(1)} %pad_maximum_fusion.refs_0_), channel_id=1, source_target_pairs={{0,1},{1,0},{2,3},{3,2},{4,5},{5,4},{6,7},{7,6},{8,9},{9,8},{10,11... | collective-permute-start | bytes 786440 | tf_op jit(solution)/shard_map/ppermute | solution.py:40
  16.6 1.5 %collective-permute-start.8 = (bf16[8,16384]{1,0:T(8,128)(2,1)S(1)}, bf16[8,16384]{1,0:T(8,128)(2,1)S(1)}, u32[]{:S(2)}, u32[]{:S(2)}) collective-permute-start(bf16[8,16384]{1,0:T(8,128)(2,1)S(1)} %pad_maximum_fusion.refs_0_), channel_id=1, source_target_pairs={{0,16},{16,0},{1,17},{17,1},{2,18},{18,2},{3,19},{19,3},{4,20},{20... | collective-permute-start | bytes 786440 | tf_op jit(solution)/shard_map/ppermute | solution.py:40
  18.1 1.9 %collective-permute-start.6 = (bf16[2,16384]{1,0:T(2,128)(2,1)}, bf16[2,16384]{1,0:T(2,128)(2,1)S(1)}, u32[]{:S(2)}, u32[]{:S(2)}) collective-permute-start(bf16[2,16384]{1,0:T(2,128)(2,1)} %bitcast.4), channel_id=1, source_target_pairs={{0,6},{2,0},{4,2},{6,4},{1,7},{3,1},{5,3},{7,5},{8,14},{10,8},{12,... | collective-permute-start | bytes 196616 | tf_op jit(solution)/shard_map/ppermute | solution.py:40
  20.0 1.9 %collective-permute-start.4 = (bf16[2,16384]{1,0:T(2,128)(2,1)}, bf16[2,16384]{1,0:T(2,128)(2,1)S(1)}, u32[]{:S(2)}, u32[]{:S(2)}) collective-permute-start(bf16[2,16384]{1,0:T(2,128)(2,1)} %bitcast.6), channel_id=1, source_target_pairs={{0,2},{2,4},{4,6},{6,0},{1,3},{3,5},{5,7},{7,1},{8,10},{10,12},{12... | collective-permute-start | bytes 196616 | tf_op jit(solution)/shard_map/ppermute | solution.py:40
  21.9 1.8 %collective-permute-done.9.refs_3_ = bf16[8,16384]{1,0:T(8,128)(2,1)S(1)} collective-permute-done((bf16[8,16384]{1,0:T(8,128)(2,1)S(1)}, bf16[8,16384]{1,0:T(8,128)(2,1)S(1)}, u32[]{:S(2)}, u32[]{:S(2)}) %collective-permute-start.9) | collective-permute-done | bytes 262176 | tf_op jit(solution)/shard_map/ppermute | solution.py:40
  23.8 1.6 %collective-permute-start.12 = (bf16[8,8192]{1,0:T(8,128)(2,1)S(1)}, bf16[8,8192]{1,0:T(8,128)(2,1)S(1)}, u32[]{:S(2)}, u32[]{:S(2)}) collective-permute-start(bf16[8,8192]{1,0:T(8,128)(2,1)S(1)} %slice.8), channel_id=1, source_target_pairs={{0,16},{16,0},{1,17},{17,1},{2,18},{18,2},{3,19},{19,3},{4,20},{20... | collective-permute-start | bytes 393224 | tf_op jit(solution)/shard_map/ppermute | solution.py:40
  25.3 1.6 %collective-permute-start.13 = (bf16[8,8192]{1,0:T(8,128)(2,1)S(1)}, bf16[8,8192]{1,0:T(8,128)(2,1)S(1)}, u32[]{:S(2)}, u32[]{:S(2)}) collective-permute-start(bf16[8,8192]{1,0:T(8,128)(2,1)S(1)} %slice.9), channel_id=1, source_target_pairs={{0,1},{1,0},{2,3},{3,2},{4,5},{5,4},{6,7},{7,6},{8,9},{9,8},{10,11... | collective-permute-start | bytes 393224 | tf_op jit(solution)/shard_map/ppermute | solution.py:40
  26.9 0.3 collective-permute-done.5
  27.2 0.2 collective-permute-start.15
  27.4 1.1 %pad_maximum_fusion.1.refs_0_ = bf16[8,16384]{1,0:T(8,128)(2,1)S(1)} fusion(bf16[2,16384]{1,0:T(2,128)(2,1)S(1)} %collective-permute-done.6, bf16[2,16384]{1,0:T(2,128)(2,1)S(1)} %collective-permute-done.5, bf16[2,16384]{1,0:T(2,128)(2,1)S(1)} %collective-permute-done.4, bf16[2,16384]{1,0:T(2,128)(2,1)} %bitcast.7), kind=kLoop, calls=%fused_computation.6 | loop fusion | flops 1048576 | bytes 524288 | tf_op jit(solution)/shard_map/concatenate | solution.py:45
  28.6 0.6 collective-permute-start.11
  29.2 1.2 %collective-permute-start.10 = (bf16[8,16384]{1,0:T(8,128)(2,1)S(1)}, bf16[8,16384]{1,0:T(8,128)(2,1)S(1)}, u32[]{:S(2)}, u32[]{:S(2)}) collective-permute-start(bf16[8,16384]{1,0:T(8,128)(2,1)S(1)} %pad_maximum_fusion.1.refs_0_), channel_id=1, source_target_pairs={{0,16},{1,17},{16,0},{17,1},{2,18},{3,19},{18,2},{19,3},{4,20},{5,... | collective-permute-start | bytes 786440 | tf_op jit(solution)/shard_map/ppermute | solution.py:59
  30.4 1.8 %collective-permute-start.14 = (bf16[8,16384]{1,0:T(8,128)(2,1)S(1)}, bf16[8,16384]{1,0:T(8,128)(2,1)S(1)}, u32[]{:S(2)}, u32[]{:S(2)}) collective-permute-start(bf16[8,16384]{1,0:T(8,128)(2,1)S(1)} %pad_maximum_fusion.1.refs_0_), channel_id=1, source_target_pairs={{0,17},{1,16},{16,1},{17,0},{2,19},{3,18},{18,3},{19,2},{4,21},{5,... | collective-permute-start | bytes 786440 | tf_op jit(solution)/shard_map/ppermute | solution.py:59
  32.2 0.5 collective-permute-start.18
  32.7 0.8 %collective-permute-done.17.refs_7_ = bf16[8,8192]{1,0:T(8,128)(2,1)S(1)} collective-permute-done((bf16[8,8192]{1,0:T(8,128)(2,1)S(1)}, bf16[8,8192]{1,0:T(8,128)(2,1)S(1)}, u32[]{:S(2)}, u32[]{:S(2)}) %collective-permute-start.17) | collective-permute-done | bytes 131104 | tf_op jit(solution)/shard_map/ppermute | solution.py:40
  33.5 0.1 collective-permute-start.7
  33.7 14.0 %stack.2.refs_8_ = f32[516,2,2,64,128]{4,3,2,1,0:T(8,128)} custom-call(s32[1548]{0:T(1024)S(1)} %concatenate.10.lists_hbm, bf16[8,16384]{1,0:T(8,128)(2,1)S(1)} %pad_maximum_fusion.refs_0_, bf16[8,16384]{1,0:T(8,128)(2,1)S(1)} %collective-permute-done.3.refs_1_, bf16[8,16384]{1,0:T(8,128)(2,1)S(1)} %collective-permute-done.8.refs_2_, ...), custom_call_target="tpu_custom_call" | custom-call | tf_op jit(solution)/shard_map/stack/pallas_call | solution.py:268
  47.7 0.4 collective-permute-start.19
  48.1 0.2 collective-permute-start.20
  48.3 0.3 collective-permute-start.21
  48.6 0.7 %collective-permute-done.19.refs_5_ = bf16[8,16384]{1,0:T(8,128)(2,1)S(1)} collective-permute-done((bf16[8,16384]{1,0:T(8,128)(2,1)S(1)}, bf16[8,16384]{1,0:T(8,128)(2,1)S(1)}, u32[]{:S(2)}, u32[]{:S(2)}) %collective-permute-start.19) | collective-permute-done | bytes 262176 | tf_op jit(solution)/shard_map/ppermute | solution.py:40
  49.3 0.4 collective-permute-done.20.refs_6_
  49.7 0.4 collective-permute-done.21.refs_7_
  50.1 13.9 %stack.3 = f32[516,2,2,64,128]{4,3,2,1,0:T(8,128)} custom-call(s32[1548]{0:T(1024)S(1)} %concatenate.10.lists_hbm, bf16[8,16384]{1,0:T(8,128)(2,1)S(1)} %pad_maximum_fusion.1.refs_0_, bf16[8,16384]{1,0:T(8,128)(2,1)S(1)} %collective-permute-done.7.refs_1_, bf16[8,16384]{1,0:T(8,128)(2,1)S(1)} %collective-permute-done.10.refs_2_, ...), custom_call_target="tpu_custom_call", output_to_operand_aliasing={{}: (9, {})} | custom-call | tf_op jit(solution)/shard_map/stack/pallas_call | solution.py:268
  (23 shorter events, 0.3 us)
Async XLA Ops:
  2.1 8.6 %collective-permute-start.2 = (bf16[2,16384]{1,0:T(2,128)(2,1)}, bf16[2,16384]{1,0:T(2,128)(2,1)S(1)}, u32[]{:S(2)}, u32[]{:S(2)}) collective-permute-start(bf16[2,16384]{1,0:T(2,128)(2,1)} %bitcast.8), channel_id=1, source_target_pairs={{0,6},{2,0},{4,2},{6,4},{1,7},{3,1},{5,3},{7,5},{8,14},{10,8},{12,... | collective-permute-start | bytes 196616 | tf_op jit(solution)/shard_map/ppermute | solution.py:40
  7.1 6.7 %collective-permute-start.1 = (bf16[2,16384]{1,0:T(2,128)(2,1)}, bf16[2,16384]{1,0:T(2,128)(2,1)S(1)}, u32[]{:S(2)}, u32[]{:S(2)}) collective-permute-start(bf16[2,16384]{1,0:T(2,128)(2,1)} %bitcast.9), channel_id=1, source_target_pairs={{0,4},{2,6},{4,0},{6,2},{1,5},{3,7},{5,1},{7,3},{8,12},{10,14},{12... | collective-permute-start | bytes 196616 | tf_op jit(solution)/shard_map/ppermute | solution.py:40
  7.1 6.7 %collective-permute-start = (bf16[2,16384]{1,0:T(2,128)(2,1)}, bf16[2,16384]{1,0:T(2,128)(2,1)S(1)}, u32[]{:S(2)}, u32[]{:S(2)}) collective-permute-start(bf16[2,16384]{1,0:T(2,128)(2,1)} %bitcast.10), channel_id=1, source_target_pairs={{0,2},{2,4},{4,6},{6,0},{1,3},{3,5},{5,7},{7,1},{8,10},{10,12},{12... | collective-permute-start | bytes 196616 | tf_op jit(solution)/shard_map/ppermute | solution.py:40
  14.9 3.2 %collective-permute-start.3 = (bf16[8,16384]{1,0:T(8,128)(2,1)S(1)}, bf16[8,16384]{1,0:T(8,128)(2,1)S(1)}, u32[]{:S(2)}, u32[]{:S(2)}) collective-permute-start(bf16[8,16384]{1,0:T(8,128)(2,1)S(1)} %pad_maximum_fusion.refs_0_), channel_id=1, source_target_pairs={{0,8},{8,0},{1,9},{9,1},{2,10},{10,2},{3,11},{11,3},{4,12},{12,4},... | collective-permute-start | bytes 786440 | tf_op jit(solution)/shard_map/ppermute | solution.py:40
  15.0 8.7 %collective-permute-start.9 = (bf16[8,16384]{1,0:T(8,128)(2,1)S(1)}, bf16[8,16384]{1,0:T(8,128)(2,1)S(1)}, u32[]{:S(2)}, u32[]{:S(2)}) collective-permute-start(bf16[8,16384]{1,0:T(8,128)(2,1)S(1)} %pad_maximum_fusion.refs_0_), channel_id=1, source_target_pairs={{0,1},{1,0},{2,3},{3,2},{4,5},{5,4},{6,7},{7,6},{8,9},{9,8},{10,11... | collective-permute-start | bytes 786440 | tf_op jit(solution)/shard_map/ppermute | solution.py:40
  16.6 8.7 %collective-permute-start.8 = (bf16[8,16384]{1,0:T(8,128)(2,1)S(1)}, bf16[8,16384]{1,0:T(8,128)(2,1)S(1)}, u32[]{:S(2)}, u32[]{:S(2)}) collective-permute-start(bf16[8,16384]{1,0:T(8,128)(2,1)S(1)} %pad_maximum_fusion.refs_0_), channel_id=1, source_target_pairs={{0,16},{16,0},{1,17},{17,1},{2,18},{18,2},{3,19},{19,3},{4,20},{20... | collective-permute-start | bytes 786440 | tf_op jit(solution)/shard_map/ppermute | solution.py:40
  18.1 8.8 %collective-permute-start.6 = (bf16[2,16384]{1,0:T(2,128)(2,1)}, bf16[2,16384]{1,0:T(2,128)(2,1)S(1)}, u32[]{:S(2)}, u32[]{:S(2)}) collective-permute-start(bf16[2,16384]{1,0:T(2,128)(2,1)} %bitcast.4), channel_id=1, source_target_pairs={{0,6},{2,0},{4,2},{6,4},{1,7},{3,1},{5,3},{7,5},{8,14},{10,8},{12,... | collective-permute-start | bytes 196616 | tf_op jit(solution)/shard_map/ppermute | solution.py:40
  20.0 7.2 %collective-permute-start.5 = (bf16[2,16384]{1,0:T(2,128)(2,1)}, bf16[2,16384]{1,0:T(2,128)(2,1)S(1)}, u32[]{:S(2)}, u32[]{:S(2)}) collective-permute-start(bf16[2,16384]{1,0:T(2,128)(2,1)} %bitcast.5), channel_id=1, source_target_pairs={{0,4},{2,6},{4,0},{6,2},{1,5},{3,7},{5,1},{7,3},{8,12},{10,14},{12... | collective-permute-start | bytes 196616 | tf_op jit(solution)/shard_map/ppermute | solution.py:40
  20.0 7.4 %collective-permute-start.4 = (bf16[2,16384]{1,0:T(2,128)(2,1)}, bf16[2,16384]{1,0:T(2,128)(2,1)S(1)}, u32[]{:S(2)}, u32[]{:S(2)}) collective-permute-start(bf16[2,16384]{1,0:T(2,128)(2,1)} %bitcast.6), channel_id=1, source_target_pairs={{0,2},{2,4},{4,6},{6,0},{1,3},{3,5},{5,7},{7,1},{8,10},{10,12},{12... | collective-permute-start | bytes 196616 | tf_op jit(solution)/shard_map/ppermute | solution.py:40
  23.8 5.4 %collective-permute-start.12 = (bf16[8,8192]{1,0:T(8,128)(2,1)S(1)}, bf16[8,8192]{1,0:T(8,128)(2,1)S(1)}, u32[]{:S(2)}, u32[]{:S(2)}) collective-permute-start(bf16[8,8192]{1,0:T(8,128)(2,1)S(1)} %slice.8), channel_id=1, source_target_pairs={{0,16},{16,0},{1,17},{17,1},{2,18},{18,2},{3,19},{19,3},{4,20},{20... | collective-permute-start | bytes 393224 | tf_op jit(solution)/shard_map/ppermute | solution.py:40
  25.3 5.0 %collective-permute-start.13 = (bf16[8,8192]{1,0:T(8,128)(2,1)S(1)}, bf16[8,8192]{1,0:T(8,128)(2,1)S(1)}, u32[]{:S(2)}, u32[]{:S(2)}) collective-permute-start(bf16[8,8192]{1,0:T(8,128)(2,1)S(1)} %slice.9), channel_id=1, source_target_pairs={{0,1},{1,0},{2,3},{3,2},{4,5},{5,4},{6,7},{7,6},{8,9},{9,8},{10,11... | collective-permute-start | bytes 393224 | tf_op jit(solution)/shard_map/ppermute | solution.py:40
  26.9 5.2 %collective-permute-start.16 = (bf16[8,16384]{1,0:T(8,128)(2,1)S(1)}, bf16[8,16384]{1,0:T(8,128)(2,1)S(1)}, u32[]{:S(2)}, u32[]{:S(2)}) collective-permute-start(bf16[8,16384]{1,0:T(8,128)(2,1)S(1)} %collective-permute-done.9.refs_3_), channel_id=1, source_target_pairs={{0,8},{8,0},{1,9},{9,1},{2,10},{10,2},{3,11},{11,3},{4,12},{12,4},... | collective-permute-start | bytes 786440 | tf_op jit(solution)/shard_map/ppermute | solution.py:40
  27.2 5.0 %collective-permute-start.15 = (bf16[8,16384]{1,0:T(8,128)(2,1)S(1)}, bf16[8,16384]{1,0:T(8,128)(2,1)S(1)}, u32[]{:S(2)}, u32[]{:S(2)}) collective-permute-start(bf16[8,16384]{1,0:T(8,128)(2,1)S(1)} %collective-permute-done.8.refs_2_), channel_id=1, source_target_pairs={{0,8},{8,0},{1,9},{9,1},{2,10},{10,2},{3,11},{11,3},{4,12},{12,4},... | collective-permute-start | bytes 786440 | tf_op jit(solution)/shard_map/ppermute | solution.py:40
  28.6 19.1 %collective-permute-start.11 = (bf16[8,16384]{1,0:T(8,128)(2,1)S(1)}, bf16[8,16384]{1,0:T(8,128)(2,1)S(1)}, u32[]{:S(2)}, u32[]{:S(2)}) collective-permute-start(bf16[8,16384]{1,0:T(8,128)(2,1)S(1)} %pad_maximum_fusion.1.refs_0_), channel_id=1, source_target_pairs={{0,1},{1,0},{16,17},{17,16},{2,3},{3,2},{18,19},{19,18},{4,5},{5,4... | collective-permute-start | bytes 786440 | tf_op jit(solution)/shard_map/ppermute | solution.py:59
  29.2 18.5 %collective-permute-start.10 = (bf16[8,16384]{1,0:T(8,128)(2,1)S(1)}, bf16[8,16384]{1,0:T(8,128)(2,1)S(1)}, u32[]{:S(2)}, u32[]{:S(2)}) collective-permute-start(bf16[8,16384]{1,0:T(8,128)(2,1)S(1)} %pad_maximum_fusion.1.refs_0_), channel_id=1, source_target_pairs={{0,16},{1,17},{16,0},{17,1},{2,18},{3,19},{18,2},{19,3},{4,20},{5,... | collective-permute-start | bytes 786440 | tf_op jit(solution)/shard_map/ppermute | solution.py:59
  30.4 17.3 %collective-permute-start.14 = (bf16[8,16384]{1,0:T(8,128)(2,1)S(1)}, bf16[8,16384]{1,0:T(8,128)(2,1)S(1)}, u32[]{:S(2)}, u32[]{:S(2)}) collective-permute-start(bf16[8,16384]{1,0:T(8,128)(2,1)S(1)} %pad_maximum_fusion.1.refs_0_), channel_id=1, source_target_pairs={{0,17},{1,16},{16,1},{17,0},{2,19},{3,18},{18,3},{19,2},{4,21},{5,... | collective-permute-start | bytes 786440 | tf_op jit(solution)/shard_map/ppermute | solution.py:59
  32.1 1.3 %collective-permute-start.17 = (bf16[8,8192]{1,0:T(8,128)(2,1)S(1)}, bf16[8,8192]{1,0:T(8,128)(2,1)S(1)}, u32[]{:S(2)}, u32[]{:S(2)}) collective-permute-start(bf16[8,8192]{1,0:T(8,128)(2,1)S(1)} %collective-permute-done.12.refs_6_), channel_id=1, source_target_pairs={{0,8},{8,0},{1,9},{9,1},{2,10},{10,2},{3,11},{11,3},{4,12},{12,4},... | collective-permute-start | bytes 393224 | tf_op jit(solution)/shard_map/ppermute | solution.py:40
  32.2 1.5 %collective-permute-start.18 = (bf16[8,8192]{1,0:T(8,128)(2,1)S(1)}, bf16[8,8192]{1,0:T(8,128)(2,1)S(1)}, u32[]{:S(2)}, u32[]{:S(2)}) collective-permute-start(bf16[8,8192]{1,0:T(8,128)(2,1)S(1)} %collective-permute-done.13.refs_8_), channel_id=1, source_target_pairs={{0,8},{8,0},{1,9},{9,1},{2,10},{10,2},{3,11},{11,3},{4,12},{12,4},... | collective-permute-start | bytes 393224 | tf_op jit(solution)/shard_map/ppermute | solution.py:40
  33.5 15.1 %collective-permute-start.7 = (bf16[8,16384]{1,0:T(8,128)(2,1)S(1)}, bf16[8,16384]{1,0:T(8,128)(2,1)S(1)}, u32[]{:S(2)}, u32[]{:S(2)}) collective-permute-start(bf16[8,16384]{1,0:T(8,128)(2,1)S(1)} %pad_maximum_fusion.1.refs_0_), channel_id=1, source_target_pairs={{0,8},{8,0},{1,9},{9,1},{2,10},{10,2},{3,11},{11,3},{4,12},{12,4},... | collective-permute-start | bytes 786440 | tf_op jit(solution)/shard_map/ppermute | solution.py:40
  47.7 1.6 %collective-permute-start.19 = (bf16[8,16384]{1,0:T(8,128)(2,1)S(1)}, bf16[8,16384]{1,0:T(8,128)(2,1)S(1)}, u32[]{:S(2)}, u32[]{:S(2)}) collective-permute-start(bf16[8,16384]{1,0:T(8,128)(2,1)S(1)} %collective-permute-done.10.refs_2_), channel_id=1, source_target_pairs={{0,8},{8,0},{1,9},{9,1},{2,10},{10,2},{3,11},{11,3},{4,12},{12,4},... | collective-permute-start | bytes 786440 | tf_op jit(solution)/shard_map/ppermute | solution.py:40
  48.1 1.6 %collective-permute-start.20 = (bf16[8,16384]{1,0:T(8,128)(2,1)S(1)}, bf16[8,16384]{1,0:T(8,128)(2,1)S(1)}, u32[]{:S(2)}, u32[]{:S(2)}) collective-permute-start(bf16[8,16384]{1,0:T(8,128)(2,1)S(1)} %collective-permute-done.11.refs_3_), channel_id=1, source_target_pairs={{0,8},{8,0},{1,9},{9,1},{2,10},{10,2},{3,11},{11,3},{4,12},{12,4},... | collective-permute-start | bytes 786440 | tf_op jit(solution)/shard_map/ppermute | solution.py:40
  48.3 1.8 %collective-permute-start.21 = (bf16[8,16384]{1,0:T(8,128)(2,1)S(1)}, bf16[8,16384]{1,0:T(8,128)(2,1)S(1)}, u32[]{:S(2)}, u32[]{:S(2)}) collective-permute-start(bf16[8,16384]{1,0:T(8,128)(2,1)S(1)} %collective-permute-done.14.refs_4_), channel_id=1, source_target_pairs={{0,8},{8,0},{1,9},{9,1},{2,10},{10,2},{3,11},{11,3},{4,12},{12,4},... | collective-permute-start | bytes 786440 | tf_op jit(solution)/shard_map/ppermute | solution.py:40

commit v7 on v6

--- a/solution.py
+++ b/solution.py
@@ -16,9 +16,9 @@
     freqs = spectra_ref.shape[0]
     power = None
     for freq in range(freqs):
-        slab = spectra_ref[freq]
-        term = jnp.sum(slab * slab, axis=1, keepdims=True)
-        power = term if power is None else power + term
+        for part in range(2):
+            row = spectra_ref[freq, :, part : part + 1, :]
+            power = row * row if power is None else power + row * row
     factor = jnp.minimum(lax.rsqrt(power / freqs), 1.0)
     for freq in range(freqs):
         out_refs[freq][...] = (spectra_ref[freq] * factor).astype(jnp.bfloat16)
@@ -40,9 +40,20 @@
     return lax.ppermute(value, axis, [(at, (at + step) % size) for at in range(size)])
 
 
-def gather_line(own):
+def join_kernel(*refs):
+    refs[-1][...] = jnp.concatenate([ref[...] for ref in refs[:-1]], axis=0)
+
+
+def gather_line(own, first):
     line = [own] + [shift(own, "col", step) for step in range(1, lax.axis_size("col"))]
-    return jnp.concatenate(line, axis=0)
+    if not first:
+        return jnp.concatenate(line, axis=0)
+    shape = (len(line) * own.shape[0], own.shape[1])
+    return pl.pallas_call(
+        join_kernel,
+        out_shape=jax.ShapeDtypeStruct(shape, own.dtype),
+        name="join",
+    )(*line)
 
 
 def gather_direct(block, near, far):
@@ -292,7 +303,7 @@
     )
     lists = by_column(tile_rows, tile_cols)
     slabs = whiten(spectra[0])
-    block = gather_line(slabs[0])
+    block = gather_line(slabs[0], True)
     block, lists = lax.optimization_barrier((block, lists))
     swapped = swap_cores([block])
     arrived, lows, highs = gather_relayed(block)
@@ -302,7 +313,7 @@
     highs = highs + swap_cores(highs)
     later = []
     for own in slabs[1:]:
-        block = gather_line(after(own, *swapped))
+        block = gather_line(after(own, *swapped), False)
         swapped = swap_cores([block])
         arrived = gather_direct(block, near, far)
         near, far = arrived, arrived

time: 64.3 us -> 67 us (1.042)
  local copies, waits for them, and re-layouts: 0.1 us -> 2.29 us
  Pallas kernels: 29.9 us -> 31.4 us
  other arithmetic: 4.74 us -> 3.6 us
  waiting for transfers between devices: 7.6 us -> 8.31 us
    unnamed x0 -> x8, local copies, waits for them, and re-layouts: none -> 2.19 us
    pallas_call x0 -> x1, Pallas kernels: none -> 1.81 us  [gather_line(): pl.pallas_call(join_kernel, out_shape=jax.ShapeDtypeStruct(shape, own.dty...]
    concatenate x2 -> x1, other arithmetic: 2.28 us -> 1.14 us  [gather_line(): return jnp.concatenate(line, axis=0)]
    ppermute x19, waiting for transfers between devices: 7.59 us -> 8.31 us  [shift(): lax.ppermute(value, axis, [(at, (at + step) % size) for at in range(size)])]
  transfers between devices with their start and end apart: 22 -> 22, of which waited for: 7 -> 7; matrix products, arithmetic and copies ran while one was open for 6% -> 6% of each run, Pallas kernels for 22% -> 21%
where the time goes in v7:
time: 67 us; the launch traced here: 66.6 us
  Pallas kernels  31.4 us (47%)
  starting transfers between devices  20.9 us (31%)
  waiting for transfers between devices  8.31 us (12%)
  other arithmetic  3.6 us (5%)
  local copies, waits for them, and re-layouts  2.29 us (3%)
    pallas_call x2, Pallas kernels, stack_bin(): pl.pallas_call(functools.partial(stack_kernel, (len(whole), len(lows), le...  27.9 us
    ppermute x19, starting transfers between devices, shift(): lax.ppermute(value, axis, [(at, (at + step) % size) for at in range(size)])  17.4 us
    ppermute x19, waiting for transfers between devices, shift(): lax.ppermute(value, axis, [(at, (at + step) % size) for at in range(size)])  8.31 us
    ppermute x3, starting transfers between devices, gather_direct(): blocks.append(lax.ppermute(sent, ('chip', 'win'), perm))  3.55 us
    unnamed x8, local copies, waits for them, and re-layouts  2.19 us
    pallas_call x1, Pallas kernels, gather_line(): pl.pallas_call(join_kernel, out_shape=jax.ShapeDtypeStruct(shape, own.dty...  1.81 us
    pallas_call x1, Pallas kernels, whiten(): pl.pallas_call(whiten_kernel, out_shape=[shape] * freqs, name='whiten')  1.74 us
    reduce_sum x1, other arithmetic, by_column(): jnp.sum(jnp.where(hit, values[None, :], 0), axis=1)  1.46 us
  transfers between devices with their start and end apart: 22, of which 7 were waited for; matrix products, arithmetic and copies ran while one was open for 6% of the time, Pallas kernels for 21%

profile of v7, /device:TPU:0, one launch (start us, length us, event | category | flops | bytes accessed | tf_op | source)
XLA Modules:
  0.0 66.6 jit_solution(2072140527488707136)
XLA Ops:
  0.0 1.7 %whiten.1 = (bf16[1,2,16384]{2,1,0:T(2,128)(2,1)}, bf16[1,2,16384]{2,1,0:T(2,128)(2,1)}) custom-call(f32[2,1,2,16384]{3,2,1,0:T(2,128)} %bitcast.3), custom_call_target="tpu_custom_call" | custom-call | tf_op jit(solution)/shard_map/whiten/pallas_call | solution.py:30
  1.7 5.0 %collective-permute-start.2 = (bf16[2,16384]{1,0:T(2,128)(2,1)}, bf16[2,16384]{1,0:T(2,128)(2,1)S(1)}, u32[]{:S(2)}, u32[]{:S(2)}) collective-permute-start(bf16[2,16384]{1,0:T(2,128)(2,1)} %bitcast.8), channel_id=1, source_target_pairs={{0,6},{2,0},{4,2},{6,4},{1,7},{3,1},{5,3},{7,5},{8,14},{10,8},{12,... | collective-permute-start | bytes 196616 | tf_op jit(solution)/shard_map/ppermute | solution.py:40
  6.8 1.0 %collective-permute-start = (bf16[2,16384]{1,0:T(2,128)(2,1)}, bf16[2,16384]{1,0:T(2,128)(2,1)S(1)}, u32[]{:S(2)}, u32[]{:S(2)}) collective-permute-start(bf16[2,16384]{1,0:T(2,128)(2,1)} %bitcast.10), channel_id=1, source_target_pairs={{0,2},{2,4},{4,6},{6,0},{1,3},{3,5},{5,7},{7,1},{8,10},{10,12},{12... | collective-permute-start | bytes 196616 | tf_op jit(solution)/shard_map/ppermute | solution.py:40
  7.8 0.7 %iota_add_fusion = s32[516]{0:T(1024)S(1)} fusion(s32[516]{0:T(1024)} %param.5), kind=kLoop, calls=%fused_computation.6 | loop fusion | flops 1032 | bytes 4128 | tf_op jit(solution)/shard_map/add | solution.py:77
  8.5 0.3 convert_reduce_fusion
  8.8 1.5 %select_reduce_fusion = (s32[516]{0:T(1024)S(1)}, s32[516]{0:T(1024)S(1)}, s32[516]{0:T(1024)S(1)}) fusion(s32[516]{0:T(1024)S(1)} %convert_reduce_fusion, s32[516]{0:T(1024)} %param.5, s32[516]{0:T(1024)} %param.4), kind=kLoop, calls=%fused_computation | loop fusion | flops 1862244 | bytes 12384 | tf_op jit(solution)/shard_map/reduce_sum | solution.py:82
  10.4 3.1 %collective-permute-done.1.refs_2_ = bf16[2,16384]{1,0:T(2,128)(2,1)S(1)} collective-permute-done((bf16[2,16384]{1,0:T(2,128)(2,1)}, bf16[2,16384]{1,0:T(2,128)(2,1)S(1)}, u32[]{:S(2)}, u32[]{:S(2)}) %collective-permute-start.1) | collective-permute-done | bytes 65568 | tf_op jit(solution)/shard_map/ppermute | solution.py:40
  13.5 0.6 copy-done.2
  14.1 0.6 copy-done.3
  14.7 1.8 %join.1.refs_0_ = bf16[8,16384]{1,0:T(8,128)(2,1)} custom-call(bf16[2,16384]{1,0:T(2,128)(2,1)} %bitcast.11, bf16[2,16384]{1,0:T(2,128)(2,1)} %copy-done.3, bf16[2,16384]{1,0:T(2,128)(2,1)} %copy-done.2, bf16[2,16384]{1,0:T(2,128)(2,1)} %copy-done.1), custom_call_target="tpu_custom_call" | custom-call | tf_op jit(solution)/shard_map/join/pallas_call | solution.py:52
  16.5 1.5 %collective-permute-start.9 = (bf16[8,16384]{1,0:T(8,128)(2,1)}, bf16[8,16384]{1,0:T(8,128)(2,1)S(1)}, u32[]{:S(2)}, u32[]{:S(2)}) collective-permute-start(bf16[8,16384]{1,0:T(8,128)(2,1)} %join.1.refs_0_), channel_id=1, source_target_pairs={{0,1},{1,0},{2,3},{3,2},{4,5},{5,4},{6,7},{7,6},{8,9},{9,8},{10,11... | collective-permute-start | bytes 786440 | tf_op jit(solution)/shard_map/ppermute | solution.py:40
  18.1 1.5 %collective-permute-start.8 = (bf16[8,16384]{1,0:T(8,128)(2,1)}, bf16[8,16384]{1,0:T(8,128)(2,1)S(1)}, u32[]{:S(2)}, u32[]{:S(2)}) collective-permute-start(bf16[8,16384]{1,0:T(8,128)(2,1)} %join.1.refs_0_), channel_id=1, source_target_pairs={{0,16},{16,0},{1,17},{17,1},{2,18},{18,2},{3,19},{19,3},{4,20},{20... | collective-permute-start | bytes 786440 | tf_op jit(solution)/shard_map/ppermute | solution.py:40
  19.5 1.9 %collective-permute-start.6 = (bf16[2,16384]{1,0:T(2,128)(2,1)}, bf16[2,16384]{1,0:T(2,128)(2,1)S(1)}, u32[]{:S(2)}, u32[]{:S(2)}) collective-permute-start(bf16[2,16384]{1,0:T(2,128)(2,1)} %bitcast.4), channel_id=1, source_target_pairs={{0,6},{2,0},{4,2},{6,4},{1,7},{3,1},{5,3},{7,5},{8,14},{10,8},{12,... | collective-permute-start | bytes 196616 | tf_op jit(solution)/shard_map/ppermute | solution.py:40
  21.4 1.3 %collective-permute-start.4 = (bf16[2,16384]{1,0:T(2,128)(2,1)}, bf16[2,16384]{1,0:T(2,128)(2,1)S(1)}, u32[]{:S(2)}, u32[]{:S(2)}) collective-permute-start(bf16[2,16384]{1,0:T(2,128)(2,1)} %bitcast.6), channel_id=1, source_target_pairs={{0,2},{2,4},{4,6},{6,0},{1,3},{3,5},{5,7},{7,1},{8,10},{10,12},{12... | collective-permute-start | bytes 196616 | tf_op jit(solution)/shard_map/ppermute | solution.py:40
  22.7 2.7 %collective-permute-done.9.refs_3_ = bf16[8,16384]{1,0:T(8,128)(2,1)S(1)} collective-permute-done((bf16[8,16384]{1,0:T(8,128)(2,1)}, bf16[8,16384]{1,0:T(8,128)(2,1)S(1)}, u32[]{:S(2)}, u32[]{:S(2)}) %collective-permute-start.9) | collective-permute-done | bytes 262176 | tf_op jit(solution)/shard_map/ppermute | solution.py:40
  25.5 1.6 %collective-permute-start.12 = (bf16[8,8192]{1,0:T(8,128)(2,1)S(1)}, bf16[8,8192]{1,0:T(8,128)(2,1)S(1)}, u32[]{:S(2)}, u32[]{:S(2)}) collective-permute-start(bf16[8,8192]{1,0:T(8,128)(2,1)S(1)} %slice.8), channel_id=1, source_target_pairs={{0,16},{16,0},{1,17},{17,1},{2,18},{18,2},{3,19},{19,3},{4,20},{20... | collective-permute-start | bytes 393224 | tf_op jit(solution)/shard_map/ppermute | solution.py:40
  27.1 1.6 %collective-permute-start.13 = (bf16[8,8192]{1,0:T(8,128)(2,1)S(1)}, bf16[8,8192]{1,0:T(8,128)(2,1)S(1)}, u32[]{:S(2)}, u32[]{:S(2)}) collective-permute-start(bf16[8,8192]{1,0:T(8,128)(2,1)S(1)} %slice.9), channel_id=1, source_target_pairs={{0,1},{1,0},{2,3},{3,2},{4,5},{5,4},{6,7},{7,6},{8,9},{9,8},{10,11... | collective-permute-start | bytes 393224 | tf_op jit(solution)/shard_map/ppermute | solution.py:40
  28.8 0.4 collective-permute-start.15
  29.2 1.1 %pad_maximum_fusion.refs_0_ = bf16[8,16384]{1,0:T(8,128)(2,1)S(1)} fusion(bf16[2,16384]{1,0:T(2,128)(2,1)S(1)} %collective-permute-done.6, bf16[2,16384]{1,0:T(2,128)(2,1)S(1)} %collective-permute-done.5, bf16[2,16384]{1,0:T(2,128)(2,1)S(1)} %collective-permute-done.4, bf16[2,16384]{1,0:T(2,128)(2,1)} %bitcast.7), kind=kLoop, calls=%fused_computation.5 | loop fusion | flops 1048576 | bytes 524288 | tf_op jit(solution)/shard_map/concatenate | solution.py:50
  30.3 0.6 collective-permute-start.11
  30.9 1.3 %collective-permute-start.10 = (bf16[8,16384]{1,0:T(8,128)(2,1)S(1)}, bf16[8,16384]{1,0:T(8,128)(2,1)S(1)}, u32[]{:S(2)}, u32[]{:S(2)}) collective-permute-start(bf16[8,16384]{1,0:T(8,128)(2,1)S(1)} %pad_maximum_fusion.refs_0_), channel_id=1, source_target_pairs={{0,16},{1,17},{16,0},{17,1},{2,18},{3,19},{18,2},{19,3},{4,20},{5,... | collective-permute-start | bytes 786440 | tf_op jit(solution)/shard_map/ppermute | solution.py:70
  32.2 1.7 %collective-permute-start.14 = (bf16[8,16384]{1,0:T(8,128)(2,1)S(1)}, bf16[8,16384]{1,0:T(8,128)(2,1)S(1)}, u32[]{:S(2)}, u32[]{:S(2)}) collective-permute-start(bf16[8,16384]{1,0:T(8,128)(2,1)S(1)} %pad_maximum_fusion.refs_0_), channel_id=1, source_target_pairs={{0,17},{1,16},{16,1},{17,0},{2,19},{3,18},{18,3},{19,2},{4,21},{5,... | collective-permute-start | bytes 786440 | tf_op jit(solution)/shard_map/ppermute | solution.py:70
  33.9 0.5 collective-permute-start.18
  34.4 0.8 %collective-permute-done.17.refs_7_ = bf16[8,8192]{1,0:T(8,128)(2,1)S(1)} collective-permute-done((bf16[8,8192]{1,0:T(8,128)(2,1)S(1)}, bf16[8,8192]{1,0:T(8,128)(2,1)S(1)}, u32[]{:S(2)}, u32[]{:S(2)}) %collective-permute-start.17) | collective-permute-done | bytes 131104 | tf_op jit(solution)/shard_map/ppermute | solution.py:40
  35.4 0.9 %copy-done = bf16[8,16384]{1,0:T(8,128)(2,1)S(1)} copy-done((bf16[8,16384]{1,0:T(8,128)(2,1)S(1)}, bf16[8,16384]{1,0:T(8,128)(2,1)}, u32[]{:S(2)}) %copy-start) | copy-done | bytes 262168
  36.4 14.0 %stack.2.refs_8_ = f32[516,2,2,64,128]{4,3,2,1,0:T(8,128)} custom-call(s32[1548]{0:T(1024)S(1)} %concatenate.6.lists_hbm, bf16[8,16384]{1,0:T(8,128)(2,1)S(1)} %copy-done, bf16[8,16384]{1,0:T(8,128)(2,1)S(1)} %collective-permute-done.3.refs_1_, bf16[8,16384]{1,0:T(8,128)(2,1)S(1)} %collective-permute-done.8.refs_2_, ...), custom_call_target="tpu_custom_call" | custom-call | tf_op jit(solution)/shard_map/stack/pallas_call | solution.py:279
  50.4 0.4 collective-permute-start.19
  51.0 0.3 collective-permute-start.21
  51.3 0.7 %collective-permute-done.19.refs_5_ = bf16[8,16384]{1,0:T(8,128)(2,1)S(1)} collective-permute-done((bf16[8,16384]{1,0:T(8,128)(2,1)S(1)}, bf16[8,16384]{1,0:T(8,128)(2,1)S(1)}, u32[]{:S(2)}, u32[]{:S(2)}) %collective-permute-start.19) | collective-permute-done | bytes 262176 | tf_op jit(solution)/shard_map/ppermute | solution.py:40
  52.0 0.4 collective-permute-done.20.refs_6_
  52.4 0.4 collective-permute-done.21.refs_7_
  52.7 13.9 %stack.3 = f32[516,2,2,64,128]{4,3,2,1,0:T(8,128)} custom-call(s32[1548]{0:T(1024)S(1)} %concatenate.6.lists_hbm, bf16[8,16384]{1,0:T(8,128)(2,1)S(1)} %pad_maximum_fusion.refs_0_, bf16[8,16384]{1,0:T(8,128)(2,1)S(1)} %collective-permute-done.7.refs_1_, bf16[8,16384]{1,0:T(8,128)(2,1)S(1)} %collective-permute-done.10.refs_2_, ...), custom_call_target="tpu_custom_call", output_to_operand_aliasing={{}: (9, {})} | custom-call | tf_op jit(solution)/shard_map/stack/pallas_call | solution.py:279
  (31 shorter events, 0.6 us)
Async XLA Ops:
  1.7 8.6 %collective-permute-start.2 = (bf16[2,16384]{1,0:T(2,128)(2,1)}, bf16[2,16384]{1,0:T(2,128)(2,1)S(1)}, u32[]{:S(2)}, u32[]{:S(2)}) collective-permute-start(bf16[2,16384]{1,0:T(2,128)(2,1)} %bitcast.8), channel_id=1, source_target_pairs={{0,6},{2,0},{4,2},{6,4},{1,7},{3,1},{5,3},{7,5},{8,14},{10,8},{12,... | collective-permute-start | bytes 196616 | tf_op jit(solution)/shard_map/ppermute | solution.py:40
  6.8 6.7 %collective-permute-start.1 = (bf16[2,16384]{1,0:T(2,128)(2,1)}, bf16[2,16384]{1,0:T(2,128)(2,1)S(1)}, u32[]{:S(2)}, u32[]{:S(2)}) collective-permute-start(bf16[2,16384]{1,0:T(2,128)(2,1)} %bitcast.9), channel_id=1, source_target_pairs={{0,4},{2,6},{4,0},{6,2},{1,5},{3,7},{5,1},{7,3},{8,12},{10,14},{12... | collective-permute-start | bytes 196616 | tf_op jit(solution)/shard_map/ppermute | solution.py:40
  6.8 6.7 %collective-permute-start = (bf16[2,16384]{1,0:T(2,128)(2,1)}, bf16[2,16384]{1,0:T(2,128)(2,1)S(1)}, u32[]{:S(2)}, u32[]{:S(2)}) collective-permute-start(bf16[2,16384]{1,0:T(2,128)(2,1)} %bitcast.10), channel_id=1, source_target_pairs={{0,2},{2,4},{4,6},{6,0},{1,3},{3,5},{5,7},{7,1},{8,10},{10,12},{12... | collective-permute-start | bytes 196616 | tf_op jit(solution)/shard_map/ppermute | solution.py:40
  10.4 3.1 %copy-start.1 = (bf16[2,16384]{1,0:T(2,128)(2,1)}, bf16[2,16384]{1,0:T(2,128)(2,1)S(1)}, u32[]{:S(2)}) copy-start(bf16[2,16384]{1,0:T(2,128)(2,1)S(1)} %collective-permute-done.2.refs_3_) | copy-start | bytes 196612
  13.5 0.6 copy-start.2
  14.1 0.6 copy-start.3
  16.5 3.0 %collective-permute-start.3 = (bf16[8,16384]{1,0:T(8,128)(2,1)}, bf16[8,16384]{1,0:T(8,128)(2,1)S(1)}, u32[]{:S(2)}, u32[]{:S(2)}) collective-permute-start(bf16[8,16384]{1,0:T(8,128)(2,1)} %join.1.refs_0_), channel_id=1, source_target_pairs={{0,8},{8,0},{1,9},{9,1},{2,10},{10,2},{3,11},{11,3},{4,12},{12,4},... | collective-permute-start | bytes 786440 | tf_op jit(solution)/shard_map/ppermute | solution.py:40
  16.5 8.9 %collective-permute-start.9 = (bf16[8,16384]{1,0:T(8,128)(2,1)}, bf16[8,16384]{1,0:T(8,128)(2,1)S(1)}, u32[]{:S(2)}, u32[]{:S(2)}) collective-permute-start(bf16[8,16384]{1,0:T(8,128)(2,1)} %join.1.refs_0_), channel_id=1, source_target_pairs={{0,1},{1,0},{2,3},{3,2},{4,5},{5,4},{6,7},{7,6},{8,9},{9,8},{10,11... | collective-permute-start | bytes 786440 | tf_op jit(solution)/shard_map/ppermute | solution.py:40
  18.1 9.0 %collective-permute-start.8 = (bf16[8,16384]{1,0:T(8,128)(2,1)}, bf16[8,16384]{1,0:T(8,128)(2,1)S(1)}, u32[]{:S(2)}, u32[]{:S(2)}) collective-permute-start(bf16[8,16384]{1,0:T(8,128)(2,1)} %join.1.refs_0_), channel_id=1, source_target_pairs={{0,16},{16,0},{1,17},{17,1},{2,18},{18,2},{3,19},{19,3},{4,20},{20... | collective-permute-start | bytes 786440 | tf_op jit(solution)/shard_map/ppermute | solution.py:40
  19.5 9.1 %collective-permute-start.6 = (bf16[2,16384]{1,0:T(2,128)(2,1)}, bf16[2,16384]{1,0:T(2,128)(2,1)S(1)}, u32[]{:S(2)}, u32[]{:S(2)}) collective-permute-start(bf16[2,16384]{1,0:T(2,128)(2,1)} %bitcast.4), channel_id=1, source_target_pairs={{0,6},{2,0},{4,2},{6,4},{1,7},{3,1},{5,3},{7,5},{8,14},{10,8},{12,... | collective-permute-start | bytes 196616 | tf_op jit(solution)/shard_map/ppermute | solution.py:40
  21.4 7.3 %collective-permute-start.5 = (bf16[2,16384]{1,0:T(2,128)(2,1)}, bf16[2,16384]{1,0:T(2,128)(2,1)S(1)}, u32[]{:S(2)}, u32[]{:S(2)}) collective-permute-start(bf16[2,16384]{1,0:T(2,128)(2,1)} %bitcast.5), channel_id=1, source_target_pairs={{0,4},{2,6},{4,0},{6,2},{1,5},{3,7},{5,1},{7,3},{8,12},{10,14},{12... | collective-permute-start | bytes 196616 | tf_op jit(solution)/shard_map/ppermute | solution.py:40
  21.4 7.7 %collective-permute-start.4 = (bf16[2,16384]{1,0:T(2,128)(2,1)}, bf16[2,16384]{1,0:T(2,128)(2,1)S(1)}, u32[]{:S(2)}, u32[]{:S(2)}) collective-permute-start(bf16[2,16384]{1,0:T(2,128)(2,1)} %bitcast.6), channel_id=1, source_target_pairs={{0,2},{2,4},{4,6},{6,0},{1,3},{3,5},{5,7},{7,1},{8,10},{10,12},{12... | collective-permute-start | bytes 196616 | tf_op jit(solution)/shard_map/ppermute | solution.py:40
  25.5 5.4 %collective-permute-start.12 = (bf16[8,8192]{1,0:T(8,128)(2,1)S(1)}, bf16[8,8192]{1,0:T(8,128)(2,1)S(1)}, u32[]{:S(2)}, u32[]{:S(2)}) collective-permute-start(bf16[8,8192]{1,0:T(8,128)(2,1)S(1)} %slice.8), channel_id=1, source_target_pairs={{0,16},{16,0},{1,17},{17,1},{2,18},{18,2},{3,19},{19,3},{4,20},{20... | collective-permute-start | bytes 393224 | tf_op jit(solution)/shard_map/ppermute | solution.py:40
  27.1 5.1 %collective-permute-start.13 = (bf16[8,8192]{1,0:T(8,128)(2,1)S(1)}, bf16[8,8192]{1,0:T(8,128)(2,1)S(1)}, u32[]{:S(2)}, u32[]{:S(2)}) collective-permute-start(bf16[8,8192]{1,0:T(8,128)(2,1)S(1)} %slice.9), channel_id=1, source_target_pairs={{0,1},{1,0},{2,3},{3,2},{4,5},{5,4},{6,7},{7,6},{8,9},{9,8},{10,11... | collective-permute-start | bytes 393224 | tf_op jit(solution)/shard_map/ppermute | solution.py:40
  28.6 5.2 %collective-permute-start.16 = (bf16[8,16384]{1,0:T(8,128)(2,1)S(1)}, bf16[8,16384]{1,0:T(8,128)(2,1)S(1)}, u32[]{:S(2)}, u32[]{:S(2)}) collective-permute-start(bf16[8,16384]{1,0:T(8,128)(2,1)S(1)} %collective-permute-done.9.refs_3_), channel_id=1, source_target_pairs={{0,8},{8,0},{1,9},{9,1},{2,10},{10,2},{3,11},{11,3},{4,12},{12,4},... | collective-permute-start | bytes 786440 | tf_op jit(solution)/shard_map/ppermute | solution.py:40
  28.8 5.1 %collective-permute-start.15 = (bf16[8,16384]{1,0:T(8,128)(2,1)S(1)}, bf16[8,16384]{1,0:T(8,128)(2,1)S(1)}, u32[]{:S(2)}, u32[]{:S(2)}) collective-permute-start(bf16[8,16384]{1,0:T(8,128)(2,1)S(1)} %collective-permute-done.8.refs_2_), channel_id=1, source_target_pairs={{0,8},{8,0},{1,9},{9,1},{2,10},{10,2},{3,11},{11,3},{4,12},{12,4},... | collective-permute-start | bytes 786440 | tf_op jit(solution)/shard_map/ppermute | solution.py:40
  30.3 20.1 %collective-permute-start.11 = (bf16[8,16384]{1,0:T(8,128)(2,1)S(1)}, bf16[8,16384]{1,0:T(8,128)(2,1)S(1)}, u32[]{:S(2)}, u32[]{:S(2)}) collective-permute-start(bf16[8,16384]{1,0:T(8,128)(2,1)S(1)} %pad_maximum_fusion.refs_0_), channel_id=1, source_target_pairs={{0,1},{1,0},{16,17},{17,16},{2,3},{3,2},{18,19},{19,18},{4,5},{5,4... | collective-permute-start | bytes 786440 | tf_op jit(solution)/shard_map/ppermute | solution.py:70
  30.9 19.5 %collective-permute-start.10 = (bf16[8,16384]{1,0:T(8,128)(2,1)S(1)}, bf16[8,16384]{1,0:T(8,128)(2,1)S(1)}, u32[]{:S(2)}, u32[]{:S(2)}) collective-permute-start(bf16[8,16384]{1,0:T(8,128)(2,1)S(1)} %pad_maximum_fusion.refs_0_), channel_id=1, source_target_pairs={{0,16},{1,17},{16,0},{17,1},{2,18},{3,19},{18,2},{19,3},{4,20},{5,... | collective-permute-start | bytes 786440 | tf_op jit(solution)/shard_map/ppermute | solution.py:70
  32.2 18.2 %collective-permute-start.14 = (bf16[8,16384]{1,0:T(8,128)(2,1)S(1)}, bf16[8,16384]{1,0:T(8,128)(2,1)S(1)}, u32[]{:S(2)}, u32[]{:S(2)}) collective-permute-start(bf16[8,16384]{1,0:T(8,128)(2,1)S(1)} %pad_maximum_fusion.refs_0_), channel_id=1, source_target_pairs={{0,17},{1,16},{16,1},{17,0},{2,19},{3,18},{18,3},{19,2},{4,21},{5,... | collective-permute-start | bytes 786440 | tf_op jit(solution)/shard_map/ppermute | solution.py:70
  33.9 1.3 %collective-permute-start.17 = (bf16[8,8192]{1,0:T(8,128)(2,1)S(1)}, bf16[8,8192]{1,0:T(8,128)(2,1)S(1)}, u32[]{:S(2)}, u32[]{:S(2)}) collective-permute-start(bf16[8,8192]{1,0:T(8,128)(2,1)S(1)} %collective-permute-done.12.refs_6_), channel_id=1, source_target_pairs={{0,8},{8,0},{1,9},{9,1},{2,10},{10,2},{3,11},{11,3},{4,12},{12,4},... | collective-permute-start | bytes 393224 | tf_op jit(solution)/shard_map/ppermute | solution.py:40
  33.9 1.5 %collective-permute-start.18 = (bf16[8,8192]{1,0:T(8,128)(2,1)S(1)}, bf16[8,8192]{1,0:T(8,128)(2,1)S(1)}, u32[]{:S(2)}, u32[]{:S(2)}) collective-permute-start(bf16[8,8192]{1,0:T(8,128)(2,1)S(1)} %collective-permute-done.13.refs_8_), channel_id=1, source_target_pairs={{0,8},{8,0},{1,9},{9,1},{2,10},{10,2},{3,11},{11,3},{4,12},{12,4},... | collective-permute-start | bytes 393224 | tf_op jit(solution)/shard_map/ppermute | solution.py:40
  35.2 16.1 %collective-permute-start.7 = (bf16[8,16384]{1,0:T(8,128)(2,1)S(1)}, bf16[8,16384]{1,0:T(8,128)(2,1)S(1)}, u32[]{:S(2)}, u32[]{:S(2)}) collective-permute-start(bf16[8,16384]{1,0:T(8,128)(2,1)S(1)} %pad_maximum_fusion.refs_0_), channel_id=1, source_target_pairs={{0,8},{8,0},{1,9},{9,1},{2,10},{10,2},{3,11},{11,3},{4,12},{12,4},... | collective-permute-start | bytes 786440 | tf_op jit(solution)/shard_map/ppermute | solution.py:40
  35.4 1.0 %copy-start = (bf16[8,16384]{1,0:T(8,128)(2,1)S(1)}, bf16[8,16384]{1,0:T(8,128)(2,1)}, u32[]{:S(2)}) copy-start(bf16[8,16384]{1,0:T(8,128)(2,1)} %join.1.refs_0_) | copy-start | bytes 786436
  50.4 1.6 %collective-permute-start.19 = (bf16[8,16384]{1,0:T(8,128)(2,1)S(1)}, bf16[8,16384]{1,0:T(8,128)(2,1)S(1)}, u32[]{:S(2)}, u32[]{:S(2)}) collective-permute-start(bf16[8,16384]{1,0:T(8,128)(2,1)S(1)} %collective-permute-done.10.refs_2_), channel_id=1, source_target_pairs={{0,8},{8,0},{1,9},{9,1},{2,10},{10,2},{3,11},{11,3},{4,12},{12,4},... | collective-permute-start | bytes 786440 | tf_op jit(solution)/shard_map/ppermute | solution.py:40
  50.8 1.6 %collective-permute-start.20 = (bf16[8,16384]{1,0:T(8,128)(2,1)S(1)}, bf16[8,16384]{1,0:T(8,128)(2,1)S(1)}, u32[]{:S(2)}, u32[]{:S(2)}) collective-permute-start(bf16[8,16384]{1,0:T(8,128)(2,1)S(1)} %collective-permute-done.11.refs_3_), channel_id=1, source_target_pairs={{0,8},{8,0},{1,9},{9,1},{2,10},{10,2},{3,11},{11,3},{4,12},{12,4},... | collective-permute-start | bytes 786440 | tf_op jit(solution)/shard_map/ppermute | solution.py:40
  51.0 1.8 %collective-permute-start.21 = (bf16[8,16384]{1,0:T(8,128)(2,1)S(1)}, bf16[8,16384]{1,0:T(8,128)(2,1)S(1)}, u32[]{:S(2)}, u32[]{:S(2)}) collective-permute-start(bf16[8,16384]{1,0:T(8,128)(2,1)S(1)} %collective-permute-done.14.refs_4_), channel_id=1, source_target_pairs={{0,8},{8,0},{1,9},{9,1},{2,10},{10,2},{3,11},{11,3},{4,12},{12,4},... | collective-permute-start | bytes 786440 | tf_op jit(solution)/shard_map/ppermute | solution.py:40

commit v8 on v6

--- a/solution.py
+++ b/solution.py
@@ -16,9 +16,9 @@
     freqs = spectra_ref.shape[0]
     power = None
     for freq in range(freqs):
-        slab = spectra_ref[freq]
-        term = jnp.sum(slab * slab, axis=1, keepdims=True)
-        power = term if power is None else power + term
+        for part in range(2):
+            row = spectra_ref[freq, :, part : part + 1, :]
+            power = row * row if power is None else power + row * row
     factor = jnp.minimum(lax.rsqrt(power / freqs), 1.0)
     for freq in range(freqs):
         out_refs[freq][...] = (spectra_ref[freq] * factor).astype(jnp.bfloat16)
@@ -246,7 +246,7 @@
     tile_total, _, parts, row_count, _ = out_shape.shape
     pack = math.gcd(tile_total, max(1, MXU // depth))
     copies = min(pack, max(1, BLOCK // depth))
-    tiles = max(pack, 24 // pack * pack)
+    tiles = max(pack, 36 // pack * pack)
     tiles = min(tiles, tile_total)
     blocks = channels // BLOCK
     vmem = pl.BlockSpec(memory_space=pltpu.VMEM)

time: 64.3 us -> 62.4 us (0.970)
  Pallas kernels: 29.9 us -> 28 us
    pallas_call x2, Pallas kernels: 27.9 us -> 26.2 us  [stack_bin(): pl.pallas_call(functools.partial(stack_kernel, (len(whole), len(lows), le...]
  transfers between devices with their start and end apart: 22 -> 22, of which waited for: 7 -> 7; matrix products, arithmetic and copies ran while one was open for 6% -> 6% of each run, Pallas kernels for 22% -> 21%
where the time goes in v8:
time: 62.4 us; the launch traced here: 62 us
  Pallas kernels  28 us (45%)
  starting transfers between devices  21.6 us (35%)
  waiting for transfers between devices  7.55 us (12%)
  other arithmetic  4.74 us (8%)
    pallas_call x2, Pallas kernels, stack_bin(): pl.pallas_call(functools.partial(stack_kernel, (len(whole), len(lows), le...  26.2 us
    ppermute x19, starting transfers between devices, shift(): lax.ppermute(value, axis, [(at, (at + step) % size) for at in range(size)])  18.1 us
    ppermute x19, waiting for transfers between devices, shift(): lax.ppermute(value, axis, [(at, (at + step) % size) for at in range(size)])  7.54 us
    ppermute x3, starting transfers between devices, gather_direct(): blocks.append(lax.ppermute(sent, ('chip', 'win'), perm))  3.55 us
    concatenate x2, other arithmetic, gather_line(): return jnp.concatenate(line, axis=0)  2.28 us
    pallas_call x1, Pallas kernels, whiten(): pl.pallas_call(whiten_kernel, out_shape=[shape] * freqs, name='whiten')  1.75 us
    reduce_sum x1, other arithmetic, by_column(): jnp.sum(jnp.where(hit, values[None, :], 0), axis=1)  1.46 us
  transfers between devices with their start and end apart: 22, of which 7 were waited for; matrix products, arithmetic and copies ran while one was open for 6% of the time, Pallas kernels for 21%

profile of v8, /device:TPU:0, one launch (start us, length us, event | category | flops | bytes accessed | tf_op | source)
XLA Modules:
  0.0 62.0 jit_solution(8273151678886996127)
XLA Ops:
  0.0 1.8 %whiten.1 = (bf16[1,2,16384]{2,1,0:T(2,128)(2,1)}, bf16[1,2,16384]{2,1,0:T(2,128)(2,1)}) custom-call(f32[2,1,2,16384]{3,2,1,0:T(2,128)} %bitcast.3), custom_call_target="tpu_custom_call" | custom-call | tf_op jit(solution)/shard_map/whiten/pallas_call | solution.py:30
  1.8 5.0 %collective-permute-start.2 = (bf16[2,16384]{1,0:T(2,128)(2,1)}, bf16[2,16384]{1,0:T(2,128)(2,1)S(1)}, u32[]{:S(2)}, u32[]{:S(2)}) collective-permute-start(bf16[2,16384]{1,0:T(2,128)(2,1)} %bitcast.8), channel_id=1, source_target_pairs={{0,6},{2,0},{4,2},{6,4},{1,7},{3,1},{5,3},{7,5},{8,14},{10,8},{12,... | collective-permute-start | bytes 196616 | tf_op jit(solution)/shard_map/ppermute | solution.py:40
  6.8 1.0 %collective-permute-start = (bf16[2,16384]{1,0:T(2,128)(2,1)}, bf16[2,16384]{1,0:T(2,128)(2,1)S(1)}, u32[]{:S(2)}, u32[]{:S(2)}) collective-permute-start(bf16[2,16384]{1,0:T(2,128)(2,1)} %bitcast.10), channel_id=1, source_target_pairs={{0,2},{2,4},{4,6},{6,0},{1,3},{3,5},{5,7},{7,1},{8,10},{10,12},{12... | collective-permute-start | bytes 196616 | tf_op jit(solution)/shard_map/ppermute | solution.py:40
  7.8 0.7 %iota_add_fusion = s32[516]{0:T(1024)S(1)} fusion(s32[516]{0:T(1024)} %param.5), kind=kLoop, calls=%fused_computation.7 | loop fusion | flops 1032 | bytes 4128 | tf_op jit(solution)/shard_map/add | solution.py:66
  8.5 0.3 convert_reduce_fusion
  8.8 1.5 %select_reduce_fusion = (s32[516]{0:T(1024)S(1)}, s32[516]{0:T(1024)S(1)}, s32[516]{0:T(1024)S(1)}) fusion(s32[516]{0:T(1024)S(1)} %convert_reduce_fusion, s32[516]{0:T(1024)} %param.5, s32[516]{0:T(1024)} %param.4), kind=kLoop, calls=%fused_computation | loop fusion | flops 1862244 | bytes 12384 | tf_op jit(solution)/shard_map/reduce_sum | solution.py:71
  10.4 3.1 %collective-permute-done.1 = bf16[2,16384]{1,0:T(2,128)(2,1)S(1)} collective-permute-done((bf16[2,16384]{1,0:T(2,128)(2,1)}, bf16[2,16384]{1,0:T(2,128)(2,1)S(1)}, u32[]{:S(2)}, u32[]{:S(2)}) %collective-permute-start.1) | collective-permute-done | bytes 65568 | tf_op jit(solution)/shard_map/ppermute | solution.py:40
  13.5 1.1 %pad_maximum_fusion.refs_0_ = bf16[8,16384]{1,0:T(8,128)(2,1)S(1)} fusion(bf16[2,16384]{1,0:T(2,128)(2,1)S(1)} %collective-permute-done.2, bf16[2,16384]{1,0:T(2,128)(2,1)S(1)} %collective-permute-done.1, bf16[2,16384]{1,0:T(2,128)(2,1)S(1)} %collective-permute-done, bf16[2,16384]{1,0:T(2,128)(2,1)} %bitcast.11), kind=kLoop, calls=%fused_computation.5 | loop fusion | flops 1048576 | bytes 524288 | tf_op jit(solution)/shard_map/concatenate | solution.py:45
  14.7 1.6 %collective-permute-start.9 = (bf16[8,16384]{1,0:T(8,128)(2,1)S(1)}, bf16[8,16384]{1,0:T(8,128)(2,1)S(1)}, u32[]{:S(2)}, u32[]{:S(2)}) collective-permute-start(bf16[8,16384]{1,0:T(8,128)(2,1)S(1)} %pad_maximum_fusion.refs_0_), channel_id=1, source_target_pairs={{0,1},{1,0},{2,3},{3,2},{4,5},{5,4},{6,7},{7,6},{8,9},{9,8},{10,11... | collective-permute-start | bytes 786440 | tf_op jit(solution)/shard_map/ppermute | solution.py:40
  16.3 1.5 %collective-permute-start.8 = (bf16[8,16384]{1,0:T(8,128)(2,1)S(1)}, bf16[8,16384]{1,0:T(8,128)(2,1)S(1)}, u32[]{:S(2)}, u32[]{:S(2)}) collective-permute-start(bf16[8,16384]{1,0:T(8,128)(2,1)S(1)} %pad_maximum_fusion.refs_0_), channel_id=1, source_target_pairs={{0,16},{16,0},{1,17},{17,1},{2,18},{18,2},{3,19},{19,3},{4,20},{20... | collective-permute-start | bytes 786440 | tf_op jit(solution)/shard_map/ppermute | solution.py:40
  17.8 1.9 %collective-permute-start.6 = (bf16[2,16384]{1,0:T(2,128)(2,1)}, bf16[2,16384]{1,0:T(2,128)(2,1)S(1)}, u32[]{:S(2)}, u32[]{:S(2)}) collective-permute-start(bf16[2,16384]{1,0:T(2,128)(2,1)} %bitcast.4), channel_id=1, source_target_pairs={{0,6},{2,0},{4,2},{6,4},{1,7},{3,1},{5,3},{7,5},{8,14},{10,8},{12,... | collective-permute-start | bytes 196616 | tf_op jit(solution)/shard_map/ppermute | solution.py:40
  19.7 1.9 %collective-permute-start.4 = (bf16[2,16384]{1,0:T(2,128)(2,1)}, bf16[2,16384]{1,0:T(2,128)(2,1)S(1)}, u32[]{:S(2)}, u32[]{:S(2)}) collective-permute-start(bf16[2,16384]{1,0:T(2,128)(2,1)} %bitcast.6), channel_id=1, source_target_pairs={{0,2},{2,4},{4,6},{6,0},{1,3},{3,5},{5,7},{7,1},{8,10},{10,12},{12... | collective-permute-start | bytes 196616 | tf_op jit(solution)/shard_map/ppermute | solution.py:40
  21.6 1.8 %collective-permute-done.9.refs_3_ = bf16[8,16384]{1,0:T(8,128)(2,1)S(1)} collective-permute-done((bf16[8,16384]{1,0:T(8,128)(2,1)S(1)}, bf16[8,16384]{1,0:T(8,128)(2,1)S(1)}, u32[]{:S(2)}, u32[]{:S(2)}) %collective-permute-start.9) | collective-permute-done | bytes 262176 | tf_op jit(solution)/shard_map/ppermute | solution.py:40
  23.4 1.6 %collective-permute-start.12 = (bf16[8,8192]{1,0:T(8,128)(2,1)S(1)}, bf16[8,8192]{1,0:T(8,128)(2,1)S(1)}, u32[]{:S(2)}, u32[]{:S(2)}) collective-permute-start(bf16[8,8192]{1,0:T(8,128)(2,1)S(1)} %slice.8), channel_id=1, source_target_pairs={{0,16},{16,0},{1,17},{17,1},{2,18},{18,2},{3,19},{19,3},{4,20},{20... | collective-permute-start | bytes 393224 | tf_op jit(solution)/shard_map/ppermute | solution.py:40
  25.0 1.6 %collective-permute-start.13 = (bf16[8,8192]{1,0:T(8,128)(2,1)S(1)}, bf16[8,8192]{1,0:T(8,128)(2,1)S(1)}, u32[]{:S(2)}, u32[]{:S(2)}) collective-permute-start(bf16[8,8192]{1,0:T(8,128)(2,1)S(1)} %slice.9), channel_id=1, source_target_pairs={{0,1},{1,0},{2,3},{3,2},{4,5},{5,4},{6,7},{7,6},{8,9},{9,8},{10,11... | collective-permute-start | bytes 393224 | tf_op jit(solution)/shard_map/ppermute | solution.py:40
  26.6 0.3 collective-permute-done.5
  26.9 0.2 collective-permute-start.15
  27.1 1.1 %pad_maximum_fusion.1.refs_0_ = bf16[8,16384]{1,0:T(8,128)(2,1)S(1)} fusion(bf16[2,16384]{1,0:T(2,128)(2,1)S(1)} %collective-permute-done.6, bf16[2,16384]{1,0:T(2,128)(2,1)S(1)} %collective-permute-done.5, bf16[2,16384]{1,0:T(2,128)(2,1)S(1)} %collective-permute-done.4, bf16[2,16384]{1,0:T(2,128)(2,1)} %bitcast.7), kind=kLoop, calls=%fused_computation.6 | loop fusion | flops 1048576 | bytes 524288 | tf_op jit(solution)/shard_map/concatenate | solution.py:45
  28.3 0.6 collective-permute-start.11
  28.8 1.2 %collective-permute-start.10 = (bf16[8,16384]{1,0:T(8,128)(2,1)S(1)}, bf16[8,16384]{1,0:T(8,128)(2,1)S(1)}, u32[]{:S(2)}, u32[]{:S(2)}) collective-permute-start(bf16[8,16384]{1,0:T(8,128)(2,1)S(1)} %pad_maximum_fusion.1.refs_0_), channel_id=1, source_target_pairs={{0,16},{1,17},{16,0},{17,1},{2,18},{3,19},{18,2},{19,3},{4,20},{5,... | collective-permute-start | bytes 786440 | tf_op jit(solution)/shard_map/ppermute | solution.py:59
  30.1 1.8 %collective-permute-start.14 = (bf16[8,16384]{1,0:T(8,128)(2,1)S(1)}, bf16[8,16384]{1,0:T(8,128)(2,1)S(1)}, u32[]{:S(2)}, u32[]{:S(2)}) collective-permute-start(bf16[8,16384]{1,0:T(8,128)(2,1)S(1)} %pad_maximum_fusion.1.refs_0_), channel_id=1, source_target_pairs={{0,17},{1,16},{16,1},{17,0},{2,19},{3,18},{18,3},{19,2},{4,21},{5,... | collective-permute-start | bytes 786440 | tf_op jit(solution)/shard_map/ppermute | solution.py:59
  31.8 0.5 collective-permute-start.18
  32.3 0.8 %collective-permute-done.17.refs_7_ = bf16[8,8192]{1,0:T(8,128)(2,1)S(1)} collective-permute-done((bf16[8,8192]{1,0:T(8,128)(2,1)S(1)}, bf16[8,8192]{1,0:T(8,128)(2,1)S(1)}, u32[]{:S(2)}, u32[]{:S(2)}) %collective-permute-start.17) | collective-permute-done | bytes 131104 | tf_op jit(solution)/shard_map/ppermute | solution.py:40
  33.2 0.1 collective-permute-start.7
  33.4 13.1 %stack.2.refs_8_ = f32[516,2,2,64,128]{4,3,2,1,0:T(8,128)} custom-call(s32[1548]{0:T(1024)S(1)} %concatenate.10.lists_hbm, bf16[8,16384]{1,0:T(8,128)(2,1)S(1)} %pad_maximum_fusion.refs_0_, bf16[8,16384]{1,0:T(8,128)(2,1)S(1)} %collective-permute-done.3.refs_1_, bf16[8,16384]{1,0:T(8,128)(2,1)S(1)} %collective-permute-done.8.refs_2_, ...), custom_call_target="tpu_custom_call" | custom-call | tf_op jit(solution)/shard_map/stack/pallas_call | solution.py:268
  46.5 0.5 collective-permute-start.19
  47.0 0.1 collective-permute-start.20
  47.1 0.4 collective-permute-start.21
  47.5 0.6 %collective-permute-done.19.refs_5_ = bf16[8,16384]{1,0:T(8,128)(2,1)S(1)} collective-permute-done((bf16[8,16384]{1,0:T(8,128)(2,1)S(1)}, bf16[8,16384]{1,0:T(8,128)(2,1)S(1)}, u32[]{:S(2)}, u32[]{:S(2)}) %collective-permute-start.19) | collective-permute-done | bytes 262176 | tf_op jit(solution)/shard_map/ppermute | solution.py:40
  48.2 0.4 collective-permute-done.20.refs_6_
  48.6 0.4 collective-permute-done.21.refs_7_
  48.9 13.1 %stack.3 = f32[516,2,2,64,128]{4,3,2,1,0:T(8,128)} custom-call(s32[1548]{0:T(1024)S(1)} %concatenate.10.lists_hbm, bf16[8,16384]{1,0:T(8,128)(2,1)S(1)} %pad_maximum_fusion.1.refs_0_, bf16[8,16384]{1,0:T(8,128)(2,1)S(1)} %collective-permute-done.7.refs_1_, bf16[8,16384]{1,0:T(8,128)(2,1)S(1)} %collective-permute-done.10.refs_2_, ...), custom_call_target="tpu_custom_call", output_to_operand_aliasing={{}: (9, {})} | custom-call | tf_op jit(solution)/shard_map/stack/pallas_call | solution.py:268
  (23 shorter events, 0.3 us)
Async XLA Ops:
  1.8 8.6 %collective-permute-start.2 = (bf16[2,16384]{1,0:T(2,128)(2,1)}, bf16[2,16384]{1,0:T(2,128)(2,1)S(1)}, u32[]{:S(2)}, u32[]{:S(2)}) collective-permute-start(bf16[2,16384]{1,0:T(2,128)(2,1)} %bitcast.8), channel_id=1, source_target_pairs={{0,6},{2,0},{4,2},{6,4},{1,7},{3,1},{5,3},{7,5},{8,14},{10,8},{12,... | collective-permute-start | bytes 196616 | tf_op jit(solution)/shard_map/ppermute | solution.py:40
  6.8 6.7 %collective-permute-start.1 = (bf16[2,16384]{1,0:T(2,128)(2,1)}, bf16[2,16384]{1,0:T(2,128)(2,1)S(1)}, u32[]{:S(2)}, u32[]{:S(2)}) collective-permute-start(bf16[2,16384]{1,0:T(2,128)(2,1)} %bitcast.9), channel_id=1, source_target_pairs={{0,4},{2,6},{4,0},{6,2},{1,5},{3,7},{5,1},{7,3},{8,12},{10,14},{12... | collective-permute-start | bytes 196616 | tf_op jit(solution)/shard_map/ppermute | solution.py:40
  6.8 6.7 %collective-permute-start = (bf16[2,16384]{1,0:T(2,128)(2,1)}, bf16[2,16384]{1,0:T(2,128)(2,1)S(1)}, u32[]{:S(2)}, u32[]{:S(2)}) collective-permute-start(bf16[2,16384]{1,0:T(2,128)(2,1)} %bitcast.10), channel_id=1, source_target_pairs={{0,2},{2,4},{4,6},{6,0},{1,3},{3,5},{5,7},{7,1},{8,10},{10,12},{12... | collective-permute-start | bytes 196616 | tf_op jit(solution)/shard_map/ppermute | solution.py:40
  14.6 3.2 %collective-permute-start.3 = (bf16[8,16384]{1,0:T(8,128)(2,1)S(1)}, bf16[8,16384]{1,0:T(8,128)(2,1)S(1)}, u32[]{:S(2)}, u32[]{:S(2)}) collective-permute-start(bf16[8,16384]{1,0:T(8,128)(2,1)S(1)} %pad_maximum_fusion.refs_0_), channel_id=1, source_target_pairs={{0,8},{8,0},{1,9},{9,1},{2,10},{10,2},{3,11},{11,3},{4,12},{12,4},... | collective-permute-start | bytes 786440 | tf_op jit(solution)/shard_map/ppermute | solution.py:40
  14.7 8.7 %collective-permute-start.9 = (bf16[8,16384]{1,0:T(8,128)(2,1)S(1)}, bf16[8,16384]{1,0:T(8,128)(2,1)S(1)}, u32[]{:S(2)}, u32[]{:S(2)}) collective-permute-start(bf16[8,16384]{1,0:T(8,128)(2,1)S(1)} %pad_maximum_fusion.refs_0_), channel_id=1, source_target_pairs={{0,1},{1,0},{2,3},{3,2},{4,5},{5,4},{6,7},{7,6},{8,9},{9,8},{10,11... | collective-permute-start | bytes 786440 | tf_op jit(solution)/shard_map/ppermute | solution.py:40
  16.3 8.7 %collective-permute-start.8 = (bf16[8,16384]{1,0:T(8,128)(2,1)S(1)}, bf16[8,16384]{1,0:T(8,128)(2,1)S(1)}, u32[]{:S(2)}, u32[]{:S(2)}) collective-permute-start(bf16[8,16384]{1,0:T(8,128)(2,1)S(1)} %pad_maximum_fusion.refs_0_), channel_id=1, source_target_pairs={{0,16},{16,0},{1,17},{17,1},{2,18},{18,2},{3,19},{19,3},{4,20},{20... | collective-permute-start | bytes 786440 | tf_op jit(solution)/shard_map/ppermute | solution.py:40
  17.8 8.8 %collective-permute-start.6 = (bf16[2,16384]{1,0:T(2,128)(2,1)}, bf16[2,16384]{1,0:T(2,128)(2,1)S(1)}, u32[]{:S(2)}, u32[]{:S(2)}) collective-permute-start(bf16[2,16384]{1,0:T(2,128)(2,1)} %bitcast.4), channel_id=1, source_target_pairs={{0,6},{2,0},{4,2},{6,4},{1,7},{3,1},{5,3},{7,5},{8,14},{10,8},{12,... | collective-permute-start | bytes 196616 | tf_op jit(solution)/shard_map/ppermute | solution.py:40
  19.7 7.2 %collective-permute-start.5 = (bf16[2,16384]{1,0:T(2,128)(2,1)}, bf16[2,16384]{1,0:T(2,128)(2,1)S(1)}, u32[]{:S(2)}, u32[]{:S(2)}) collective-permute-start(bf16[2,16384]{1,0:T(2,128)(2,1)} %bitcast.5), channel_id=1, source_target_pairs={{0,4},{2,6},{4,0},{6,2},{1,5},{3,7},{5,1},{7,3},{8,12},{10,14},{12... | collective-permute-start | bytes 196616 | tf_op jit(solution)/shard_map/ppermute | solution.py:40
  19.7 7.4 %collective-permute-start.4 = (bf16[2,16384]{1,0:T(2,128)(2,1)}, bf16[2,16384]{1,0:T(2,128)(2,1)S(1)}, u32[]{:S(2)}, u32[]{:S(2)}) collective-permute-start(bf16[2,16384]{1,0:T(2,128)(2,1)} %bitcast.6), channel_id=1, source_target_pairs={{0,2},{2,4},{4,6},{6,0},{1,3},{3,5},{5,7},{7,1},{8,10},{10,12},{12... | collective-permute-start | bytes 196616 | tf_op jit(solution)/shard_map/ppermute | solution.py:40
  23.4 5.4 %collective-permute-start.12 = (bf16[8,8192]{1,0:T(8,128)(2,1)S(1)}, bf16[8,8192]{1,0:T(8,128)(2,1)S(1)}, u32[]{:S(2)}, u32[]{:S(2)}) collective-permute-start(bf16[8,8192]{1,0:T(8,128)(2,1)S(1)} %slice.8), channel_id=1, source_target_pairs={{0,16},{16,0},{1,17},{17,1},{2,18},{18,2},{3,19},{19,3},{4,20},{20... | collective-permute-start | bytes 393224 | tf_op jit(solution)/shard_map/ppermute | solution.py:40
  25.0 5.0 %collective-permute-start.13 = (bf16[8,8192]{1,0:T(8,128)(2,1)S(1)}, bf16[8,8192]{1,0:T(8,128)(2,1)S(1)}, u32[]{:S(2)}, u32[]{:S(2)}) collective-permute-start(bf16[8,8192]{1,0:T(8,128)(2,1)S(1)} %slice.9), channel_id=1, source_target_pairs={{0,1},{1,0},{2,3},{3,2},{4,5},{5,4},{6,7},{7,6},{8,9},{9,8},{10,11... | collective-permute-start | bytes 393224 | tf_op jit(solution)/shard_map/ppermute | solution.py:40
  26.6 5.2 %collective-permute-start.16 = (bf16[8,16384]{1,0:T(8,128)(2,1)S(1)}, bf16[8,16384]{1,0:T(8,128)(2,1)S(1)}, u32[]{:S(2)}, u32[]{:S(2)}) collective-permute-start(bf16[8,16384]{1,0:T(8,128)(2,1)S(1)} %collective-permute-done.9.refs_3_), channel_id=1, source_target_pairs={{0,8},{8,0},{1,9},{9,1},{2,10},{10,2},{3,11},{11,3},{4,12},{12,4},... | collective-permute-start | bytes 786440 | tf_op jit(solution)/shard_map/ppermute | solution.py:40
  26.9 5.0 %collective-permute-start.15 = (bf16[8,16384]{1,0:T(8,128)(2,1)S(1)}, bf16[8,16384]{1,0:T(8,128)(2,1)S(1)}, u32[]{:S(2)}, u32[]{:S(2)}) collective-permute-start(bf16[8,16384]{1,0:T(8,128)(2,1)S(1)} %collective-permute-done.8.refs_2_), channel_id=1, source_target_pairs={{0,8},{8,0},{1,9},{9,1},{2,10},{10,2},{3,11},{11,3},{4,12},{12,4},... | collective-permute-start | bytes 786440 | tf_op jit(solution)/shard_map/ppermute | solution.py:40
  28.3 18.2 %collective-permute-start.11 = (bf16[8,16384]{1,0:T(8,128)(2,1)S(1)}, bf16[8,16384]{1,0:T(8,128)(2,1)S(1)}, u32[]{:S(2)}, u32[]{:S(2)}) collective-permute-start(bf16[8,16384]{1,0:T(8,128)(2,1)S(1)} %pad_maximum_fusion.1.refs_0_), channel_id=1, source_target_pairs={{0,1},{1,0},{16,17},{17,16},{2,3},{3,2},{18,19},{19,18},{4,5},{5,4... | collective-permute-start | bytes 786440 | tf_op jit(solution)/shard_map/ppermute | solution.py:59
  28.8 17.6 %collective-permute-start.10 = (bf16[8,16384]{1,0:T(8,128)(2,1)S(1)}, bf16[8,16384]{1,0:T(8,128)(2,1)S(1)}, u32[]{:S(2)}, u32[]{:S(2)}) collective-permute-start(bf16[8,16384]{1,0:T(8,128)(2,1)S(1)} %pad_maximum_fusion.1.refs_0_), channel_id=1, source_target_pairs={{0,16},{1,17},{16,0},{17,1},{2,18},{3,19},{18,2},{19,3},{4,20},{5,... | collective-permute-start | bytes 786440 | tf_op jit(solution)/shard_map/ppermute | solution.py:59
  30.1 16.4 %collective-permute-start.14 = (bf16[8,16384]{1,0:T(8,128)(2,1)S(1)}, bf16[8,16384]{1,0:T(8,128)(2,1)S(1)}, u32[]{:S(2)}, u32[]{:S(2)}) collective-permute-start(bf16[8,16384]{1,0:T(8,128)(2,1)S(1)} %pad_maximum_fusion.1.refs_0_), channel_id=1, source_target_pairs={{0,17},{1,16},{16,1},{17,0},{2,19},{3,18},{18,3},{19,2},{4,21},{5,... | collective-permute-start | bytes 786440 | tf_op jit(solution)/shard_map/ppermute | solution.py:59
  31.8 1.3 %collective-permute-start.17 = (bf16[8,8192]{1,0:T(8,128)(2,1)S(1)}, bf16[8,8192]{1,0:T(8,128)(2,1)S(1)}, u32[]{:S(2)}, u32[]{:S(2)}) collective-permute-start(bf16[8,8192]{1,0:T(8,128)(2,1)S(1)} %collective-permute-done.12.refs_6_), channel_id=1, source_target_pairs={{0,8},{8,0},{1,9},{9,1},{2,10},{10,2},{3,11},{11,3},{4,12},{12,4},... | collective-permute-start | bytes 393224 | tf_op jit(solution)/shard_map/ppermute | solution.py:40
  31.8 1.5 %collective-permute-start.18 = (bf16[8,8192]{1,0:T(8,128)(2,1)S(1)}, bf16[8,8192]{1,0:T(8,128)(2,1)S(1)}, u32[]{:S(2)}, u32[]{:S(2)}) collective-permute-start(bf16[8,8192]{1,0:T(8,128)(2,1)S(1)} %collective-permute-done.13.refs_8_), channel_id=1, source_target_pairs={{0,8},{8,0},{1,9},{9,1},{2,10},{10,2},{3,11},{11,3},{4,12},{12,4},... | collective-permute-start | bytes 393224 | tf_op jit(solution)/shard_map/ppermute | solution.py:40
  33.2 14.3 %collective-permute-start.7 = (bf16[8,16384]{1,0:T(8,128)(2,1)S(1)}, bf16[8,16384]{1,0:T(8,128)(2,1)S(1)}, u32[]{:S(2)}, u32[]{:S(2)}) collective-permute-start(bf16[8,16384]{1,0:T(8,128)(2,1)S(1)} %pad_maximum_fusion.1.refs_0_), channel_id=1, source_target_pairs={{0,8},{8,0},{1,9},{9,1},{2,10},{10,2},{3,11},{11,3},{4,12},{12,4},... | collective-permute-start | bytes 786440 | tf_op jit(solution)/shard_map/ppermute | solution.py:40
  46.5 1.7 %collective-permute-start.19 = (bf16[8,16384]{1,0:T(8,128)(2,1)S(1)}, bf16[8,16384]{1,0:T(8,128)(2,1)S(1)}, u32[]{:S(2)}, u32[]{:S(2)}) collective-permute-start(bf16[8,16384]{1,0:T(8,128)(2,1)S(1)} %collective-permute-done.10.refs_2_), channel_id=1, source_target_pairs={{0,8},{8,0},{1,9},{9,1},{2,10},{10,2},{3,11},{11,3},{4,12},{12,4},... | collective-permute-start | bytes 786440 | tf_op jit(solution)/shard_map/ppermute | solution.py:40
  47.0 1.5 %collective-permute-start.20 = (bf16[8,16384]{1,0:T(8,128)(2,1)S(1)}, bf16[8,16384]{1,0:T(8,128)(2,1)S(1)}, u32[]{:S(2)}, u32[]{:S(2)}) collective-permute-start(bf16[8,16384]{1,0:T(8,128)(2,1)S(1)} %collective-permute-done.11.refs_3_), channel_id=1, source_target_pairs={{0,8},{8,0},{1,9},{9,1},{2,10},{10,2},{3,11},{11,3},{4,12},{12,4},... | collective-permute-start | bytes 786440 | tf_op jit(solution)/shard_map/ppermute | solution.py:40
  47.1 1.8 %collective-permute-start.21 = (bf16[8,16384]{1,0:T(8,128)(2,1)S(1)}, bf16[8,16384]{1,0:T(8,128)(2,1)S(1)}, u32[]{:S(2)}, u32[]{:S(2)}) collective-permute-start(bf16[8,16384]{1,0:T(8,128)(2,1)S(1)} %collective-permute-done.14.refs_4_), channel_id=1, source_target_pairs={{0,8},{8,0},{1,9},{9,1},{2,10},{10,2},{3,11},{11,3},{4,12},{12,4},... | collective-permute-start | bytes 786440 | tf_op jit(solution)/shard_map/ppermute | solution.py:40

commit v9 on v8

--- a/solution.py
+++ b/solution.py
@@ -10,6 +10,7 @@
 
 BLOCK = 128
 MXU = 256
+LAG = 3
 
 
 def whiten_kernel(spectra_ref, *out_refs):
@@ -203,6 +204,9 @@
                 mine = product[member * row_count : (member + 1) * row_count]
                 ring_ref[slot, group * pack + member, 0] = mine[:, :BLOCK]
                 ring_ref[slot, group * pack + member, 1] = mine[:, BLOCK:]
+            ready = (group + 1 - LAG) * pack
+            send(first, slot, range(max(0, ready - pack), max(0, ready)))
+        send(first, slot, range(max(0, count - LAG * pack), count))
 
     def needed(last):
         return lists_ref[total + last] // (2 * span) + 1
@@ -221,7 +225,6 @@
             sent(slot, tiles)
 
         compute(first, slot, tiles)
-        send(first, slot, range(tiles))
         return need
 
     done = lax.fori_loop(0, steps, stack, jnp.int32(1))
@@ -233,7 +236,6 @@
             sent(slot, tiles)
             flying = flying[1:]
         compute(steps * tiles, slot, rest)
-        send(steps * tiles, slot, range(rest))
         flying.append((slot, rest))
     for slot, count in flying:
         sent(slot, count)
@@ -246,7 +248,7 @@
     tile_total, _, parts, row_count, _ = out_shape.shape
     pack = math.gcd(tile_total, max(1, MXU // depth))
     copies = min(pack, max(1, BLOCK // depth))
-    tiles = max(pack, 36 // pack * pack)
+    tiles = max(pack, 72 // pack * pack)
     tiles = min(tiles, tile_total)
     blocks = channels // BLOCK
     vmem = pl.BlockSpec(memory_space=pltpu.VMEM)
@@ -257,7 +259,7 @@
         in_specs.append(pl.BlockSpec(memory_space=pl.ANY))
         aliases = {len(operands): 0}
         operands.append(so_far)
-    slots = 4
+    slots = 3
     scratch = [
         ((copies, blocks * row_count, copies * depth), jnp.bfloat16),
         ((blocks, depth, 2 * BLOCK), jnp.bfloat16),

time: 62.4 us -> 62 us (level)
  no operation moved by 1% of the time
where the time goes in v9:
time: 62 us; the launch traced here: 61.7 us
  Pallas kernels  27.7 us (45%)
  starting transfers between devices  21.4 us (35%)
  waiting for transfers between devices  7.71 us (12%)
  other arithmetic  4.74 us (8%)
    pallas_call x2, Pallas kernels, stack_bin(): pl.pallas_call(functools.partial(stack_kernel, (len(whole), len(lows), le...  26 us
    ppermute x19, starting transfers between devices, shift(): lax.ppermute(value, axis, [(at, (at + step) % size) for at in range(size)])  17.8 us
    ppermute x19, waiting for transfers between devices, shift(): lax.ppermute(value, axis, [(at, (at + step) % size) for at in range(size)])  7.7 us
    ppermute x3, starting transfers between devices, gather_direct(): blocks.append(lax.ppermute(sent, ('chip', 'win'), perm))  3.55 us
    concatenate x2, other arithmetic, gather_line(): return jnp.concatenate(line, axis=0)  2.28 us
    pallas_call x1, Pallas kernels, whiten(): pl.pallas_call(whiten_kernel, out_shape=[shape] * freqs, name='whiten')  1.75 us
    reduce_sum x1, other arithmetic, by_column(): jnp.sum(jnp.where(hit, values[None, :], 0), axis=1)  1.46 us
  transfers between devices with their start and end apart: 22, of which 7 were waited for; matrix products, arithmetic and copies ran while one was open for 6% of the time, Pallas kernels for 21%

profile of v9, /device:TPU:0, one launch (start us, length us, event | category | flops | bytes accessed | tf_op | source)
XLA Modules:
  0.0 61.7 jit_solution(18132934599842898490)
XLA Ops:
  0.0 1.8 %whiten.1 = (bf16[1,2,16384]{2,1,0:T(2,128)(2,1)}, bf16[1,2,16384]{2,1,0:T(2,128)(2,1)}) custom-call(f32[2,1,2,16384]{3,2,1,0:T(2,128)} %bitcast.3), custom_call_target="tpu_custom_call" | custom-call | tf_op jit(solution)/shard_map/whiten/pallas_call | solution.py:31
  1.8 5.0 %collective-permute-start.2 = (bf16[2,16384]{1,0:T(2,128)(2,1)}, bf16[2,16384]{1,0:T(2,128)(2,1)S(1)}, u32[]{:S(2)}, u32[]{:S(2)}) collective-permute-start(bf16[2,16384]{1,0:T(2,128)(2,1)} %bitcast.8), channel_id=1, source_target_pairs={{0,6},{2,0},{4,2},{6,4},{1,7},{3,1},{5,3},{7,5},{8,14},{10,8},{12,... | collective-permute-start | bytes 196616 | tf_op jit(solution)/shard_map/ppermute | solution.py:41
  6.8 1.0 %collective-permute-start = (bf16[2,16384]{1,0:T(2,128)(2,1)}, bf16[2,16384]{1,0:T(2,128)(2,1)S(1)}, u32[]{:S(2)}, u32[]{:S(2)}) collective-permute-start(bf16[2,16384]{1,0:T(2,128)(2,1)} %bitcast.10), channel_id=1, source_target_pairs={{0,2},{2,4},{4,6},{6,0},{1,3},{3,5},{5,7},{7,1},{8,10},{10,12},{12... | collective-permute-start | bytes 196616 | tf_op jit(solution)/shard_map/ppermute | solution.py:41
  7.8 0.7 %iota_add_fusion = s32[516]{0:T(1024)S(1)} fusion(s32[516]{0:T(1024)} %param.5), kind=kLoop, calls=%fused_computation.7 | loop fusion | flops 1032 | bytes 4128 | tf_op jit(solution)/shard_map/add | solution.py:67
  8.5 0.3 convert_reduce_fusion
  8.8 1.5 %select_reduce_fusion = (s32[516]{0:T(1024)S(1)}, s32[516]{0:T(1024)S(1)}, s32[516]{0:T(1024)S(1)}) fusion(s32[516]{0:T(1024)S(1)} %convert_reduce_fusion, s32[516]{0:T(1024)} %param.5, s32[516]{0:T(1024)} %param.4), kind=kLoop, calls=%fused_computation | loop fusion | flops 1862244 | bytes 12384 | tf_op jit(solution)/shard_map/reduce_sum | solution.py:72
  10.4 3.1 %collective-permute-done.1 = bf16[2,16384]{1,0:T(2,128)(2,1)S(1)} collective-permute-done((bf16[2,16384]{1,0:T(2,128)(2,1)}, bf16[2,16384]{1,0:T(2,128)(2,1)S(1)}, u32[]{:S(2)}, u32[]{:S(2)}) %collective-permute-start.1) | collective-permute-done | bytes 65568 | tf_op jit(solution)/shard_map/ppermute | solution.py:41
  13.5 1.1 %pad_maximum_fusion.refs_0_ = bf16[8,16384]{1,0:T(8,128)(2,1)S(1)} fusion(bf16[2,16384]{1,0:T(2,128)(2,1)S(1)} %collective-permute-done.2, bf16[2,16384]{1,0:T(2,128)(2,1)S(1)} %collective-permute-done.1, bf16[2,16384]{1,0:T(2,128)(2,1)S(1)} %collective-permute-done, bf16[2,16384]{1,0:T(2,128)(2,1)} %bitcast.11), kind=kLoop, calls=%fused_computation.5 | loop fusion | flops 1048576 | bytes 524288 | tf_op jit(solution)/shard_map/concatenate | solution.py:46
  14.7 1.6 %collective-permute-start.9 = (bf16[8,16384]{1,0:T(8,128)(2,1)S(1)}, bf16[8,16384]{1,0:T(8,128)(2,1)S(1)}, u32[]{:S(2)}, u32[]{:S(2)}) collective-permute-start(bf16[8,16384]{1,0:T(8,128)(2,1)S(1)} %pad_maximum_fusion.refs_0_), channel_id=1, source_target_pairs={{0,1},{1,0},{2,3},{3,2},{4,5},{5,4},{6,7},{7,6},{8,9},{9,8},{10,11... | collective-permute-start | bytes 786440 | tf_op jit(solution)/shard_map/ppermute | solution.py:41
  16.3 1.5 %collective-permute-start.8 = (bf16[8,16384]{1,0:T(8,128)(2,1)S(1)}, bf16[8,16384]{1,0:T(8,128)(2,1)S(1)}, u32[]{:S(2)}, u32[]{:S(2)}) collective-permute-start(bf16[8,16384]{1,0:T(8,128)(2,1)S(1)} %pad_maximum_fusion.refs_0_), channel_id=1, source_target_pairs={{0,16},{16,0},{1,17},{17,1},{2,18},{18,2},{3,19},{19,3},{4,20},{20... | collective-permute-start | bytes 786440 | tf_op jit(solution)/shard_map/ppermute | solution.py:41
  17.8 1.9 %collective-permute-start.6 = (bf16[2,16384]{1,0:T(2,128)(2,1)}, bf16[2,16384]{1,0:T(2,128)(2,1)S(1)}, u32[]{:S(2)}, u32[]{:S(2)}) collective-permute-start(bf16[2,16384]{1,0:T(2,128)(2,1)} %bitcast.4), channel_id=1, source_target_pairs={{0,6},{2,0},{4,2},{6,4},{1,7},{3,1},{5,3},{7,5},{8,14},{10,8},{12,... | collective-permute-start | bytes 196616 | tf_op jit(solution)/shard_map/ppermute | solution.py:41
  19.7 1.9 %collective-permute-start.4 = (bf16[2,16384]{1,0:T(2,128)(2,1)}, bf16[2,16384]{1,0:T(2,128)(2,1)S(1)}, u32[]{:S(2)}, u32[]{:S(2)}) collective-permute-start(bf16[2,16384]{1,0:T(2,128)(2,1)} %bitcast.6), channel_id=1, source_target_pairs={{0,2},{2,4},{4,6},{6,0},{1,3},{3,5},{5,7},{7,1},{8,10},{10,12},{12... | collective-permute-start | bytes 196616 | tf_op jit(solution)/shard_map/ppermute | solution.py:41
  21.6 1.8 %collective-permute-done.9.refs_3_ = bf16[8,16384]{1,0:T(8,128)(2,1)S(1)} collective-permute-done((bf16[8,16384]{1,0:T(8,128)(2,1)S(1)}, bf16[8,16384]{1,0:T(8,128)(2,1)S(1)}, u32[]{:S(2)}, u32[]{:S(2)}) %collective-permute-start.9) | collective-permute-done | bytes 262176 | tf_op jit(solution)/shard_map/ppermute | solution.py:41
  23.4 1.6 %collective-permute-start.12 = (bf16[8,8192]{1,0:T(8,128)(2,1)S(1)}, bf16[8,8192]{1,0:T(8,128)(2,1)S(1)}, u32[]{:S(2)}, u32[]{:S(2)}) collective-permute-start(bf16[8,8192]{1,0:T(8,128)(2,1)S(1)} %slice.8), channel_id=1, source_target_pairs={{0,16},{16,0},{1,17},{17,1},{2,18},{18,2},{3,19},{19,3},{4,20},{20... | collective-permute-start | bytes 393224 | tf_op jit(solution)/shard_map/ppermute | solution.py:41
  25.0 1.6 %collective-permute-start.13 = (bf16[8,8192]{1,0:T(8,128)(2,1)S(1)}, bf16[8,8192]{1,0:T(8,128)(2,1)S(1)}, u32[]{:S(2)}, u32[]{:S(2)}) collective-permute-start(bf16[8,8192]{1,0:T(8,128)(2,1)S(1)} %slice.9), channel_id=1, source_target_pairs={{0,1},{1,0},{2,3},{3,2},{4,5},{5,4},{6,7},{7,6},{8,9},{9,8},{10,11... | collective-permute-start | bytes 393224 | tf_op jit(solution)/shard_map/ppermute | solution.py:41
  26.6 0.3 collective-permute-done.5
  26.9 0.2 collective-permute-start.15
  27.1 1.1 %pad_maximum_fusion.1.refs_0_ = bf16[8,16384]{1,0:T(8,128)(2,1)S(1)} fusion(bf16[2,16384]{1,0:T(2,128)(2,1)S(1)} %collective-permute-done.6, bf16[2,16384]{1,0:T(2,128)(2,1)S(1)} %collective-permute-done.5, bf16[2,16384]{1,0:T(2,128)(2,1)S(1)} %collective-permute-done.4, bf16[2,16384]{1,0:T(2,128)(2,1)} %bitcast.7), kind=kLoop, calls=%fused_computation.6 | loop fusion | flops 1048576 | bytes 524288 | tf_op jit(solution)/shard_map/concatenate | solution.py:46
  28.3 0.6 collective-permute-start.11
  28.8 1.2 %collective-permute-start.10 = (bf16[8,16384]{1,0:T(8,128)(2,1)S(1)}, bf16[8,16384]{1,0:T(8,128)(2,1)S(1)}, u32[]{:S(2)}, u32[]{:S(2)}) collective-permute-start(bf16[8,16384]{1,0:T(8,128)(2,1)S(1)} %pad_maximum_fusion.1.refs_0_), channel_id=1, source_target_pairs={{0,16},{1,17},{16,0},{17,1},{2,18},{3,19},{18,2},{19,3},{4,20},{5,... | collective-permute-start | bytes 786440 | tf_op jit(solution)/shard_map/ppermute | solution.py:60
  30.1 1.8 %collective-permute-start.14 = (bf16[8,16384]{1,0:T(8,128)(2,1)S(1)}, bf16[8,16384]{1,0:T(8,128)(2,1)S(1)}, u32[]{:S(2)}, u32[]{:S(2)}) collective-permute-start(bf16[8,16384]{1,0:T(8,128)(2,1)S(1)} %pad_maximum_fusion.1.refs_0_), channel_id=1, source_target_pairs={{0,17},{1,16},{16,1},{17,0},{2,19},{3,18},{18,3},{19,2},{4,21},{5,... | collective-permute-start | bytes 786440 | tf_op jit(solution)/shard_map/ppermute | solution.py:60
  31.8 0.5 collective-permute-start.18
  32.3 0.8 %collective-permute-done.17.refs_7_ = bf16[8,8192]{1,0:T(8,128)(2,1)S(1)} collective-permute-done((bf16[8,8192]{1,0:T(8,128)(2,1)S(1)}, bf16[8,8192]{1,0:T(8,128)(2,1)S(1)}, u32[]{:S(2)}, u32[]{:S(2)}) %collective-permute-start.17) | collective-permute-done | bytes 131104 | tf_op jit(solution)/shard_map/ppermute | solution.py:41
  33.2 0.1 collective-permute-start.7
  33.4 13.0 %stack.2.refs_8_ = f32[516,2,2,64,128]{4,3,2,1,0:T(8,128)} custom-call(s32[1548]{0:T(1024)S(1)} %concatenate.10.lists_hbm, bf16[8,16384]{1,0:T(8,128)(2,1)S(1)} %pad_maximum_fusion.refs_0_, bf16[8,16384]{1,0:T(8,128)(2,1)S(1)} %collective-permute-done.3.refs_1_, bf16[8,16384]{1,0:T(8,128)(2,1)S(1)} %collective-permute-done.8.refs_2_, ...), custom_call_target="tpu_custom_call" | custom-call | tf_op jit(solution)/shard_map/stack/pallas_call | solution.py:270
  46.4 0.3 collective-permute-start.19
  46.7 0.3 collective-permute-start.20
  47.0 0.2 collective-permute-start.21
  47.2 0.8 %collective-permute-done.19.refs_5_ = bf16[8,16384]{1,0:T(8,128)(2,1)S(1)} collective-permute-done((bf16[8,16384]{1,0:T(8,128)(2,1)S(1)}, bf16[8,16384]{1,0:T(8,128)(2,1)S(1)}, u32[]{:S(2)}, u32[]{:S(2)}) %collective-permute-start.19) | collective-permute-done | bytes 262176 | tf_op jit(solution)/shard_map/ppermute | solution.py:41
  48.0 0.4 collective-permute-done.20.refs_6_
  48.4 0.4 collective-permute-done.21.refs_7_
  48.7 13.0 %stack.3 = f32[516,2,2,64,128]{4,3,2,1,0:T(8,128)} custom-call(s32[1548]{0:T(1024)S(1)} %concatenate.10.lists_hbm, bf16[8,16384]{1,0:T(8,128)(2,1)S(1)} %pad_maximum_fusion.1.refs_0_, bf16[8,16384]{1,0:T(8,128)(2,1)S(1)} %collective-permute-done.7.refs_1_, bf16[8,16384]{1,0:T(8,128)(2,1)S(1)} %collective-permute-done.10.refs_2_, ...), custom_call_target="tpu_custom_call", output_to_operand_aliasing={{}: (9, {})} | custom-call | tf_op jit(solution)/shard_map/stack/pallas_call | solution.py:270
  (23 shorter events, 0.3 us)
Async XLA Ops:
  1.8 8.6 %collective-permute-start.2 = (bf16[2,16384]{1,0:T(2,128)(2,1)}, bf16[2,16384]{1,0:T(2,128)(2,1)S(1)}, u32[]{:S(2)}, u32[]{:S(2)}) collective-permute-start(bf16[2,16384]{1,0:T(2,128)(2,1)} %bitcast.8), channel_id=1, source_target_pairs={{0,6},{2,0},{4,2},{6,4},{1,7},{3,1},{5,3},{7,5},{8,14},{10,8},{12,... | collective-permute-start | bytes 196616 | tf_op jit(solution)/shard_map/ppermute | solution.py:41
  6.8 6.7 %collective-permute-start.1 = (bf16[2,16384]{1,0:T(2,128)(2,1)}, bf16[2,16384]{1,0:T(2,128)(2,1)S(1)}, u32[]{:S(2)}, u32[]{:S(2)}) collective-permute-start(bf16[2,16384]{1,0:T(2,128)(2,1)} %bitcast.9), channel_id=1, source_target_pairs={{0,4},{2,6},{4,0},{6,2},{1,5},{3,7},{5,1},{7,3},{8,12},{10,14},{12... | collective-permute-start | bytes 196616 | tf_op jit(solution)/shard_map/ppermute | solution.py:41
  6.8 6.7 %collective-permute-start = (bf16[2,16384]{1,0:T(2,128)(2,1)}, bf16[2,16384]{1,0:T(2,128)(2,1)S(1)}, u32[]{:S(2)}, u32[]{:S(2)}) collective-permute-start(bf16[2,16384]{1,0:T(2,128)(2,1)} %bitcast.10), channel_id=1, source_target_pairs={{0,2},{2,4},{4,6},{6,0},{1,3},{3,5},{5,7},{7,1},{8,10},{10,12},{12... | collective-permute-start | bytes 196616 | tf_op jit(solution)/shard_map/ppermute | solution.py:41
  14.6 3.2 %collective-permute-start.3 = (bf16[8,16384]{1,0:T(8,128)(2,1)S(1)}, bf16[8,16384]{1,0:T(8,128)(2,1)S(1)}, u32[]{:S(2)}, u32[]{:S(2)}) collective-permute-start(bf16[8,16384]{1,0:T(8,128)(2,1)S(1)} %pad_maximum_fusion.refs_0_), channel_id=1, source_target_pairs={{0,8},{8,0},{1,9},{9,1},{2,10},{10,2},{3,11},{11,3},{4,12},{12,4},... | collective-permute-start | bytes 786440 | tf_op jit(solution)/shard_map/ppermute | solution.py:41
  14.7 8.7 %collective-permute-start.9 = (bf16[8,16384]{1,0:T(8,128)(2,1)S(1)}, bf16[8,16384]{1,0:T(8,128)(2,1)S(1)}, u32[]{:S(2)}, u32[]{:S(2)}) collective-permute-start(bf16[8,16384]{1,0:T(8,128)(2,1)S(1)} %pad_maximum_fusion.refs_0_), channel_id=1, source_target_pairs={{0,1},{1,0},{2,3},{3,2},{4,5},{5,4},{6,7},{7,6},{8,9},{9,8},{10,11... | collective-permute-start | bytes 786440 | tf_op jit(solution)/shard_map/ppermute | solution.py:41
  16.3 8.7 %collective-permute-start.8 = (bf16[8,16384]{1,0:T(8,128)(2,1)S(1)}, bf16[8,16384]{1,0:T(8,128)(2,1)S(1)}, u32[]{:S(2)}, u32[]{:S(2)}) collective-permute-start(bf16[8,16384]{1,0:T(8,128)(2,1)S(1)} %pad_maximum_fusion.refs_0_), channel_id=1, source_target_pairs={{0,16},{16,0},{1,17},{17,1},{2,18},{18,2},{3,19},{19,3},{4,20},{20... | collective-permute-start | bytes 786440 | tf_op jit(solution)/shard_map/ppermute | solution.py:41
  17.8 8.8 %collective-permute-start.6 = (bf16[2,16384]{1,0:T(2,128)(2,1)}, bf16[2,16384]{1,0:T(2,128)(2,1)S(1)}, u32[]{:S(2)}, u32[]{:S(2)}) collective-permute-start(bf16[2,16384]{1,0:T(2,128)(2,1)} %bitcast.4), channel_id=1, source_target_pairs={{0,6},{2,0},{4,2},{6,4},{1,7},{3,1},{5,3},{7,5},{8,14},{10,8},{12,... | collective-permute-start | bytes 196616 | tf_op jit(solution)/shard_map/ppermute | solution.py:41
  19.7 7.2 %collective-permute-start.5 = (bf16[2,16384]{1,0:T(2,128)(2,1)}, bf16[2,16384]{1,0:T(2,128)(2,1)S(1)}, u32[]{:S(2)}, u32[]{:S(2)}) collective-permute-start(bf16[2,16384]{1,0:T(2,128)(2,1)} %bitcast.5), channel_id=1, source_target_pairs={{0,4},{2,6},{4,0},{6,2},{1,5},{3,7},{5,1},{7,3},{8,12},{10,14},{12... | collective-permute-start | bytes 196616 | tf_op jit(solution)/shard_map/ppermute | solution.py:41
  19.7 7.4 %collective-permute-start.4 = (bf16[2,16384]{1,0:T(2,128)(2,1)}, bf16[2,16384]{1,0:T(2,128)(2,1)S(1)}, u32[]{:S(2)}, u32[]{:S(2)}) collective-permute-start(bf16[2,16384]{1,0:T(2,128)(2,1)} %bitcast.6), channel_id=1, source_target_pairs={{0,2},{2,4},{4,6},{6,0},{1,3},{3,5},{5,7},{7,1},{8,10},{10,12},{12... | collective-permute-start | bytes 196616 | tf_op jit(solution)/shard_map/ppermute | solution.py:41
  23.4 5.4 %collective-permute-start.12 = (bf16[8,8192]{1,0:T(8,128)(2,1)S(1)}, bf16[8,8192]{1,0:T(8,128)(2,1)S(1)}, u32[]{:S(2)}, u32[]{:S(2)}) collective-permute-start(bf16[8,8192]{1,0:T(8,128)(2,1)S(1)} %slice.8), channel_id=1, source_target_pairs={{0,16},{16,0},{1,17},{17,1},{2,18},{18,2},{3,19},{19,3},{4,20},{20... | collective-permute-start | bytes 393224 | tf_op jit(solution)/shard_map/ppermute | solution.py:41
  25.0 5.0 %collective-permute-start.13 = (bf16[8,8192]{1,0:T(8,128)(2,1)S(1)}, bf16[8,8192]{1,0:T(8,128)(2,1)S(1)}, u32[]{:S(2)}, u32[]{:S(2)}) collective-permute-start(bf16[8,8192]{1,0:T(8,128)(2,1)S(1)} %slice.9), channel_id=1, source_target_pairs={{0,1},{1,0},{2,3},{3,2},{4,5},{5,4},{6,7},{7,6},{8,9},{9,8},{10,11... | collective-permute-start | bytes 393224 | tf_op jit(solution)/shard_map/ppermute | solution.py:41
  26.6 5.2 %collective-permute-start.16 = (bf16[8,16384]{1,0:T(8,128)(2,1)S(1)}, bf16[8,16384]{1,0:T(8,128)(2,1)S(1)}, u32[]{:S(2)}, u32[]{:S(2)}) collective-permute-start(bf16[8,16384]{1,0:T(8,128)(2,1)S(1)} %collective-permute-done.9.refs_3_), channel_id=1, source_target_pairs={{0,8},{8,0},{1,9},{9,1},{2,10},{10,2},{3,11},{11,3},{4,12},{12,4},... | collective-permute-start | bytes 786440 | tf_op jit(solution)/shard_map/ppermute | solution.py:41
  26.9 5.0 %collective-permute-start.15 = (bf16[8,16384]{1,0:T(8,128)(2,1)S(1)}, bf16[8,16384]{1,0:T(8,128)(2,1)S(1)}, u32[]{:S(2)}, u32[]{:S(2)}) collective-permute-start(bf16[8,16384]{1,0:T(8,128)(2,1)S(1)} %collective-permute-done.8.refs_2_), channel_id=1, source_target_pairs={{0,8},{8,0},{1,9},{9,1},{2,10},{10,2},{3,11},{11,3},{4,12},{12,4},... | collective-permute-start | bytes 786440 | tf_op jit(solution)/shard_map/ppermute | solution.py:41
  28.3 18.1 %collective-permute-start.11 = (bf16[8,16384]{1,0:T(8,128)(2,1)S(1)}, bf16[8,16384]{1,0:T(8,128)(2,1)S(1)}, u32[]{:S(2)}, u32[]{:S(2)}) collective-permute-start(bf16[8,16384]{1,0:T(8,128)(2,1)S(1)} %pad_maximum_fusion.1.refs_0_), channel_id=1, source_target_pairs={{0,1},{1,0},{16,17},{17,16},{2,3},{3,2},{18,19},{19,18},{4,5},{5,4... | collective-permute-start | bytes 786440 | tf_op jit(solution)/shard_map/ppermute | solution.py:60
  28.8 17.5 %collective-permute-start.10 = (bf16[8,16384]{1,0:T(8,128)(2,1)S(1)}, bf16[8,16384]{1,0:T(8,128)(2,1)S(1)}, u32[]{:S(2)}, u32[]{:S(2)}) collective-permute-start(bf16[8,16384]{1,0:T(8,128)(2,1)S(1)} %pad_maximum_fusion.1.refs_0_), channel_id=1, source_target_pairs={{0,16},{1,17},{16,0},{17,1},{2,18},{3,19},{18,2},{19,3},{4,20},{5,... | collective-permute-start | bytes 786440 | tf_op jit(solution)/shard_map/ppermute | solution.py:60
  30.1 16.3 %collective-permute-start.14 = (bf16[8,16384]{1,0:T(8,128)(2,1)S(1)}, bf16[8,16384]{1,0:T(8,128)(2,1)S(1)}, u32[]{:S(2)}, u32[]{:S(2)}) collective-permute-start(bf16[8,16384]{1,0:T(8,128)(2,1)S(1)} %pad_maximum_fusion.1.refs_0_), channel_id=1, source_target_pairs={{0,17},{1,16},{16,1},{17,0},{2,19},{3,18},{18,3},{19,2},{4,21},{5,... | collective-permute-start | bytes 786440 | tf_op jit(solution)/shard_map/ppermute | solution.py:60
  31.8 1.3 %collective-permute-start.17 = (bf16[8,8192]{1,0:T(8,128)(2,1)S(1)}, bf16[8,8192]{1,0:T(8,128)(2,1)S(1)}, u32[]{:S(2)}, u32[]{:S(2)}) collective-permute-start(bf16[8,8192]{1,0:T(8,128)(2,1)S(1)} %collective-permute-done.12.refs_6_), channel_id=1, source_target_pairs={{0,8},{8,0},{1,9},{9,1},{2,10},{10,2},{3,11},{11,3},{4,12},{12,4},... | collective-permute-start | bytes 393224 | tf_op jit(solution)/shard_map/ppermute | solution.py:41
  31.8 1.5 %collective-permute-start.18 = (bf16[8,8192]{1,0:T(8,128)(2,1)S(1)}, bf16[8,8192]{1,0:T(8,128)(2,1)S(1)}, u32[]{:S(2)}, u32[]{:S(2)}) collective-permute-start(bf16[8,8192]{1,0:T(8,128)(2,1)S(1)} %collective-permute-done.13.refs_8_), channel_id=1, source_target_pairs={{0,8},{8,0},{1,9},{9,1},{2,10},{10,2},{3,11},{11,3},{4,12},{12,4},... | collective-permute-start | bytes 393224 | tf_op jit(solution)/shard_map/ppermute | solution.py:41
  33.2 14.0 %collective-permute-start.7 = (bf16[8,16384]{1,0:T(8,128)(2,1)S(1)}, bf16[8,16384]{1,0:T(8,128)(2,1)S(1)}, u32[]{:S(2)}, u32[]{:S(2)}) collective-permute-start(bf16[8,16384]{1,0:T(8,128)(2,1)S(1)} %pad_maximum_fusion.1.refs_0_), channel_id=1, source_target_pairs={{0,8},{8,0},{1,9},{9,1},{2,10},{10,2},{3,11},{11,3},{4,12},{12,4},... | collective-permute-start | bytes 786440 | tf_op jit(solution)/shard_map/ppermute | solution.py:41
  46.4 1.6 %collective-permute-start.19 = (bf16[8,16384]{1,0:T(8,128)(2,1)S(1)}, bf16[8,16384]{1,0:T(8,128)(2,1)S(1)}, u32[]{:S(2)}, u32[]{:S(2)}) collective-permute-start(bf16[8,16384]{1,0:T(8,128)(2,1)S(1)} %collective-permute-done.10.refs_2_), channel_id=1, source_target_pairs={{0,8},{8,0},{1,9},{9,1},{2,10},{10,2},{3,11},{11,3},{4,12},{12,4},... | collective-permute-start | bytes 786440 | tf_op jit(solution)/shard_map/ppermute | solution.py:41
  46.7 1.7 %collective-permute-start.20 = (bf16[8,16384]{1,0:T(8,128)(2,1)S(1)}, bf16[8,16384]{1,0:T(8,128)(2,1)S(1)}, u32[]{:S(2)}, u32[]{:S(2)}) collective-permute-start(bf16[8,16384]{1,0:T(8,128)(2,1)S(1)} %collective-permute-done.11.refs_3_), channel_id=1, source_target_pairs={{0,8},{8,0},{1,9},{9,1},{2,10},{10,2},{3,11},{11,3},{4,12},{12,4},... | collective-permute-start | bytes 786440 | tf_op jit(solution)/shard_map/ppermute | solution.py:41
  47.0 1.8 %collective-permute-start.21 = (bf16[8,16384]{1,0:T(8,128)(2,1)S(1)}, bf16[8,16384]{1,0:T(8,128)(2,1)S(1)}, u32[]{:S(2)}, u32[]{:S(2)}) collective-permute-start(bf16[8,16384]{1,0:T(8,128)(2,1)S(1)} %collective-permute-done.14.refs_4_), channel_id=1, source_target_pairs={{0,8},{8,0},{1,9},{9,1},{2,10},{10,2},{3,11},{11,3},{4,12},{12,4},... | collective-permute-start | bytes 786440 | tf_op jit(solution)/shard_map/ppermute | solution.py:41
